TPU v7x, 32 devices: a whole 2x2x4 slice. The times are simulated.
32 devices in a mesh: dp: 16 (over z, y, core), space: 2 (over x).
Axes of the slice: x: 2, y: 2, z: 4, core: 2. Of those that a mesh axis runs over, the one named last changes fastest.
Arguments:
- fields: bfloat16 [16, 32, 16, 40, 128], P('dp', None, 'space'), may hold values from -6 to 6
- cotangent: bfloat16 [16, 32, 16, 40, 128], P('dp', None, 'space'), may hold values from -30 to 30
- spectral_weight: bfloat16 [16, 2, 32, 32, 144], P('space'), may hold values from -1 to 1
- channel_weight: bfloat16 [32, 32], replicated, may hold values from -1 to 1
- channel_bias: float32 [32], replicated, may hold values from -3 to 3
Outputs:
- grad_fields: bfloat16 [16, 32, 16, 40, 128], P('dp', None, 'space')
- grad_spectral: float32 [16, 2, 32, 32, 144], P('space')
- grad_channel: float32 [32, 32], replicated
- grad_bias: float32 [32], replicated
All inputs are finite; a program needn't handle non-finite values.
Results may differ from a plain program's by a relative error of at most 0.02.
Values may be sent and summed in bfloat16 or wider, within the bound.
No kernel may reach another device: no remote copies, remote signals or barrier semaphores. Data moves between devices by JAX's collectives and lax.ppermute only.
A program may use at most 128 MiB of HBM per device.

v0:
```python
import math

import jax
import jax.numpy as jnp
from jax import lax
from jax.sharding import PartitionSpec as P

MX = 16
MY = 16
MZ = 9


two_pi = 2.0 * math.pi
highest = lax.Precision.HIGHEST


def signed_index(index, modes):
    return jnp.where(index < modes // 2, index, index - modes)


def plane_table(ny_len, nz_len, my_modes, mz_modes):
    ky_modes = signed_index(jnp.arange(my_modes, dtype=jnp.int32), my_modes)
    kz_modes = jnp.arange(mz_modes, dtype=jnp.int32)
    y_pos = jnp.arange(ny_len, dtype=jnp.int32)
    z_pos = jnp.arange(nz_len, dtype=jnp.int32)
    phases = (
        y_pos[:, None, None, None] * ky_modes[None, None, :, None] * nz_len
        + z_pos[None, :, None, None] * kz_modes[None, None, None, :] * ny_len
    ) % (ny_len * nz_len)
    angles = phases.astype(jnp.float32) * (two_pi / (ny_len * nz_len))
    row_count = ny_len * nz_len
    pair_count = my_modes * mz_modes
    cosine = jnp.cos(angles).reshape(row_count, pair_count)
    sines = -jnp.sin(angles).reshape(row_count, pair_count)
    return jnp.stack([cosine, sines], axis=1).astype(jnp.bfloat16)


def pair_weight(my_modes, mz_modes):
    kz_modes = jnp.arange(my_modes * mz_modes, dtype=jnp.int32) % mz_modes
    return jnp.where(kz_modes == 0, 1.0, 2.0).astype(jnp.float32)


def line_table(kx_index, x_pos, nx_len, mx_modes):
    kx_modes = signed_index(kx_index, mx_modes)
    phases = kx_modes[:, None] * x_pos[None, :] % nx_len
    angles = phases.astype(jnp.float32) * (two_pi / nx_len)
    cosine = jnp.cos(angles)
    sines = jnp.sin(angles)
    upper = jnp.stack([cosine, sines], axis=-1)
    lower = jnp.stack([-sines, cosine], axis=-1)
    return jnp.stack([upper, lower], axis=1)


def mix_modes(weights, spectrum):
    w_real, w_imag = (weights[:, 0], weights[:, 1])
    s_real, s_imag = (spectrum[:, :, :, 0], spectrum[:, :, :, 1])
    form = "aiop,biap->boap"
    real = jnp.einsum(form, w_real, s_real, precision=highest) - jnp.einsum(
        form, w_imag, s_imag, precision=highest
    )
    imag = jnp.einsum(form, w_real, s_imag, precision=highest) + jnp.einsum(
        form, w_imag, s_real, precision=highest
    )
    return jnp.stack([real, imag], axis=3)


def mix_back(weights, grads):
    w_real, w_imag = (weights[:, 0], weights[:, 1])
    g_real, g_imag = (grads[:, :, :, 0], grads[:, :, :, 1])
    form = "aiop,boap->biap"
    real = jnp.einsum(form, w_real, g_real, precision=highest) + jnp.einsum(
        form, w_imag, g_imag, precision=highest
    )
    imag = jnp.einsum(form, w_real, g_imag, precision=highest) - jnp.einsum(
        form, w_imag, g_real, precision=highest
    )
    return jnp.stack([real, imag], axis=3)


def weight_terms(spectrum, grads):
    s_real, s_imag = (spectrum[:, :, :, 0], spectrum[:, :, :, 1])
    g_real, g_imag = (grads[:, :, :, 0], grads[:, :, :, 1])
    form = "boap,biap->aiop"
    real = jnp.einsum(form, g_real, s_real, precision=highest) + jnp.einsum(
        form, g_imag, s_imag, precision=highest
    )
    imag = jnp.einsum(form, g_imag, s_real, precision=highest) - jnp.einsum(
        form, g_real, s_imag, precision=highest
    )
    return jnp.stack([real, imag], axis=1)


def gelu_slope(values):
    return 0.5 * (1.0 + lax.erf(values * (1.0 / math.sqrt(2.0)))) + values * jnp.exp(
        -0.5 * values * values
    ) * (1.0 / math.sqrt(2.0 * math.pi))


def shards(fields, cotangent, spectral_weight, channel_weight, channel_bias):
    cells, chans, planes, ny_len, nz_len = fields.shape
    space_count = lax.axis_size("space")
    pair_count = spectral_weight.shape[4]
    nx_len = planes * space_count
    cell_count = cells * lax.axis_size("dp")
    scale = 1.0 / math.sqrt(nx_len * ny_len * nz_len)
    space_index = lax.axis_index("space")
    my_planes = space_index * planes + jnp.arange(planes, dtype=jnp.int32)
    basis = plane_table(ny_len, nz_len, MY, MZ)
    kz_scale = pair_weight(MY, MZ)
    flat = fields.reshape(cells, chans, planes, ny_len * nz_len)

    def own_modes(spectrum):
        table = line_table(jnp.arange(MX, dtype=jnp.int32), my_planes, nx_len, MX)
        terms = jnp.einsum(
            "aixj,bcxjp->bcaip", table, spectrum.astype(jnp.float32), precision=highest
        )
        result = lax.psum_scatter(
            terms.astype(jnp.bfloat16), "space", scatter_dimension=2, tiled=True
        ).astype(jnp.float32)
        return result

    def spread_modes(modes):
        empty = jnp.zeros((cells, chans, planes, 2, pair_count), jnp.float32)
        piece = lax.all_gather(modes.astype(jnp.bfloat16), "space", axis=2, tiled=True).astype(
            jnp.float32
        )
        mode_pos = jnp.arange(piece.shape[2], dtype=jnp.int32)
        table = line_table(mode_pos, my_planes, nx_len, MX)
        return empty + jnp.einsum("aixj,bcaip->bcxjp", table, piece, precision=highest)

    plane_spec = jnp.einsum(
        "bcxq,qjp->bcxjp", flat, basis, preferred_element_type=jnp.float32
    ).astype(jnp.bfloat16)
    field_modes = scale * own_modes(plane_spec)
    weights = spectral_weight.astype(jnp.float32)
    mixed_modes = mix_modes(weights, field_modes)
    mixed_planes = spread_modes(mixed_modes).astype(jnp.bfloat16) * kz_scale.astype(jnp.bfloat16)
    spectral_out = jnp.einsum(
        "boxjp,qjp->boxq", mixed_planes, basis, preferred_element_type=jnp.float32
    )
    local_out = jnp.einsum(
        "oi,bixq->boxq", channel_weight, flat, preferred_element_type=jnp.float32
    )
    summed = scale * spectral_out + local_out + channel_bias[None, :, None, None]
    upstream = cotangent.reshape(cells, chans, planes, ny_len * nz_len)
    hidden = (upstream.astype(jnp.float32) * gelu_slope(summed)).astype(jnp.bfloat16)
    back_planes = (
        jnp.einsum("boxq,qjp->boxjp", hidden, basis, preferred_element_type=jnp.float32)
        * (scale * kz_scale)
    ).astype(jnp.bfloat16)
    grad_modes_out = own_modes(back_planes)
    grad_modes_in = mix_back(weights, grad_modes_out)
    grad_planes = (scale * spread_modes(grad_modes_in)).astype(jnp.bfloat16)
    spectral_back = jnp.einsum(
        "bcxjp,qjp->bcxq", grad_planes, basis, preferred_element_type=jnp.float32
    )
    local_back = jnp.einsum(
        "oi,boxq->bixq", channel_weight, hidden, preferred_element_type=jnp.float32
    )
    grad_fields = (spectral_back + local_back).astype(jnp.bfloat16).reshape(fields.shape)
    cell_norm = 1.0 / math.sqrt(cell_count)
    grad_spectral = (
        lax.psum(weight_terms(field_modes, grad_modes_out).astype(jnp.bfloat16), "dp").astype(
            jnp.float32
        )
        * cell_norm
    )
    voxel_norm = 1.0 / math.sqrt(cell_count * nx_len * ny_len * nz_len)
    local_channel = jnp.einsum("boxq,bixq->oi", hidden, flat, preferred_element_type=jnp.float32)
    local_bias = jnp.sum(hidden, axis=(0, 2, 3), dtype=jnp.float32)
    channel_total, bias_total = lax.psum((local_channel, local_bias), ("dp", "space"))
    return (grad_fields, grad_spectral, channel_total * voxel_norm, bias_total * voxel_norm)


def solution(mesh):
    in_specs = (
        P("dp", None, "space", None, None),
        P("dp", None, "space", None, None),
        P("space", None, None, None, None),
        P(),
        P(),
    )
    out_specs = (P("dp", None, "space", None, None), P("space", None, None, None, None), P(), P())
    return jax.shard_map(shards, mesh=mesh, in_specs=in_specs, out_specs=out_specs, check_vma=False)
```

profile of v0, /device:TPU:1, one launch (start us, length us, event | category | flops | bytes accessed | tf_op | source)
XLA Modules:
  0.0 333.3 jit_solution(13315554155920800230)
XLA Ops:
  7.5 5.2 %reshape.544 = bf16[32,8,5120,1]{2,1,0,3:T(8,128)(2,1)} reshape(bf16[1,32,8,40,128]{4,3,2,1,0:T(8,128)(2,1)} %param.5) | data formatting | bytes 5242880 | tf_op jit(solution)/shard_map/reshape.8
  12.6 2.3 add_remainder_fusion
  14.9 2.7 rem.77
  17.6 11.1 %cosine_convert_fusion = (bf16[5120,1,144]{0,2,1:T(8,128)(2,1)S(1)}, bf16[5120,1,144]{0,2,1:T(8,128)(2,1)S(1)}) fusion(s32[5120,1,144]{0,2,1:T(8,128)S(1)} %rem.77), kind=kLoop, calls=%fused_computation.49 | loop fusion | flops 7372800 | bytes 5898240 | tf_op jit(solution)/shard_map/convert.31
  28.8 2.0 fusion.24
  30.9 0.6 fusion.50
  32.0 1.4 reshape.579
  33.7 2.5 reshape.531
  36.2 5.4 %reshape.542 = f32[1,32,8,5120]{3,2,1,0:T(8,128)} reshape(bf16[1,32,8,40,128]{4,3,2,1,0:T(8,128)(2,1)} %param.6) | data formatting | bytes 7864320 | tf_op jit(solution)/shard_map/convert_element_type | solution.py:146
  41.7 6.0 %fusion.37 = f32[8,5120,32]{1,2,0:T(8,128)} fusion(bf16[32,8,5120]{2,1,0:T(8,128)(2,1)S(1)} %copy-done.3, bf16[32,32]{1,0:T(8,128)(2,1)S(1)} %copy-done), kind=kOutput, calls=%fused_computation.58 | convolution fusion | flops 83886080 | bytes 7866368 | tf_op jit(solution)/shard_map/oi,bixq->boxq/dot_general | solution.py:141
  47.7 1.3 reshape.580
  49.7 6.0 %fusion = (f32[8,144,32]{1,2,0:T(8,128)S(1)}, f32[8,144,32]{1,2,0:T(8,128)S(1)}, f32[8,144,32]{1,2,0:T(8,128)S(1)}, f32[8,144,32]{1,2,0:T(8,128)S(1)}) fusion(f32[8,144,32]{1,2,0:T(8,128)S(1)} %copy.125, bf16[8,2,32,32,144]{4,3,2,1,0:T(8,128)(2,1)} %param.7, f32[8,144,32]{1,2,0:T(8,128)S(1)} %copy.126), kind=kLoop, calls=%fused_computation.9 | loop fusion | flops 11649024 | bytes 5603328
  55.7 0.6 fusion.81
  56.4 9.0 %all_gather.6 = bf16[1,32,16,2,144]{4,2,3,1,0:T(8,128)(2,1)S(1)} all-gather(bf16[1,32,8,2,144]{4,2,3,1,0:T(8,128)(2,1)S(1)} %pad_maximum_fusion.2), channel_id=1, replica_groups=mesh['dp'=16,'space'=2] {'space'}, dimensions={2}, use_global_device_ids=true | all-gather | bytes 442368 | tf_op jit(solution)/shard_map/all_gather | solution.py:124
  65.9 6.6 %convert_reduce_fusion = (f32[32]{0:T(128)S(1)}, bf16[1,32,8,5120]{3,2,1,0:T(8,128)(2,1)S(1)}) fusion(f32[1,32,8,5120]{3,2,1,0:T(8,128)S(1)} %copy-done.11, f32[32]{0:T(128)S(1)} %copy-done.13, f32[8,5120,32]{1,2,0:T(8,128)S(1)} %bitcast.304, bf16[32,8,2,144]{3,1,2,0:T(8,128)(2,1)S(1)} %fusion.67, bf16[5120,1,144]{0,2,1:T(8,128)(2,1)S(1)} %copy-done.9, ...), kind=kOutput, calls=%fused_computation.35 | convolution fusion | flops 776110080 | bytes 16204032 | tf_op jit(solution)/shard_map/boxjp,qjp->boxq/dot_general | solution.py:138
  72.5 5.5 %fusion.68 = f32[32,32]{1,0:T(8,128)S(1)} fusion(bf16[32,8,5120]{2,1,0:T(8,128)(2,1)S(1)} %copy-done.4, bf16[32,8,5120]{2,1,0:T(8,128)(2,1)S(1)} %bitcast.301), kind=kOutput, calls=%fused_computation.79 | convolution fusion | flops 83886080 | bytes 5246976 | tf_op jit(solution)/shard_map/boxq,bixq->oi/dot_general | solution.py:169
  78.0 1.6 fusion.61
  79.7 0.6 fusion.49
  80.3 1.3 copy.204
  81.6 2.4 reshape.581
  84.1 41.1 %all-reduce = (f32[32,32]{1,0:T(8,128)S(1)}, f32[32]{0:T(128)S(1)}) all-reduce(f32[32,32]{1,0:T(8,128)S(1)} %fusion.68, f32[32]{0:T(128)S(1)} %get-tuple-element.43), channel_id=1, replica_groups=mesh['dp'=16,'space'=2] {'dp','space'}, use_global_device_ids=true, to_apply=%region_3.4 | all-reduce | flops 1056 | bytes 8448 | tf_op jit(solution)/shard_map/psum | solution.py:171
  125.2 0.6 broadcast_multiply_fusion
  125.8 4.1 %fusion.34 = f32[8,5120,32]{1,2,0:T(8,128)} fusion(bf16[32,8,5120]{2,1,0:T(8,128)(2,1)S(1)} %bitcast.302, bf16[32,32]{1,0:T(8,128)(2,1)S(1)} %copy-done), kind=kOutput, calls=%fused_computation.55 | convolution fusion | flops 83886080 | bytes 7866368 | tf_op jit(solution)/shard_map/oi,boxq->bixq/dot_general | solution.py:157
  129.9 1.3 reshape.582
  132.2 4.0 %fusion.20 = (bf16[8,1,32,32,144]{4,3,2,1,0:T(8,128)(2,1)S(1)}, bf16[8,1,32,32,144]{4,3,2,1,0:T(8,128)(2,1)}) fusion(f32[8,144,32]{1,2,0:T(8,128)S(1)} %copy.126, f32[8,144,32]{1,2,0:T(8,128)S(1)} %copy.125, f32[8,144,32]{1,2,0:T(8,128)S(1)} %copy.34, f32[8,144,32]{1,2,0:T(8,128)S(1)} %copy.32), kind=kLoop, calls=%fused_computation.37 | loop fusion | flops 9437184 | bytes 5308416 | tf_op jit(solution)/shard_map/stack | solution.py:90
  136.2 7.2 %pad_maximum_fusion = bf16[8,2,32,32,144]{4,3,2,1,0:T(8,128)(2,1)} fusion(bf16[8,1,32,32,144]{4,3,2,1,0:T(8,128)(2,1)} %get-tuple-element.29, bf16[8,1,32,32,144]{4,3,2,1,0:T(8,128)(2,1)S(1)} %get-tuple-element.28), kind=kLoop, calls=%fused_computation.17 | loop fusion | flops 2359296 | bytes 9437184 | tf_op jit(solution)/shard_map/stack | solution.py:90
  144.2 10.1 %fusion.4 = (f32[8,144,32]{1,2,0:T(8,128)S(1)}, f32[8,144,32]{1,2,0:T(8,128)S(1)}, f32[8,144,32]{1,2,0:T(8,128)S(1)}, f32[8,144,32]{1,2,0:T(8,128)S(1)}) fusion(f32[8,144,32]{1,2,0:T(8,128)S(1)} %copy.127, bf16[8,2,32,32,144]{4,3,2,1,0:T(8,128)(2,1)} %param.7, f32[8,144,32]{1,2,0:T(8,128)S(1)} %copy.128), kind=kLoop, calls=%fused_computation.13 | loop fusion | flops 11649024 | bytes 5603328
  154.9 7.2 %all_gather.7 = bf16[1,32,16,2,144]{4,2,3,1,0:T(8,128)(2,1)S(1)} all-gather(bf16[1,32,8,2,144]{4,2,3,1,0:T(8,128)(2,1)S(1)} %pad_maximum_fusion.3), channel_id=1, replica_groups=mesh['dp'=16,'space'=2] {'space'}, dimensions={2}, use_global_device_ids=true | all-gather | bytes 442368 | tf_op jit(solution)/shard_map/all_gather | solution.py:124
  162.5 4.0 %fusion.39 = bf16[1,32,8,40,128]{4,2,3,1,0:T(8,128)(2,1)S(1)} fusion(f32[8,5120,32]{1,2,0:T(8,128)S(1)} %bitcast.300, bf16[32,8,2,144]{3,1,2,0:T(8,128)(2,1)S(1)} %fusion.59, bf16[5120,1,144]{0,2,1:T(8,128)(2,1)S(1)} %copy-done.10, bf16[5120,1,144]{0,2,1:T(8,128)(2,1)S(1)} %copy-done.7), kind=kOutput, calls=%fused_computation.60 | convolution fusion | flops 759070720 | bytes 10960896 | tf_op jit(solution)/shard_map/bcxjp,qjp->bcxq/dot_general | solution.py:154
  166.5 2.0 copy.38
  168.5 145.7 %all-reduce.3.cloned.1.call-done = bf16[8,2,32,32,144]{4,3,2,1,0:T(8,128)(2,1)} async-done(((bf16[8,2,32,32,144]{4,3,2,1,0:T(8,128)(2,1)}), bf16[8,2,32,32,144]{4,3,2,1,0:T(8,128)(2,1)}) %all-reduce.3.cloned.1.call-update) | async-done | bytes 4718608 | tf_op jit(solution)/shard_map/psum | solution.py:163
  314.3 12.0 %convert_multiply_fusion = f32[8,2,32,32,144]{4,3,2,1,0:T(8,128)} fusion(bf16[8,2,32,32,144]{4,3,2,1,0:T(8,128)(2,1)} %all-reduce.3.cloned.1.call-done), kind=kLoop, calls=%fused_computation | loop fusion | flops 4718592 | bytes 14155776 | tf_op jit(solution)/shard_map/mul | solution.py:163
  (73 shorter events, 4.9 us)
Async XLA Ops:
  7.2 34.5 %copy-start = (bf16[32,32]{1,0:T(8,128)(2,1)S(1)}, bf16[32,32]{1,0:T(8,128)(2,1)}, u32[]{:S(2)}) copy-start(bf16[32,32]{1,0:T(8,128)(2,1)} %param.8) | copy-start | bytes 6148
  7.2 40.5 %reduce-scatter.7.cloned.1.call-start = ((), (), s32[]{:S(2)}) async-start(), calls=%async_computation.3 | async-start | bytes 442368
  17.6 11.2 %copy-start.12 = (bf16[32,8,5120,1]{2,1,0,3:T(8,128)(2,1)S(1)}, bf16[32,8,5120,1]{2,1,0,3:T(8,128)(2,1)}, u32[]{:S(2)}) copy-start(bf16[32,8,5120,1]{2,1,0,3:T(8,128)(2,1)} %reshape.544) | copy-start | bytes 7864324
  28.8 2.1 copy-start.5
  28.8 2.1 copy-start.8
  30.9 2.8 copy-start.2
  33.5 96.4 %reduce-scatter.9.cloned.1.call-start = ((), (), s32[]{:S(2)}) async-start(), calls=%async_computation.4 | async-start | bytes 442368
  36.2 5.4 %copy-start.3 = (bf16[32,8,5120]{2,1,0:T(8,128)(2,1)S(1)}, bf16[32,8,5120]{2,1,0:T(8,128)(2,1)}, u32[]{:S(2)}) copy-start(bf16[32,8,5120]{2,1,0:T(8,128)(2,1)} %reshape.531) | copy-start | bytes 7864324
  49.6 16.2 %slice-start.2 = ((s8[5242880]{0:T(1024)(128)(4,1)}), s8[4194304]{0:T(1024)(128)(4,1)S(1)}, s32[]{:S(2)}) async-start(s8[5242880]{0:T(1024)(128)(4,1)} %bitcast.303), calls=%async_computation.7 | async-start | bytes 8388608
  49.7 16.2 %copy-start.6 = (bf16[5120,1,144]{0,2,1:T(8,128)(2,1)S(1)}, bf16[5120,1,144]{0,2,1:T(8,128)(2,1)}, u32[]{:S(2)}) copy-start(bf16[5120,1,144]{0,2,1:T(8,128)(2,1)} %copy-done.5) | copy-start | bytes 4423684
  49.7 16.2 %copy-start.9 = (bf16[5120,1,144]{0,2,1:T(8,128)(2,1)S(1)}, bf16[5120,1,144]{0,2,1:T(8,128)(2,1)}, u32[]{:S(2)}) copy-start(bf16[5120,1,144]{0,2,1:T(8,128)(2,1)} %copy-done.8) | copy-start | bytes 4423684
  49.7 16.2 %slice-start.3 = ((s8[5242880]{0:T(1024)(128)(4,1)}), s8[1048576]{0:T(1024)(128)(4,1)S(1)}, s32[]{:S(2)}) async-start(s8[5242880]{0:T(1024)(128)(4,1)} %bitcast.303), calls=%async_computation.8 | async-start | bytes 2097152
  49.7 16.2 %copy-start.11 = (f32[1,32,8,5120]{3,2,1,0:T(8,128)S(1)}, f32[1,32,8,5120]{3,2,1,0:T(8,128)}, u32[]{:S(2)}) copy-start(f32[1,32,8,5120]{3,2,1,0:T(8,128)} %reshape.542) | copy-start | bytes 15728644
  49.7 16.2 %copy-start.13 = (f32[32]{0:T(128)S(1)}, f32[32]{0:T(128)}, u32[]{:S(2)}) copy-start(f32[32]{0:T(128)} %param.9) | copy-start | bytes 388
  65.9 6.6 %copy-start.4 = (bf16[32,8,5120]{2,1,0:T(8,128)(2,1)S(1)}, bf16[32,8,5120]{2,1,0:T(8,128)(2,1)}, u32[]{:S(2)}) copy-start(bf16[32,8,5120]{2,1,0:T(8,128)(2,1)} %reshape.531) | copy-start | bytes 7864324
  84.0 230.2 %all-reduce.3.cloned.1.call-start = ((), (), s32[]{:S(2)}) async-start(), calls=%async_computation.2 | async-start | bytes 16777216 | tf_op jit(solution)/shard_map/psum | solution.py:163
  144.0 18.5 %slice-start = ((s8[5242880]{0:T(1024)(128)(4,1)}), s8[4194304]{0:T(1024)(128)(4,1)S(1)}, s32[]{:S(2)}) async-start(s8[5242880]{0:T(1024)(128)(4,1)} %bitcast.299), calls=%async_computation.5 | async-start | bytes 8388608
  144.1 18.4 %slice-start.1 = ((s8[5242880]{0:T(1024)(128)(4,1)}), s8[1048576]{0:T(1024)(128)(4,1)S(1)}, s32[]{:S(2)}) async-start(s8[5242880]{0:T(1024)(128)(4,1)} %bitcast.299), calls=%async_computation.6 | async-start | bytes 2097152
  144.2 18.4 %copy-start.7 = (bf16[5120,1,144]{0,2,1:T(8,128)(2,1)S(1)}, bf16[5120,1,144]{0,2,1:T(8,128)(2,1)}, u32[]{:S(2)}) copy-start(bf16[5120,1,144]{0,2,1:T(8,128)(2,1)} %copy-done.5) | copy-start | bytes 4423684
  144.2 18.4 %copy-start.10 = (bf16[5120,1,144]{0,2,1:T(8,128)(2,1)S(1)}, bf16[5120,1,144]{0,2,1:T(8,128)(2,1)}, u32[]{:S(2)}) copy-start(bf16[5120,1,144]{0,2,1:T(8,128)(2,1)} %copy-done.8) | copy-start | bytes 4423684
  314.3 12.0 %copy-start.1 = (bf16[32,32]{1,0:T(8,128)(2,1)S(1)}, bf16[32,32]{1,0:T(8,128)(2,1)}, u32[]{:S(2)}) copy-start(bf16[32,32]{1,0:T(8,128)(2,1)} %param.8) | copy-start | bytes 6148
Sparse Core Ops, SparseCore 0:
  33.6 14.1 reduce-scatter.6
  84.2 14.3 reduce-scatter.8
  143.6 170.6 all-reduce.2
where the time goes:
time: 339 us; the launch traced here: 333 us
  waiting for transfers between devices  146 us (43%)
  blocking collectives  57.2 us (17%)
  other arithmetic  56 us (17%)
  matrix products  32 us (9%)
  local copies, waits for them, and re-layouts  27.2 us (8%)
  between operations  14.8 us (4%)
    psum x1, waiting for transfers between devices, shards(): lax.psum(weight_terms(field_modes, grad_modes_out).astype(jnp.bfloat16),...  146 us
    psum x1, blocking collectives, shards(): lax.psum((local_channel, local_bias), ('dp', 'space'))  41.1 us
    all_gather x2, blocking collectives, spread_modes(): lax.all_gather(modes.astype(jnp.bfloat16), 'space', axis=2, tiled=True)  16.1 us
    unnamed x4, other arithmetic  16.1 us
    mul x1, other arithmetic, shards(): lax.psum(weight_terms(field_modes, grad_modes_out).astype(jnp.bfloat16),...  12 us
    another operation x3, other arithmetic  11.5 us
    another operation x2, other arithmetic, weight_terms(): return jnp.stack([real, imag], axis=1)  11.2 us
    unnamed x48, local copies, waits for them, and re-layouts  10.8 us
  transfers between devices with their start and end apart: 3, of which 1 were waited for; matrix products, arithmetic and copies ran while one was open for 11% of the time, Pallas kernels for 0%

commit v1 on v0

v1 whole, which is shorter than its diff:
```python
import functools
import math

import jax
import jax.numpy as jnp
import ml_dtypes
import numpy as np
from jax import lax
from jax.experimental import pallas as pl
from jax.experimental.pallas import tpu as pltpu
from jax.sharding import PartitionSpec as P

MX = 16
MY = 16
MZ = 9
LANES = 128
BF16 = jnp.bfloat16
F32 = jnp.float32
VMEM_LIMIT = 50 * 1024 * 1024
TWO_PI = 2.0 * math.pi


def signed(index, modes):
    return np.where(index < modes // 2, index, index - modes)


def plane_columns(own):
    pairs = MY * MZ
    rest = pairs - LANES
    return np.concatenate([np.arange(LANES), LANES + np.tile(np.arange(rest), own)])


def plane_table(ny_len, nz_len, own):
    ky = signed(np.arange(MY), MY)
    kz = np.arange(MZ)
    y_pos = np.arange(ny_len)
    z_pos = np.arange(nz_len)
    phases = (
        y_pos[:, None, None, None] * ky[None, None, :, None] * nz_len
        + z_pos[None, :, None, None] * kz[None, None, None, :] * ny_len
    ) % (ny_len * nz_len)
    angles = phases.astype(np.float32) * np.float32(TWO_PI / (ny_len * nz_len))
    angles = angles.reshape(ny_len * nz_len, MY * MZ)
    columns = plane_columns(own)
    table = np.zeros((ny_len * nz_len, 2, 2 * LANES), np.float32)
    table[:, 0, : len(columns)] = np.cos(angles)[:, columns]
    table[:, 1, : len(columns)] = -np.sin(angles)[:, columns]
    return table.reshape(ny_len * nz_len, 4 * LANES).astype(ml_dtypes.bfloat16)


def column_weight(own, scale):
    columns = plane_columns(own)
    weight = np.zeros((2, 2 * LANES), np.float32)
    weight[:, : len(columns)] = np.where(columns % MZ == 0, 1.0, 2.0)
    return (weight * scale).reshape(1, 4 * LANES).astype(np.float32)


def line_tables(chans, planes, count):
    own = MX // count
    length = planes * count
    tables = []
    for s in range(count):
        place = (s + np.arange(count)) % count
        index = (place[:, None] * own + np.arange(own)[None, :]).reshape(-1)
        phases = signed(index, MX)[:, None] * (s * planes + np.arange(planes))[None, :] % length
        angles = phases.astype(np.float32) * np.float32(TWO_PI / length)
        cosine, sines = np.cos(angles), np.sin(angles)
        line = np.stack([np.stack([cosine, sines], -1), np.stack([-sines, cosine], -1)], 1)
        whole = np.einsum("arxj,cd->arcjdx", line, np.eye(chans, dtype=np.float32))
        tables.append(whole.reshape(MX * 2 * chans, 2 * chans * planes))
    return np.stack(tables).astype(ml_dtypes.bfloat16)


def dot(left, right):
    return jnp.dot(left, right, preferred_element_type=F32)


def dot_nt(left, right):
    return lax.dot_general(left, right, (((1,), (1,)), ((), ())), preferred_element_type=F32)


def tail_mask(a, rows, rest):
    lane = lax.broadcasted_iota(jnp.int32, (rows, LANES), 1)
    return (lane >= a * rest) & (lane < (a + 1) * rest)


def spread_rows(block_ref, rows_ref, out_ref, start):
    count, ny_len, nz_len = block_ref.shape
    rows_ref[...] = block_ref[...].astype(F32).reshape(count * ny_len, nz_len)
    for y in range(ny_len):
        piece = rows_ref[pl.ds(y, count, stride=ny_len), :]
        out_ref[pl.ds(start, count), y * nz_len : (y + 1) * nz_len] = piece.astype(BF16)


def emit_modes(terms, refs, own, rest):
    height = terms.shape[0] // (own * len(refs))
    for k, ref in enumerate(refs):
        tail = jnp.zeros((height, LANES), F32)
        for a in range(own):
            first = (k * own + a) * height
            block = terms[first : first + height]
            ref[a] = block[:, :LANES].astype(ref.dtype)
            tail = jnp.where(tail_mask(a, height, rest), block[:, LANES:], tail)
        ref[own] = tail.astype(ref.dtype)


def line_forward(spec, line_ref):
    half = 2 * LANES
    depth = line_ref.shape[2] // 2
    return dot(line_ref[0, :, :depth], spec[:, :half]) + dot(line_ref[0, :, depth:], spec[:, half:])


def planes_of(mode_refs, inverse_ref, weight_ref, stack_ref, planes_ref, own, rest):
    height = mode_refs[0].shape[1]
    half = 2 * LANES
    for k, ref in enumerate(mode_refs):
        tail = ref[own].astype(F32)
        for a in range(own):
            first = (k * own + a) * height
            stack_ref[first : first + height, :LANES] = ref[a]
            masked = jnp.where(tail_mask(a, height, rest), tail, 0.0)
            stack_ref[first : first + height, LANES:] = masked.astype(BF16)
    depth = inverse_ref.shape[1] // 2
    for j in range(2):
        part = dot(inverse_ref[0, j * depth : (j + 1) * depth, :], stack_ref[...])
        columns = slice(j * half, (j + 1) * half)
        planes_ref[:, columns] = (part * weight_ref[:, columns]).astype(BF16)


def gelu_slope(values):
    size = jnp.abs(values) * (1.0 / math.sqrt(2.0))
    bell = jnp.exp(-(size * size))
    t = 1.0 / (1.0 + 0.3275911 * size)
    poly = t * (
        0.127414796 + t * (-0.142248368 + t * (0.7107068705 + t * (-0.7265760135 + t * 0.5307027145)))
    )
    tail = poly * bell
    upper = jnp.where(values >= 0.0, 1.0 - tail, tail)
    return upper + values * bell * (1.0 / math.sqrt(2.0 * math.pi))


def forward_kernel(own, rest, count, s_ref, fields_ref, line_ref, basis_hbm, flat_ref, *more):
    outs, (rows_ref, basis_ref, sem) = more[:count], more[count:]
    step = pl.program_id(0)
    copy = pltpu.make_async_copy(basis_hbm, basis_ref, sem)

    @pl.when(step == 0)
    def _():
        copy.start()

    rows = fields_ref.shape[0]
    spread_rows(fields_ref, rows_ref, flat_ref, pl.multiple_of(step * rows, rows))

    @pl.when(step == pl.num_programs(0) - 1)
    def _():
        copy.wait()
        spec = dot(flat_ref[...], basis_ref[...]).astype(BF16)
        emit_modes(line_forward(spec, line_ref), outs, own, rest)


def relayout_kernel(block_ref, out_ref, rows_ref):
    spread_rows(block_ref, rows_ref, out_ref, 0)


def sum_modes(mode_refs, scale, total_ref, out_ref, own):
    for blk in range(own + 1):
        total = mode_refs[0][blk]
        for ref in mode_refs[1:]:
            total = total + ref[blk].astype(F32)
        total = total * scale
        total_ref[blk] = total
        out_ref[blk] = total.astype(BF16)


def load_wide(total_ref, wide_ref, a, own, rest):
    wide_ref[:, :LANES] = total_ref[a]
    wide_ref[:, LANES:] = pltpu.roll(total_ref[own], lax.rem(LANES - a * rest, LANES), 1)


def store_wide(wide_ref, tail_ref, out_ref, a, own, rest):
    out_ref[a] = wide_ref[:, :LANES].astype(BF16)
    moved = pltpu.roll(wide_ref[:, LANES:], a * rest, 1)
    height = moved.shape[0]
    tail_ref[...] = jnp.where(tail_mask(a, height, rest), moved, tail_ref[...])

    @pl.when(a == own - 1)
    def _():
        out_ref[own] = tail_ref[...].astype(BF16)


def mix_kernel(own, rest, count, scale, *refs):
    modes, (weight_ref, out_ref, sum_ref) = refs[:count], refs[count : count + 3]
    total_ref, wide_ref, result_ref, tail_ref = refs[count + 3 :]
    a = pl.program_id(0)

    @pl.when(a == 0)
    def _():
        sum_modes(modes, scale, total_ref, sum_ref, own)
        result_ref[...] = jnp.zeros_like(result_ref)
        tail_ref[...] = jnp.zeros_like(tail_ref)

    load_wide(total_ref, wide_ref, a, own, rest)
    chans = weight_ref.shape[2]
    pairs = weight_ref.shape[4]
    real = jnp.zeros((chans, pairs), F32)
    imag = jnp.zeros((chans, pairs), F32)
    for i in range(chans):
        w_real = weight_ref[0, 0, i].astype(F32)
        w_imag = weight_ref[0, 1, i].astype(F32)
        u_real = wide_ref[i : i + 1, :pairs]
        u_imag = wide_ref[chans + i : chans + i + 1, :pairs]
        real = real + (w_real * u_real - w_imag * u_imag)
        imag = imag + (w_real * u_imag + w_imag * u_real)
    result_ref[:chans, :pairs] = real
    result_ref[chans:, :pairs] = imag
    store_wide(result_ref, tail_ref, out_ref, a, own, rest)


def mix_back_kernel(own, rest, count, *refs):
    modes, (chan_ref, weight_ref, out_ref, sum_ref) = refs[:count], refs[count : count + 4]
    total_ref, wide_ref, result_ref, tail_ref = refs[count + 4 :]
    a = pl.program_id(0)
    chans = weight_ref.shape[2]
    pairs = weight_ref.shape[4]

    @pl.when(a == 0)
    def _():
        sum_modes(modes, 1.0, total_ref, sum_ref, own)
        chan = chan_ref[...]
        for ref in modes[1:]:
            chan = chan + (ref[own + 1, :chans].astype(F32) + ref[own + 1, chans:].astype(F32))
        upper = chan.astype(BF16)
        sum_ref[own + 1, :chans] = upper
        sum_ref[own + 1, chans:] = (chan - upper.astype(F32)).astype(BF16)
        result_ref[...] = jnp.zeros_like(result_ref)
        tail_ref[...] = jnp.zeros_like(tail_ref)

    load_wide(total_ref, wide_ref, a, own, rest)
    g_real = wide_ref[:chans, :pairs]
    g_imag = wide_ref[chans:, :pairs]
    for i in range(chans):
        w_real = weight_ref[0, 0, i].astype(F32)
        w_imag = weight_ref[0, 1, i].astype(F32)
        real = jnp.sum(w_real * g_real + w_imag * g_imag, axis=0, keepdims=True)
        imag = jnp.sum(w_real * g_imag - w_imag * g_real, axis=0, keepdims=True)
        result_ref[i : i + 1, :pairs] = real
        result_ref[chans + i : chans + i + 1, :pairs] = imag
    store_wide(result_ref, tail_ref, out_ref, a, own, rest)


def middle_kernel(own, rest, count, planes, s_ref, *refs):
    modes, refs = refs[:count], refs[count:]
    inverse_ref, line_ref, weight_ref, mix_ref, bias_ref, flat_ref, cot_ref, basis_ref = refs[:8]
    hidden_ref, chan_ref, refs = refs[8], refs[9], refs[10:]
    outs, (stack_ref, planes_ref, back_ref, cross_ref) = refs[:count], refs[count:]
    step = pl.program_id(0)

    @pl.when(step == 0)
    def _():
        planes_of(modes, inverse_ref, weight_ref, stack_ref, planes_ref, own, rest)
        back_ref[...] = jnp.zeros_like(back_ref)
        cross_ref[...] = jnp.zeros_like(cross_ref)

    flat = flat_ref[...]
    summed = dot_nt(planes_ref[...], basis_ref[...]) + dot(mix_ref[...], flat) + bias_ref[...]
    hidden = (cot_ref[...].astype(F32) * gelu_slope(summed)).astype(BF16)
    hidden_ref[...] = hidden
    back_ref[...] += dot(hidden, basis_ref[...])
    cross_ref[...] += dot_nt(hidden, flat)

    @pl.when(step == pl.num_programs(0) - 1)
    def _():
        back = back_ref[...]
        spec = (back * weight_ref[...]).astype(BF16)
        emit_modes(line_forward(spec, line_ref), outs, own, rest)
        rows = cross_ref.shape[0]
        chans = rows // planes
        row = lax.broadcasted_iota(jnp.int32, (rows, rows), 0)
        column = lax.broadcasted_iota(jnp.int32, (rows, rows), 1)
        same = lax.rem(row, planes) == lax.rem(column, planes)
        cross = jnp.where(same, cross_ref[...], 0.0)
        row = lax.broadcasted_iota(jnp.int32, (chans, rows), 0)
        column = lax.broadcasted_iota(jnp.int32, (chans, rows), 1)
        group = jnp.where((column >= row * planes) & (column < (row + 1) * planes), 1.0, 0.0)
        row = lax.broadcasted_iota(jnp.int32, (rows, LANES), 0)
        column = lax.broadcasted_iota(jnp.int32, (rows, LANES), 1)
        place = jnp.where((row >= column * planes) & (row < (column + 1) * planes), 1.0, 0.0)
        exact = functools.partial(jnp.dot, preferred_element_type=F32, precision=lax.Precision.HIGHEST)
        sums = jnp.where(column == chans, back[:, :1], 0.0)
        chan = exact(group, exact(cross, place) + sums)
        chan_ref[...] = chan
        upper = chan.astype(BF16)
        lower = (chan - upper.astype(F32)).astype(BF16)
        for ref in outs[1:]:
            ref[own + 1, :chans] = upper
            ref[own + 1, chans:] = lower


def last_kernel(own, rest, count, steps, s_ref, *refs):
    modes, refs = refs[:count], refs[count:]
    inverse_ref, weight_ref, mix_ref, hidden_ref, basis_ref, out_ref = refs[:6]
    stack_ref, planes_ref, rows_ref = refs[6:]
    step = pl.program_id(0)
    block, ny_len, nz_len = out_ref.shape
    rows = planes_ref.shape[0]

    @pl.when(step == 0)
    def _():
        planes_of(modes, inverse_ref, weight_ref, stack_ref, planes_ref, own, rest)

    @pl.when(step < steps)
    def _():
        total = dot_nt(planes_ref[...], basis_ref[...]) + dot(mix_ref[...], hidden_ref[...])
        group = total.shape[1] // nz_len
        for y in range(group):
            rows_ref[pl.ds(step * group + y, rows, stride=ny_len), :] = total[:, y * nz_len : (y + 1) * nz_len]

    @pl.when(step >= steps)
    def _():
        start = pl.multiple_of((step - steps) * (block * ny_len), block * ny_len)
        piece = rows_ref[pl.ds(start, block * ny_len), :]
        out_ref[...] = piece.reshape(block, ny_len, nz_len).astype(BF16)


def outer_kernel(own, rest, cells, cell_norm, voxel_norm, *refs):
    u_refs, g_refs, c_refs = refs[:cells], refs[cells : 2 * cells], refs[2 * cells : 3 * cells]
    out_ref, chan_ref, u_all, g_all, tail_ref = refs[3 * cells :]
    step = pl.program_id(0)
    chans = g_all.shape[2]
    for b in range(cells):
        g_real = g_refs[b][0, :chans].astype(F32)
        g_imag = g_refs[b][0, chans:].astype(F32)
        u_real = u_refs[b][0, :chans].astype(F32) * cell_norm
        u_imag = u_refs[b][0, chans:].astype(F32) * cell_norm
        g_all[b, 0] = g_real + g_imag
        g_all[b, 1] = g_real
        g_all[b, 2] = g_imag
        u_all[b, 0] = u_real
        u_all[b, 1] = u_real + u_imag
        u_all[b, 2] = u_real - u_imag

    def products(i):
        sums = [None] * 3
        for b in range(cells):
            for t in range(3):
                term = u_all[b, t, pl.ds(i, 1), :] * g_all[b, t]
                sums[t] = term if sums[t] is None else sums[t] + term
        return sums[0] - sums[2], sums[0] - sums[1]

    @pl.when(step == 0)
    def _():
        chan = jnp.zeros(chan_ref.shape, F32)
        for ref in c_refs:
            chan = chan + (ref[0, :chans].astype(F32) + ref[0, chans:].astype(F32))
        chan_ref[...] = chan * voxel_norm

        @pl.loop(0, chans)
        def _(i):
            real, imag = products(i)
            tail_ref[0, i] = real
            tail_ref[1, i] = imag

    @pl.when(step > 0)
    def _():
        a = step - 1
        shift = lax.rem(LANES - a * rest, LANES)

        @pl.loop(0, chans)
        def _(i):
            for r, main in enumerate(products(i)):
                out_ref[0, r, i, :, :LANES] = main
                moved = pltpu.roll(tail_ref[r, i], shift, 1)
                out_ref[0, r, i, :, LANES:] = moved[:, :rest]


def params(**kw):
    return pltpu.CompilerParams(vmem_limit_bytes=VMEM_LIMIT, **kw)


def whole(shape):
    return pl.BlockSpec(shape, lambda *_: (0,) * len(shape))


def at_place(shape):
    return pl.BlockSpec((1,) + shape, lambda i, s: (s[0],) + (0,) * len(shape))


def relayout(array, rows):
    total, ny_len, nz_len = array.shape
    return pl.pallas_call(
        relayout_kernel,
        grid=(total // rows,),
        in_specs=[pl.BlockSpec((rows, ny_len, nz_len), lambda i: (i, 0, 0))],
        out_specs=pl.BlockSpec((rows, ny_len * nz_len), lambda i: (i, 0)),
        out_shape=jax.ShapeDtypeStruct((total, ny_len * nz_len), BF16),
        scratch_shapes=[pltpu.VMEM((rows * ny_len, nz_len), F32)],
        compiler_params=params(),
        name="relayout",
    )(array)


def send(array, axis, count, shift):
    return lax.ppermute(array, axis, [(i, (i + shift) % count) for i in range(count)])


def swap(array, bit, count):
    return lax.ppermute(array, "dp", [(i, i ^ bit) for i in range(count)])


def gather_cells(array, count):
    if count & (count - 1) or count < 4:
        every = lax.all_gather(array, "dp")
        return [every[b] for b in range(count)]
    pieces = [array, swap(array, 2, count)]
    for z in range(1, count // 4):
        far = swap(array, 4 * z, count)
        pieces += [far, swap(far, 2, count)]
    return pieces + [swap(piece, 1, count) for piece in pieces]


def shards(count, cell_count, fields, cotangent, spectral_weight, channel_weight, channel_bias):
    _, chans, planes, ny_len, nz_len = fields.shape
    own, _, _, _, pairs = spectral_weight.shape
    rest = pairs - LANES
    rows = chans * planes
    columns = ny_len * nz_len
    block = min(rows, 64)
    scale = 1.0 / math.sqrt(planes * count * columns)
    cell_norm = 1.0 / math.sqrt(cell_count)
    voxel_norm = 1.0 / math.sqrt(cell_count * planes * count * columns)
    height = 2 * chans
    wide = 4 * LANES

    basis = jnp.asarray(plane_table(ny_len, nz_len, own))
    line_np = line_tables(chans, planes, count)
    line = jnp.asarray(line_np)
    inverse = jnp.asarray(np.ascontiguousarray(np.swapaxes(line_np, 1, 2)))
    up_weight = jnp.asarray(column_weight(own, scale))
    down_weight = jnp.full((1, wide), scale, F32)
    place = lax.axis_index("space").astype(jnp.int32).reshape(1)
    eye = jnp.eye(planes, dtype=BF16)
    mix_up = jnp.einsum("oi,xw->oxiw", channel_weight, eye).reshape(rows, rows)
    mix_down = jnp.einsum("oi,xw->ixow", channel_weight, eye).reshape(rows, rows)
    bias = jnp.repeat(channel_bias, planes).reshape(rows, 1)

    modes = jax.ShapeDtypeStruct((own + 1, height, LANES), F32)
    sent = jax.ShapeDtypeStruct((own + 1, height, LANES), BF16)
    tagged = jax.ShapeDtypeStruct((own + 2, height, LANES), BF16)

    flat, mine, *others = pl.pallas_call(
        functools.partial(forward_kernel, own, rest, count),
        grid_spec=pltpu.PrefetchScalarGridSpec(
            num_scalar_prefetch=1,
            grid=(rows // block,),
            in_specs=[
                pl.BlockSpec((block, ny_len, nz_len), lambda i, s: (i, 0, 0)),
                at_place(line.shape[1:]),
                pl.BlockSpec(memory_space=pl.ANY),
            ],
            out_specs=[whole((rows, columns)), whole(modes.shape)] + [whole(sent.shape)] * (count - 1),
            scratch_shapes=[
                pltpu.VMEM((block * ny_len, nz_len), F32),
                pltpu.VMEM(basis.shape, BF16),
                pltpu.SemaphoreType.DMA,
            ],
        ),
        out_shape=[jax.ShapeDtypeStruct((rows, columns), BF16), modes] + [sent] * (count - 1),
        compiler_params=params(),
        name="forward",
    )(place, fields.reshape(rows, ny_len, nz_len), line, basis)
    cot = relayout(cotangent.reshape(rows, ny_len, nz_len), block)
    arrived = [send(array, "space", count, k + 1) for k, array in enumerate(others)]

    weight_spec = pl.BlockSpec((1,) + spectral_weight.shape[1:], lambda a: (a, 0, 0, 0, 0))
    mix_scratch = [
        pltpu.VMEM(modes.shape, F32),
        pltpu.VMEM((height, 2 * LANES), F32),
        pltpu.VMEM((height, 2 * LANES), F32),
        pltpu.VMEM((height, LANES), F32),
    ]
    mixed, field_modes = pl.pallas_call(
        functools.partial(mix_kernel, own, rest, count, scale),
        grid=(own,),
        in_specs=[whole(modes.shape)] * count + [weight_spec],
        out_specs=[whole(sent.shape), whole(sent.shape)],
        out_shape=[sent, sent],
        scratch_shapes=mix_scratch,
        compiler_params=params(),
        name="mix",
    )(mine, *arrived, spectral_weight)

    all_mixed = [mixed] + [send(mixed, "space", count, -k) for k in range(1, count)]
    all_u = gather_cells(field_modes, cell_count)
    step_columns = 4 * nz_len
    steps = columns // step_columns
    hidden, chan, mine, *others = pl.pallas_call(
        functools.partial(middle_kernel, own, rest, count, planes),
        grid_spec=pltpu.PrefetchScalarGridSpec(
            num_scalar_prefetch=1,
            grid=(steps,),
            in_specs=[whole(sent.shape)] * count
            + [
                at_place(inverse.shape[1:]),
                at_place(line.shape[1:]),
                whole((1, wide)),
                whole((rows, rows)),
                whole((rows, 1)),
                pl.BlockSpec((rows, step_columns), lambda i, s: (0, i)),
                pl.BlockSpec((rows, step_columns), lambda i, s: (0, i)),
                pl.BlockSpec((step_columns, wide), lambda i, s: (i, 0)),
            ],
            out_specs=[
                pl.BlockSpec((rows, step_columns), lambda i, s: (0, i)),
                whole((chans, LANES)),
                whole(modes.shape),
            ]
            + [whole(tagged.shape)] * (count - 1),
            scratch_shapes=[
                pltpu.VMEM((count * own * height, 2 * LANES), BF16),
                pltpu.VMEM((rows, wide), BF16),
                pltpu.VMEM((rows, wide), F32),
                pltpu.VMEM((rows, rows), F32),
            ],
        ),
        out_shape=[
            jax.ShapeDtypeStruct((rows, columns), BF16),
            jax.ShapeDtypeStruct((chans, LANES), F32),
            modes,
        ]
        + [tagged] * (count - 1),
        compiler_params=params(),
        name="middle",
    )(place, *all_mixed, inverse, line, up_weight, mix_up, bias, flat, cot, basis)
    arrived = [send(array, "space", count, k + 1) for k, array in enumerate(others)]

    returned, grad_modes = pl.pallas_call(
        functools.partial(mix_back_kernel, own, rest, count),
        grid=(own,),
        in_specs=[whole(modes.shape)] + [whole(tagged.shape)] * (count - 1) + [whole((chans, LANES)), weight_spec],
        out_specs=[whole(sent.shape), whole(tagged.shape)],
        out_shape=[sent, tagged],
        scratch_shapes=mix_scratch,
        compiler_params=params(),
        name="mix_back",
    )(mine, *arrived, chan, spectral_weight)

    all_g = gather_cells(grad_modes, cell_count)
    all_returned = [returned] + [send(returned, "space", count, -k) for k in range(1, count)]
    grad_fields = pl.pallas_call(
        functools.partial(last_kernel, own, rest, count, steps),
        grid_spec=pltpu.PrefetchScalarGridSpec(
            num_scalar_prefetch=1,
            grid=(steps + rows // block,),
            in_specs=[whole(sent.shape)] * count
            + [
                at_place(inverse.shape[1:]),
                whole((1, wide)),
                whole((rows, rows)),
                pl.BlockSpec((rows, step_columns), lambda i, s: (0, jnp.minimum(i, steps - 1))),
                pl.BlockSpec((step_columns, wide), lambda i, s: (jnp.minimum(i, steps - 1), 0)),
            ],
            out_specs=pl.BlockSpec((block, ny_len, nz_len), lambda i, s: (jnp.maximum(i - steps, 0), 0, 0)),
            scratch_shapes=[
                pltpu.VMEM((count * own * height, 2 * LANES), BF16),
                pltpu.VMEM((rows, wide), BF16),
                pltpu.VMEM((rows * ny_len, nz_len), F32),
            ],
        ),
        out_shape=jax.ShapeDtypeStruct((rows, ny_len, nz_len), BF16),
        compiler_params=params(),
        name="last",
    )(place, *all_returned, inverse, down_weight, mix_down, hidden, basis)

    one = pl.BlockSpec((1, height, LANES), lambda i: (jnp.where(i == 0, own, i - 1), 0, 0))
    tag = pl.BlockSpec((1, height, LANES), lambda i: (own + 1, 0, 0))
    grad_spectral, chan_total = pl.pallas_call(
        functools.partial(outer_kernel, own, rest, cell_count, cell_norm, voxel_norm),
        grid=(own + 1,),
        in_specs=[one] * (2 * cell_count) + [tag] * cell_count,
        out_specs=[
            pl.BlockSpec((1,) + spectral_weight.shape[1:], lambda i: (jnp.maximum(i - 1, 0), 0, 0, 0, 0)),
            whole((chans, LANES)),
        ],
        out_shape=[
            jax.ShapeDtypeStruct(spectral_weight.shape, F32),
            jax.ShapeDtypeStruct((chans, LANES), F32),
        ],
        scratch_shapes=[
            pltpu.VMEM((cell_count, 3, chans, LANES), F32),
            pltpu.VMEM((cell_count, 3, chans, LANES), F32),
            pltpu.VMEM((2, chans, chans, LANES), F32),
        ],
        compiler_params=params(),
        name="outer",
    )(*all_u, *all_g, *all_g)
    return (grad_fields.reshape(fields.shape), grad_spectral, chan_total[:, :chans], chan_total[:, chans])


def solution(mesh):
    in_specs = (
        P("dp", None, "space", None, None),
        P("dp", None, "space", None, None),
        P("space", None, None, None, None),
        P(),
        P(),
    )
    out_specs = (P("dp", None, "space", None, None), P("space", None, None, None, None), P(), P())
    body = functools.partial(shards, mesh.shape["space"], mesh.shape["dp"])
    return jax.shard_map(body, mesh=mesh, in_specs=in_specs, out_specs=out_specs, check_vma=False)
```

time: 339 us -> 167 us (0.49); the launches traced: 333 us -> 166 us
  waiting for transfers between devices: 146 us -> 20.3 us
  Pallas kernels: 0 us -> 86.9 us
  blocking collectives: 57.2 us -> 0 us
  other arithmetic: 56 us -> 2.31 us
  matrix products: 32 us -> 0 us
  starting transfers between devices: 0.29 us -> 30 us
  between operations: 14.8 us -> 1.13 us
    psum x1 -> x0, waiting for transfers between devices: 146 us -> none  [shards(): lax.psum(weight_terms(field_modes, grad_modes_out).astype(jnp.bfloat16),...]
    pallas_call x0 -> x7, Pallas kernels: none -> 86.9 us  [the longest x1 32.9 us: shards(): pl.pallas_call(functools.partial(outer_kernel, own, rest, cell_count, cel...]
    psum x1 -> x0, blocking collectives: 41.1 us -> none  [shards(): lax.psum((local_channel, local_bias), ('dp', 'space'))]
    dot_general x11 -> x0, matrix products: 32 us -> none  [the longest x1 6.63 us: shards(): jnp.einsum('boxjp,qjp->boxq', mixed_planes, basis, preferred_element_type...]
    ppermute x0 -> x34, starting transfers between devices: none -> 30 us  [the longest x30 25.2 us: swap(): return lax.ppermute(array, 'dp', [(i, i ^ bit) for i in range(count)])]
    another operation x11 -> x1, other arithmetic: 24 us -> 0.01 us
    ppermute x0 -> x34, waiting for transfers between devices: none -> 20.3 us  [the longest x30 16.9 us: swap(): return lax.ppermute(array, 'dp', [(i, i ^ bit) for i in range(count)])]
    all_gather x2 -> x0, blocking collectives: 16.1 us -> none  [spread_modes(): lax.all_gather(modes.astype(jnp.bfloat16), 'space', axis=2, tiled=True)]
  transfers between devices with their start and end apart: 3 -> 34, of which waited for: 1 -> 6; matrix products, arithmetic and copies ran while one was open for 11% -> 8% of each run, Pallas kernels for 0% -> 23%
where the time goes in v1:
time: 167 us; the launch traced here: 166 us
  Pallas kernels  86.9 us (52%)
  starting transfers between devices  30 us (18%)
  local copies, waits for them, and re-layouts  25.4 us (15%)
  waiting for transfers between devices  20.3 us (12%)
  other arithmetic  2.31 us (1%)
    pallas_call x1, Pallas kernels, shards(): pl.pallas_call(functools.partial(outer_kernel, own, rest, cell_count, cel...  32.9 us
    ppermute x30, starting transfers between devices, swap(): return lax.ppermute(array, 'dp', [(i, i ^ bit) for i in range(count)])  25.2 us
    ppermute x30, waiting for transfers between devices, swap(): return lax.ppermute(array, 'dp', [(i, i ^ bit) for i in range(count)])  16.9 us
    pallas_call x1, Pallas kernels, shards(): pl.pallas_call(functools.partial(middle_kernel, own, rest, count, planes)...  15.5 us
    unnamed x91, local copies, waits for them, and re-layouts  13 us
    pallas_call x1, Pallas kernels, shards(): pl.pallas_call(functools.partial(last_kernel, own, rest, count, steps), g...  11.2 us
    pallas_call x1, Pallas kernels, shards(): pl.pallas_call(functools.partial(mix_back_kernel, own, rest, count), grid...  8.49 us
    pallas_call x1, Pallas kernels, shards(): pl.pallas_call(functools.partial(forward_kernel, own, rest, count), grid_...  7.88 us
  transfers between devices with their start and end apart: 34, of which 6 were waited for; matrix products, arithmetic and copies ran while one was open for 8% of the time, Pallas kernels for 23%

profile of v1, /device:TPU:1, one launch (start us, length us, event | category | flops | bytes accessed | tf_op | source)
XLA Modules:
  0.0 166.0 jit_solution(4178968027970848984)
XLA Ops:
  0.6 1.6 copy-done.1
  2.2 7.9 %forward.1 = (bf16[256,5120]{1,0:T(8,128)(2,1)}, f32[9,64,128]{2,1,0:T(8,128)S(1)}, bf16[9,64,128]{2,1,0:T(8,128)(2,1)S(1)}) custom-call(s32[1]{0:T(128)} %bitcast.s_ref, bf16[256,40,128]{2,1,0:T(8,128)(2,1)} %bitcast.13, bf16[2,1024,512]{2,1,0:T(8,128)(2,1)S(1)} %copy-done.1, bf16[5120,512]{1,0:T(8,128)(2,1)} %constant.14.clone.basis_hbm.refs_9_.refs_6_), custom_call_target="tpu_custom_call" | custom-call | tf_op jit(solution)/shard_map/forward/pallas_call | solution.py:450
  10.1 2.1 %collective-permute-start = (bf16[9,64,128]{2,1,0:T(8,128)(2,1)S(1)}, bf16[9,64,128]{2,1,0:T(8,128)(2,1)S(1)}, u32[]{:S(2)}, u32[]{:S(2)}) collective-permute-start(bf16[9,64,128]{2,1,0:T(8,128)(2,1)S(1)} %get-tuple-element.18), channel_id=1, source_target_pairs={{0,1},{1,0},{2,3},{3,2},{4,5},{5,4},{6,7},{7,6},{8,9},{9,8},{10,11... | collective-permute-start | bytes 442376 | tf_op jit(solution)/shard_map/ppermute | solution.py:403
  12.3 3.5 %collective-permute-done.refs_1_ = bf16[9,64,128]{2,1,0:T(8,128)(2,1)S(1)} collective-permute-done((bf16[9,64,128]{2,1,0:T(8,128)(2,1)S(1)}, bf16[9,64,128]{2,1,0:T(8,128)(2,1)S(1)}, u32[]{:S(2)}, u32[]{:S(2)}) %collective-permute-start) | collective-permute-done | bytes 147488 | tf_op jit(solution)/shard_map/ppermute | solution.py:403
  15.8 7.5 %mix.1 = (bf16[9,64,128]{2,1,0:T(8,128)(2,1)S(1)}, bf16[9,64,128]{2,1,0:T(8,128)(2,1)S(1)}) custom-call(f32[9,64,128]{2,1,0:T(8,128)S(1)} %get-tuple-element.17.refs_0_, bf16[9,64,128]{2,1,0:T(8,128)(2,1)S(1)} %collective-permute-done.refs_1_, bf16[8,2,32,32,144]{4,3,2,1,0:T(8,128)(2,1)} %refs_3_.2), custom_call_target="tpu_custom_call" | custom-call | tf_op jit(solution)/shard_map/mix/pallas_call | solution.py:481
  23.4 1.3 collective-permute-start.11
  24.7 3.6 %collective-permute-start.9 = (bf16[9,64,128]{2,1,0:T(8,128)(2,1)S(1)}, bf16[9,64,128]{2,1,0:T(8,128)(2,1)S(1)}, u32[]{:S(2)}, u32[]{:S(2)}) collective-permute-start(bf16[9,64,128]{2,1,0:T(8,128)(2,1)S(1)} %get-tuple-element.26.refs_0_), channel_id=1, source_target_pairs={{0,24},{2,26},{4,28},{6,30},{8,16},{10,18},{12,20},{14,22},{16,8},... | collective-permute-start | bytes 442376 | tf_op jit(solution)/shard_map/ppermute | solution.py:407
  28.3 1.2 collective-permute-start.1
  29.5 2.3 %multiply_bitcast_fusion = (bf16[32,8,32,8]{3,2,1,0:T(8,128)(2,1)}, bf16[32,8,32,8]{3,0,1,2:T(8,128)(2,1)}) fusion(bf16[32,32]{0,1:T(8,128)(2,1)S(1)} %copy.15, bf16[8,8]{1,0:T(8,128)(2,1)S(1)} %fusion), kind=kLoop, calls=%fused_computation | loop fusion | flops 65536 | bytes 264320 | tf_op jit(solution)/shard_map/oi,xw->ixow/transpose | solution.py:443
  32.0 3.4 %relayout.1.refs_8_ = bf16[256,5120]{1,0:T(8,128)(2,1)S(1)} custom-call(bf16[256,40,128]{2,1,0:T(8,128)(2,1)} %bitcast.14), custom_call_target="tpu_custom_call" | custom-call | tf_op jit(solution)/shard_map/relayout/pallas_call | solution.py:390
  35.4 1.5 copy-done
  36.9 2.7 %copy.16 = bf16[32,8,32,8]{3,2,1,0:T(8,128)(2,1)} copy(bf16[32,8,32,8]{3,0,1,2:T(8,128)(2,1)S(1)} %copy-done.40) | data formatting | bytes 262144 | tf_op jit(solution)/shard_map/oi,xw->oxiw/transpose | solution.py:442
  39.6 4.1 %reshape.28.refs_5_ = bf16[256,256]{1,0:T(8,128)(2,1)S(1)} reshape(bf16[32,8,32,8]{3,2,1,0:T(8,128)(2,1)} %copy.16) | data formatting | bytes 262144 | tf_op jit(solution)/shard_map/reshape | solution.py:442
  43.6 15.5 %middle.1 = (bf16[256,5120]{1,0:T(8,128)(2,1)}, f32[32,128]{1,0:T(8,128)S(1)}, f32[9,64,128]{2,1,0:T(8,128)S(1)}, bf16[10,64,128]{2,1,0:T(8,128)(2,1)S(1)}) custom-call(s32[1]{0:T(128)} %bitcast.s_ref, bf16[9,64,128]{2,1,0:T(8,128)(2,1)S(1)} %get-tuple-element.19.refs_0_, bf16[9,64,128]{2,1,0:T(8,128)(2,1)S(1)} %collective-permute-done.1.refs_1_, ...), custom_call_target="tpu_custom_call" | custom-call | tf_op jit(solution)/shard_map/middle/pallas_call | solution.py:496
  59.7 1.3 collective-permute-start.4
  61.0 1.7 %collective-permute-start.17 = (bf16[9,64,128]{2,1,0:T(8,128)(2,1)S(1)}, bf16[9,64,128]{2,1,0:T(8,128)(2,1)S(1)}, u32[]{:S(2)}, u32[]{:S(2)}) collective-permute-start(bf16[9,64,128]{2,1,0:T(8,128)(2,1)S(1)} %collective-permute-done.9.refs_6_), channel_id=1, source_target_pairs={{0,2},{2,0},{4,6},{6,4},{8,10},{10,8},{12,14},{14,12},{16,18},{18,... | collective-permute-start | bytes 442376 | tf_op jit(solution)/shard_map/ppermute | solution.py:407
  62.7 5.6 %collective-permute-done.7.refs_4_ = bf16[9,64,128]{2,1,0:T(8,128)(2,1)S(1)} collective-permute-done((bf16[9,64,128]{2,1,0:T(8,128)(2,1)S(1)}, bf16[9,64,128]{2,1,0:T(8,128)(2,1)S(1)}, u32[]{:S(2)}, u32[]{:S(2)}) %collective-permute-start.7) | collective-permute-done | bytes 147488 | tf_op jit(solution)/shard_map/ppermute | solution.py:407
  68.2 1.2 collective-permute-start.10
  71.2 1.2 collective-permute-start.6
  73.1 8.5 %mix_back.1 = (bf16[9,64,128]{2,1,0:T(8,128)(2,1)S(1)}, bf16[10,64,128]{2,1,0:T(8,128)(2,1)S(1)}) custom-call(f32[9,64,128]{2,1,0:T(8,128)S(1)} %get-tuple-element.21.refs_0_, bf16[10,64,128]{2,1,0:T(8,128)(2,1)S(1)} %collective-permute-done.2.refs_1_, f32[32,128]{1,0:T(8,128)S(1)} %get-tuple-element.23.refs_2_, bf16[8,2,32,32,144]{4,3,2,1,0:T(8,128)(2,1)} %refs_3_.2), custom_call_target="tpu_custom_call" | custom-call | tf_op jit(solution)/shard_map/mix_back/pallas_call | solution.py:536
  86.1 1.2 collective-permute-start.3
  92.2 2.5 %collective-permute-start.20 = (bf16[10,64,128]{2,1,0:T(8,128)(2,1)S(1)}, bf16[10,64,128]{2,1,0:T(8,128)(2,1)S(1)}, u32[]{:S(2)}, u32[]{:S(2)}) collective-permute-start(bf16[10,64,128]{2,1,0:T(8,128)(2,1)S(1)} %get-tuple-element.27.refs_16_.refs_32_), channel_id=1, source_target_pairs={{0,8},{2,10},{4,12},{6,14},{8,0},{10,2},{12,4},{14,6},{16,24},{18,... | collective-permute-start | bytes 491528 | tf_op jit(solution)/shard_map/ppermute | solution.py:407
  95.9 1.9 %collective-permute-start.32 = (bf16[10,64,128]{2,1,0:T(8,128)(2,1)S(1)}, bf16[10,64,128]{2,1,0:T(8,128)(2,1)S(1)}, u32[]{:S(2)}, u32[]{:S(2)}) collective-permute-start(bf16[10,64,128]{2,1,0:T(8,128)(2,1)S(1)} %collective-permute-done.24.refs_22_.refs_38_), channel_id=1, source_target_pairs={{0,2},{2,0},{4,6},{6,4},{8,10},{10,8},{12,14},{14,12},{16,18},{18,... | collective-permute-start | bytes 491528 | tf_op jit(solution)/shard_map/ppermute | solution.py:407
  98.1 5.5 %collective-permute-done.22.refs_20_.refs_36_ = bf16[10,64,128]{2,1,0:T(8,128)(2,1)S(1)} collective-permute-done((bf16[10,64,128]{2,1,0:T(8,128)(2,1)S(1)}, bf16[10,64,128]{2,1,0:T(8,128)(2,1)S(1)}, u32[]{:S(2)}, u32[]{:S(2)}) %collective-permute-start.22) | collective-permute-done | bytes 163872 | tf_op jit(solution)/shard_map/ppermute | solution.py:407
  104.1 1.2 collective-permute-start.23
  106.7 3.1 %collective-permute-done.23.refs_21_.refs_37_ = bf16[10,64,128]{2,1,0:T(8,128)(2,1)S(1)} collective-permute-done((bf16[10,64,128]{2,1,0:T(8,128)(2,1)S(1)}, bf16[10,64,128]{2,1,0:T(8,128)(2,1)S(1)}, u32[]{:S(2)}, u32[]{:S(2)}) %collective-permute-start.23) | collective-permute-done | bytes 163872 | tf_op jit(solution)/shard_map/ppermute | solution.py:407
  109.8 1.3 collective-permute-start.31
  111.1 2.3 %collective-permute-done.21.refs_19_.refs_35_ = bf16[10,64,128]{2,1,0:T(8,128)(2,1)} collective-permute-done((bf16[10,64,128]{2,1,0:T(8,128)(2,1)S(1)}, bf16[10,64,128]{2,1,0:T(8,128)(2,1)}, u32[]{:S(2)}, u32[]{:S(2)}) %collective-permute-start.21) | collective-permute-done | bytes 163872 | tf_op jit(solution)/shard_map/ppermute | solution.py:407
  114.3 4.1 %reshape.30.refs_4_ = bf16[256,256]{1,0:T(8,128)(2,1)S(1)} reshape(bf16[32,8,32,8]{3,2,1,0:T(8,128)(2,1)} %get-tuple-element.30) | data formatting | bytes 262144 | tf_op jit(solution)/shard_map/reshape | solution.py:443
  120.3 11.2 %last.1 = bf16[256,40,128]{2,1,0:T(8,128)(2,1)} custom-call(s32[1]{0:T(128)} %bitcast.s_ref, bf16[9,64,128]{2,1,0:T(8,128)(2,1)S(1)} %copy-done.4, bf16[9,64,128]{2,1,0:T(8,128)(2,1)S(1)} %copy-done.6, bf16[2,512,1024]{2,1,0:T(8,128)(2,1)S(1)} %copy-done.2, f32[1,512]{1,0:T(1,128)S(1)} %broadcast_in_dim.7.refs_3_, bf16[256,256]{1,0:T(8,128)(2,1)S(1)} %reshape.30.refs_4_, ...), custom_call_target="tpu_custom_call" | custom-call | tf_op jit(solution)/shard_map/last/pallas_call | solution.py:549
  131.7 32.9 %outer.1 = (f32[8,2,32,32,144]{4,3,2,1,0:T(8,128)}, f32[32,128]{1,0:T(8,128)}) custom-call(bf16[9,64,128]{2,1,0:T(8,128)(2,1)S(1)} %copy-done.8, bf16[9,64,128]{2,1,0:T(8,128)(2,1)S(1)} %copy-done.18, bf16[9,64,128]{2,1,0:T(8,128)(2,1)S(1)} %copy-done.16, bf16[9,64,128]{2,1,0:T(8,128)(2,1)S(1)} %copy-done.28, bf16[9,64,128]{2,1,0:T(8,128)(2,1)S(1)} %copy-done.14, ...), custom_call_target="tpu_custom_call" | custom-call | tf_op jit(solution)/shard_map/outer/pallas_call | solution.py:576
  164.6 1.4 slice_reduce_fusion
  (143 shorter events, 18.5 us)
Async XLA Ops:
  23.4 36.3 %collective-permute-start.11 = (bf16[9,64,128]{2,1,0:T(8,128)(2,1)S(1)}, bf16[9,64,128]{2,1,0:T(8,128)(2,1)S(1)}, u32[]{:S(2)}, u32[]{:S(2)}) collective-permute-start(bf16[9,64,128]{2,1,0:T(8,128)(2,1)S(1)} %get-tuple-element.26.refs_0_), channel_id=1, source_target_pairs={{0,2},{2,0},{4,6},{6,4},{8,10},{10,8},{12,14},{14,12},{16,18},{18,... | collective-permute-start | bytes 442376 | tf_op jit(solution)/shard_map/ppermute | solution.py:407
  24.7 36.3 %collective-permute-start.9 = (bf16[9,64,128]{2,1,0:T(8,128)(2,1)S(1)}, bf16[9,64,128]{2,1,0:T(8,128)(2,1)S(1)}, u32[]{:S(2)}, u32[]{:S(2)}) collective-permute-start(bf16[9,64,128]{2,1,0:T(8,128)(2,1)S(1)} %get-tuple-element.26.refs_0_), channel_id=1, source_target_pairs={{0,24},{2,26},{4,28},{6,30},{8,16},{10,18},{12,20},{14,22},{16,8},... | collective-permute-start | bytes 442376 | tf_op jit(solution)/shard_map/ppermute | solution.py:407
  28.3 15.4 %collective-permute-start.1 = (bf16[9,64,128]{2,1,0:T(8,128)(2,1)S(1)}, bf16[9,64,128]{2,1,0:T(8,128)(2,1)S(1)}, u32[]{:S(2)}, u32[]{:S(2)}) collective-permute-start(bf16[9,64,128]{2,1,0:T(8,128)(2,1)S(1)} %get-tuple-element.19.refs_0_), channel_id=1, source_target_pairs={{0,1},{1,0},{2,3},{3,2},{4,5},{5,4},{6,7},{7,6},{8,9},{9,8},{10,11... | collective-permute-start | bytes 442376 | tf_op jit(solution)/shard_map/ppermute | solution.py:403
  59.1 13.4 %collective-permute-start.2 = (bf16[10,64,128]{2,1,0:T(8,128)(2,1)S(1)}, bf16[10,64,128]{2,1,0:T(8,128)(2,1)S(1)}, u32[]{:S(2)}, u32[]{:S(2)}) collective-permute-start(bf16[10,64,128]{2,1,0:T(8,128)(2,1)S(1)} %get-tuple-element.22), channel_id=1, source_target_pairs={{0,1},{1,0},{2,3},{3,2},{4,5},{5,4},{6,7},{7,6},{8,9},{9,8},{10,11... | collective-permute-start | bytes 491528 | tf_op jit(solution)/shard_map/ppermute | solution.py:403
  59.4 8.9 %collective-permute-start.7 = (bf16[9,64,128]{2,1,0:T(8,128)(2,1)S(1)}, bf16[9,64,128]{2,1,0:T(8,128)(2,1)S(1)}, u32[]{:S(2)}, u32[]{:S(2)}) collective-permute-start(bf16[9,64,128]{2,1,0:T(8,128)(2,1)S(1)} %get-tuple-element.26.refs_0_), channel_id=1, source_target_pairs={{0,16},{2,18},{4,20},{6,22},{8,24},{10,26},{12,28},{14,30},{16,0},... | collective-permute-start | bytes 442376 | tf_op jit(solution)/shard_map/ppermute | solution.py:407
  59.4 10.1 %collective-permute-start.5 = (bf16[9,64,128]{2,1,0:T(8,128)(2,1)S(1)}, bf16[9,64,128]{2,1,0:T(8,128)(2,1)S(1)}, u32[]{:S(2)}, u32[]{:S(2)}) collective-permute-start(bf16[9,64,128]{2,1,0:T(8,128)(2,1)S(1)} %get-tuple-element.26.refs_0_), channel_id=1, source_target_pairs={{0,8},{2,10},{4,12},{6,14},{8,0},{10,2},{12,4},{14,6},{16,24},{18,... | collective-permute-start | bytes 442376 | tf_op jit(solution)/shard_map/ppermute | solution.py:407
  59.7 10.7 %collective-permute-start.4 = (bf16[9,64,128]{2,1,0:T(8,128)(2,1)S(1)}, bf16[9,64,128]{2,1,0:T(8,128)(2,1)S(1)}, u32[]{:S(2)}, u32[]{:S(2)}) collective-permute-start(bf16[9,64,128]{2,1,0:T(8,128)(2,1)S(1)} %get-tuple-element.26.refs_0_), channel_id=1, source_target_pairs={{0,4},{2,6},{4,0},{6,2},{8,12},{10,14},{12,8},{14,10},{16,20},{18,... | collective-permute-start | bytes 442376 | tf_op jit(solution)/shard_map/ppermute | solution.py:407
  61.0 9.6 %collective-permute-start.17 = (bf16[9,64,128]{2,1,0:T(8,128)(2,1)S(1)}, bf16[9,64,128]{2,1,0:T(8,128)(2,1)S(1)}, u32[]{:S(2)}, u32[]{:S(2)}) collective-permute-start(bf16[9,64,128]{2,1,0:T(8,128)(2,1)S(1)} %collective-permute-done.9.refs_6_), channel_id=1, source_target_pairs={{0,2},{2,0},{4,6},{6,4},{8,10},{10,8},{12,14},{14,12},{16,18},{18,... | collective-permute-start | bytes 442376 | tf_op jit(solution)/shard_map/ppermute | solution.py:407
  68.2 13.4 %collective-permute-start.10 = (bf16[9,64,128]{2,1,0:T(8,128)(2,1)S(1)}, bf16[9,64,128]{2,1,0:T(8,128)(2,1)S(1)}, u32[]{:S(2)}, u32[]{:S(2)}) collective-permute-start(bf16[9,64,128]{2,1,0:T(8,128)(2,1)S(1)} %collective-permute-done.9.refs_6_), channel_id=1, source_target_pairs={{0,4},{2,6},{4,0},{6,2},{8,12},{10,14},{12,8},{14,10},{16,20},{18,... | collective-permute-start | bytes 442376 | tf_op jit(solution)/shard_map/ppermute | solution.py:407
  69.5 12.2 %collective-permute-start.15 = (bf16[9,64,128]{2,1,0:T(8,128)(2,1)S(1)}, bf16[9,64,128]{2,1,0:T(8,128)(2,1)S(1)}, u32[]{:S(2)}, u32[]{:S(2)}) collective-permute-start(bf16[9,64,128]{2,1,0:T(8,128)(2,1)S(1)} %collective-permute-done.7.refs_4_), channel_id=1, source_target_pairs={{0,2},{2,0},{4,6},{6,4},{8,10},{10,8},{12,14},{14,12},{16,18},{18,... | collective-permute-start | bytes 442376 | tf_op jit(solution)/shard_map/ppermute | solution.py:407
  70.3 13.2 %collective-permute-start.8 = (bf16[9,64,128]{2,1,0:T(8,128)(2,1)S(1)}, bf16[9,64,128]{2,1,0:T(8,128)(2,1)S(1)}, u32[]{:S(2)}, u32[]{:S(2)}) collective-permute-start(bf16[9,64,128]{2,1,0:T(8,128)(2,1)S(1)} %collective-permute-done.7.refs_4_), channel_id=1, source_target_pairs={{0,4},{2,6},{4,0},{6,2},{8,12},{10,14},{12,8},{14,10},{16,20},{18,... | collective-permute-start | bytes 442376 | tf_op jit(solution)/shard_map/ppermute | solution.py:407
  71.2 13.0 %collective-permute-start.6 = (bf16[9,64,128]{2,1,0:T(8,128)(2,1)S(1)}, bf16[9,64,128]{2,1,0:T(8,128)(2,1)S(1)}, u32[]{:S(2)}, u32[]{:S(2)}) collective-permute-start(bf16[9,64,128]{2,1,0:T(8,128)(2,1)S(1)} %collective-permute-done.5.refs_2_), channel_id=1, source_target_pairs={{0,4},{2,6},{4,0},{6,2},{8,12},{10,14},{12,8},{14,10},{16,20},{18,... | collective-permute-start | bytes 442376 | tf_op jit(solution)/shard_map/ppermute | solution.py:407
  72.5 12.9 %collective-permute-start.13 = (bf16[9,64,128]{2,1,0:T(8,128)(2,1)S(1)}, bf16[9,64,128]{2,1,0:T(8,128)(2,1)S(1)}, u32[]{:S(2)}, u32[]{:S(2)}) collective-permute-start(bf16[9,64,128]{2,1,0:T(8,128)(2,1)S(1)} %collective-permute-done.5.refs_2_), channel_id=1, source_target_pairs={{0,2},{2,0},{4,6},{6,4},{8,10},{10,8},{12,14},{14,12},{16,18},{18,... | collective-permute-start | bytes 442376 | tf_op jit(solution)/shard_map/ppermute | solution.py:407
  81.6 6.3 %collective-permute-start.12 = (bf16[9,64,128]{2,1,0:T(8,128)(2,1)S(1)}, bf16[9,64,128]{2,1,0:T(8,128)(2,1)S(1)}, u32[]{:S(2)}, u32[]{:S(2)}) collective-permute-start(bf16[9,64,128]{2,1,0:T(8,128)(2,1)S(1)} %collective-permute-done.4.refs_1_), channel_id=1, source_target_pairs={{0,2},{2,0},{4,6},{6,4},{8,10},{10,8},{12,14},{14,12},{16,18},{18,... | collective-permute-start | bytes 442376 | tf_op jit(solution)/shard_map/ppermute | solution.py:407
  82.4 7.2 %collective-permute-start.18 = (bf16[9,64,128]{2,1,0:T(8,128)(2,1)S(1)}, bf16[9,64,128]{2,1,0:T(8,128)(2,1)S(1)}, u32[]{:S(2)}, u32[]{:S(2)}) collective-permute-start(bf16[9,64,128]{2,1,0:T(8,128)(2,1)S(1)} %collective-permute-done.10.refs_7_), channel_id=1, source_target_pairs={{0,2},{2,0},{4,6},{6,4},{8,10},{10,8},{12,14},{14,12},{16,18},{18,... | collective-permute-start | bytes 442376 | tf_op jit(solution)/shard_map/ppermute | solution.py:407
  83.5 7.3 %collective-permute-start.16 = (bf16[9,64,128]{2,1,0:T(8,128)(2,1)S(1)}, bf16[9,64,128]{2,1,0:T(8,128)(2,1)S(1)}, u32[]{:S(2)}, u32[]{:S(2)}) collective-permute-start(bf16[9,64,128]{2,1,0:T(8,128)(2,1)S(1)} %collective-permute-done.8.refs_5_), channel_id=1, source_target_pairs={{0,2},{2,0},{4,6},{6,4},{8,10},{10,8},{12,14},{14,12},{16,18},{18,... | collective-permute-start | bytes 442376 | tf_op jit(solution)/shard_map/ppermute | solution.py:407
  84.2 7.3 %collective-permute-start.14 = (bf16[9,64,128]{2,1,0:T(8,128)(2,1)S(1)}, bf16[9,64,128]{2,1,0:T(8,128)(2,1)S(1)}, u32[]{:S(2)}, u32[]{:S(2)}) collective-permute-start(bf16[9,64,128]{2,1,0:T(8,128)(2,1)S(1)} %collective-permute-done.6.refs_3_), channel_id=1, source_target_pairs={{0,2},{2,0},{4,6},{6,4},{8,10},{10,8},{12,14},{14,12},{16,18},{18,... | collective-permute-start | bytes 442376 | tf_op jit(solution)/shard_map/ppermute | solution.py:407
  86.1 8.7 %collective-permute-start.3 = (bf16[9,64,128]{2,1,0:T(8,128)(2,1)S(1)}, bf16[9,64,128]{2,1,0:T(8,128)(2,1)S(1)}, u32[]{:S(2)}, u32[]{:S(2)}) collective-permute-start(bf16[9,64,128]{2,1,0:T(8,128)(2,1)S(1)} %get-tuple-element.24.refs_0_), channel_id=1, source_target_pairs={{0,1},{1,0},{2,3},{3,2},{4,5},{5,4},{6,7},{7,6},{8,9},{9,8},{10,11... | collective-permute-start | bytes 442376 | tf_op jit(solution)/shard_map/ppermute | solution.py:403
  88.6 7.3 %collective-permute-start.24 = (bf16[10,64,128]{2,1,0:T(8,128)(2,1)S(1)}, bf16[10,64,128]{2,1,0:T(8,128)(2,1)S(1)}, u32[]{:S(2)}, u32[]{:S(2)}) collective-permute-start(bf16[10,64,128]{2,1,0:T(8,128)(2,1)S(1)} %get-tuple-element.27.refs_16_.refs_32_), channel_id=1, source_target_pairs={{0,24},{2,26},{4,28},{6,30},{8,16},{10,18},{12,20},{14,22},{16,8},... | collective-permute-start | bytes 491528 | tf_op jit(solution)/shard_map/ppermute | solution.py:407
  90.3 7.6 %collective-permute-start.26 = (bf16[10,64,128]{2,1,0:T(8,128)(2,1)S(1)}, bf16[10,64,128]{2,1,0:T(8,128)(2,1)S(1)}, u32[]{:S(2)}, u32[]{:S(2)}) collective-permute-start(bf16[10,64,128]{2,1,0:T(8,128)(2,1)S(1)} %get-tuple-element.27.refs_16_.refs_32_), channel_id=1, source_target_pairs={{0,2},{2,0},{4,6},{6,4},{8,10},{10,8},{12,14},{14,12},{16,18},{18,... | collective-permute-start | bytes 491528 | tf_op jit(solution)/shard_map/ppermute | solution.py:407
  91.5 12.1 %collective-permute-start.22 = (bf16[10,64,128]{2,1,0:T(8,128)(2,1)S(1)}, bf16[10,64,128]{2,1,0:T(8,128)(2,1)S(1)}, u32[]{:S(2)}, u32[]{:S(2)}) collective-permute-start(bf16[10,64,128]{2,1,0:T(8,128)(2,1)S(1)} %get-tuple-element.27.refs_16_.refs_32_), channel_id=1, source_target_pairs={{0,16},{2,18},{4,20},{6,22},{8,24},{10,26},{12,28},{14,30},{16,0},... | collective-permute-start | bytes 491528 | tf_op jit(solution)/shard_map/ppermute | solution.py:407
  92.2 11.9 %collective-permute-start.20 = (bf16[10,64,128]{2,1,0:T(8,128)(2,1)S(1)}, bf16[10,64,128]{2,1,0:T(8,128)(2,1)S(1)}, u32[]{:S(2)}, u32[]{:S(2)}) collective-permute-start(bf16[10,64,128]{2,1,0:T(8,128)(2,1)S(1)} %get-tuple-element.27.refs_16_.refs_32_), channel_id=1, source_target_pairs={{0,8},{2,10},{4,12},{6,14},{8,0},{10,2},{12,4},{14,6},{16,24},{18,... | collective-permute-start | bytes 491528 | tf_op jit(solution)/shard_map/ppermute | solution.py:407
  95.4 9.8 %collective-permute-start.19 = (bf16[10,64,128]{2,1,0:T(8,128)(2,1)S(1)}, bf16[10,64,128]{2,1,0:T(8,128)(2,1)S(1)}, u32[]{:S(2)}, u32[]{:S(2)}) collective-permute-start(bf16[10,64,128]{2,1,0:T(8,128)(2,1)S(1)} %get-tuple-element.27.refs_16_.refs_32_), channel_id=1, source_target_pairs={{0,4},{2,6},{4,0},{6,2},{8,12},{10,14},{12,8},{14,10},{16,20},{18,... | collective-permute-start | bytes 491528 | tf_op jit(solution)/shard_map/ppermute | solution.py:407
  95.9 9.6 %collective-permute-start.32 = (bf16[10,64,128]{2,1,0:T(8,128)(2,1)S(1)}, bf16[10,64,128]{2,1,0:T(8,128)(2,1)S(1)}, u32[]{:S(2)}, u32[]{:S(2)}) collective-permute-start(bf16[10,64,128]{2,1,0:T(8,128)(2,1)S(1)} %collective-permute-done.24.refs_22_.refs_38_), channel_id=1, source_target_pairs={{0,2},{2,0},{4,6},{6,4},{8,10},{10,8},{12,14},{14,12},{16,18},{18,... | collective-permute-start | bytes 491528 | tf_op jit(solution)/shard_map/ppermute | solution.py:407
  97.9 8.3 %collective-permute-start.25 = (bf16[10,64,128]{2,1,0:T(8,128)(2,1)S(1)}, bf16[10,64,128]{2,1,0:T(8,128)(2,1)S(1)}, u32[]{:S(2)}, u32[]{:S(2)}) collective-permute-start(bf16[10,64,128]{2,1,0:T(8,128)(2,1)S(1)} %collective-permute-done.24.refs_22_.refs_38_), channel_id=1, source_target_pairs={{0,4},{2,6},{4,0},{6,2},{8,12},{10,14},{12,8},{14,10},{16,20},{18,... | collective-permute-start | bytes 491528 | tf_op jit(solution)/shard_map/ppermute | solution.py:407
  104.1 5.8 %collective-permute-start.23 = (bf16[10,64,128]{2,1,0:T(8,128)(2,1)S(1)}, bf16[10,64,128]{2,1,0:T(8,128)(2,1)S(1)}, u32[]{:S(2)}, u32[]{:S(2)}) collective-permute-start(bf16[10,64,128]{2,1,0:T(8,128)(2,1)S(1)} %collective-permute-done.22.refs_20_.refs_36_), channel_id=1, source_target_pairs={{0,4},{2,6},{4,0},{6,2},{8,12},{10,14},{12,8},{14,10},{16,20},{18,... | collective-permute-start | bytes 491528 | tf_op jit(solution)/shard_map/ppermute | solution.py:407
  105.3 8.2 %collective-permute-start.21 = (bf16[10,64,128]{2,1,0:T(8,128)(2,1)S(1)}, bf16[10,64,128]{2,1,0:T(8,128)(2,1)}, u32[]{:S(2)}, u32[]{:S(2)}) collective-permute-start(bf16[10,64,128]{2,1,0:T(8,128)(2,1)S(1)} %collective-permute-done.20.refs_18_.refs_34_), channel_id=1, source_target_pairs={{0,4},{2,6},{4,0},{6,2},{8,12},{10,14},{12,8},{14,10},{16,20},{18,... | collective-permute-start | bytes 491528 | tf_op jit(solution)/shard_map/ppermute | solution.py:407
  105.5 26.0 %collective-permute-start.28 = (bf16[10,64,128]{2,1,0:T(8,128)(2,1)S(1)}, bf16[10,64,128]{2,1,0:T(8,128)(2,1)}, u32[]{:S(2)}, u32[]{:S(2)}) collective-permute-start(bf16[10,64,128]{2,1,0:T(8,128)(2,1)S(1)} %collective-permute-done.20.refs_18_.refs_34_), channel_id=1, source_target_pairs={{0,2},{2,0},{4,6},{6,4},{8,10},{10,8},{12,14},{14,12},{16,18},{18,... | collective-permute-start | bytes 491528 | tf_op jit(solution)/shard_map/ppermute | solution.py:407
  106.2 25.3 %collective-permute-start.27 = (bf16[10,64,128]{2,1,0:T(8,128)(2,1)S(1)}, bf16[10,64,128]{2,1,0:T(8,128)(2,1)}, u32[]{:S(2)}, u32[]{:S(2)}) collective-permute-start(bf16[10,64,128]{2,1,0:T(8,128)(2,1)S(1)} %collective-permute-done.19.refs_17_.refs_33_), channel_id=1, source_target_pairs={{0,2},{2,0},{4,6},{6,4},{8,10},{10,8},{12,14},{14,12},{16,18},{18,... | collective-permute-start | bytes 491528 | tf_op jit(solution)/shard_map/ppermute | solution.py:407
  106.2 25.3 %collective-permute-start.33 = (bf16[10,64,128]{2,1,0:T(8,128)(2,1)S(1)}, bf16[10,64,128]{2,1,0:T(8,128)(2,1)}, u32[]{:S(2)}, u32[]{:S(2)}) collective-permute-start(bf16[10,64,128]{2,1,0:T(8,128)(2,1)S(1)} %collective-permute-done.25.refs_23_.refs_39_), channel_id=1, source_target_pairs={{0,2},{2,0},{4,6},{6,4},{8,10},{10,8},{12,14},{14,12},{16,18},{18,... | collective-permute-start | bytes 491528 | tf_op jit(solution)/shard_map/ppermute | solution.py:407
  109.8 21.7 %collective-permute-start.31 = (bf16[10,64,128]{2,1,0:T(8,128)(2,1)S(1)}, bf16[10,64,128]{2,1,0:T(8,128)(2,1)}, u32[]{:S(2)}, u32[]{:S(2)}) collective-permute-start(bf16[10,64,128]{2,1,0:T(8,128)(2,1)S(1)} %collective-permute-done.23.refs_21_.refs_37_), channel_id=1, source_target_pairs={{0,2},{2,0},{4,6},{6,4},{8,10},{10,8},{12,14},{14,12},{16,18},{18,... | collective-permute-start | bytes 491528 | tf_op jit(solution)/shard_map/ppermute | solution.py:407
  113.4 18.1 %collective-permute-start.29 = (bf16[10,64,128]{2,1,0:T(8,128)(2,1)}, bf16[10,64,128]{2,1,0:T(8,128)(2,1)}, u32[]{:S(2)}, u32[]{:S(2)}) collective-permute-start(bf16[10,64,128]{2,1,0:T(8,128)(2,1)} %collective-permute-done.21.refs_19_.refs_35_), channel_id=1, source_target_pairs={{0,2},{2,0},{4,6},{6,4},{8,10},{10,8},{12,14},{14,12},{16,18},{18,... | collective-permute-start | bytes 491528 | tf_op jit(solution)/shard_map/ppermute | solution.py:407
  (47 other events, 372.4 us)

commit v2 on v0

v2 whole, which is shorter than its diff:
```python
import functools
import math

import jax
import jax.numpy as jnp
import ml_dtypes
import numpy as np
from jax import lax
from jax.experimental import pallas as pl
from jax.experimental.pallas import tpu as pltpu
from jax.sharding import PartitionSpec as P

MX = 16
MY = 16
MZ = 9
LANES = 128
BF16 = jnp.bfloat16
F32 = jnp.float32
TWO_PI = 2.0 * math.pi


def signed(index, modes):
    return np.where(index < modes // 2, index, index - modes)


def plane_columns(own):
    pairs = MY * MZ
    rest = pairs - LANES
    return np.concatenate([np.arange(LANES), LANES + np.tile(np.arange(rest), own)])


def plane_table(ny_len, nz_len, own):
    ky = signed(np.arange(MY), MY)
    kz = np.arange(MZ)
    y_pos = np.arange(ny_len)
    z_pos = np.arange(nz_len)
    phases = (
        y_pos[:, None, None, None] * ky[None, None, :, None] * nz_len
        + z_pos[None, :, None, None] * kz[None, None, None, :] * ny_len
    ) % (ny_len * nz_len)
    angles = phases.astype(np.float32) * np.float32(TWO_PI / (ny_len * nz_len))
    angles = angles.reshape(ny_len * nz_len, MY * MZ)
    columns = plane_columns(own)
    table = np.zeros((ny_len * nz_len, 2, 2 * LANES), np.float32)
    table[:, 0, : len(columns)] = np.cos(angles)[:, columns]
    table[:, 1, : len(columns)] = -np.sin(angles)[:, columns]
    return table.reshape(ny_len * nz_len, 4 * LANES).astype(ml_dtypes.bfloat16)


def column_weight(own, scale):
    columns = plane_columns(own)
    weight = np.zeros((2, 2 * LANES), np.float32)
    weight[:, : len(columns)] = np.where(columns % MZ == 0, 1.0, 2.0)
    return (weight * scale).reshape(1, 4 * LANES).astype(np.float32)


def line_tables(chans, planes, count):
    own = MX // count
    length = planes * count
    tables = []
    for s in range(count):
        place = (s + np.arange(count)) % count
        index = (place[:, None] * own + np.arange(own)[None, :]).reshape(-1)
        phases = signed(index, MX)[:, None] * (s * planes + np.arange(planes))[None, :] % length
        angles = phases.astype(np.float32) * np.float32(TWO_PI / length)
        cosine, sines = np.cos(angles), np.sin(angles)
        line = np.stack([np.stack([cosine, sines], -1), np.stack([-sines, cosine], -1)], 1)
        whole = np.einsum("arxj,cd->arcjdx", line, np.eye(chans, dtype=np.float32))
        tables.append(whole.reshape(MX * 2 * chans, 2 * chans * planes))
    return np.stack(tables).astype(ml_dtypes.bfloat16)


def dot(left, right):
    return jnp.dot(left, right, preferred_element_type=F32)


def dot_nt(left, right):
    return lax.dot_general(left, right, (((1,), (1,)), ((), ())), preferred_element_type=F32)


def tail_mask(a, rows, rest):
    lane = lax.broadcasted_iota(jnp.int32, (rows, LANES), 1)
    return (lane >= a * rest) & (lane < (a + 1) * rest)


def spread_rows(block_ref, out_ref, start, count):
    _, ny_len, nz_len = block_ref.shape
    turned = jnp.swapaxes(block_ref[start : start + count], 0, 1)
    for y in range(ny_len):
        out_ref[start : start + count, y * nz_len : (y + 1) * nz_len] = turned[y]


def emit_modes(terms, refs, own, rest):
    height = terms.shape[0] // (own * len(refs))
    for k, ref in enumerate(refs):
        tail = jnp.zeros((height, LANES), F32)
        for a in range(own):
            first = (k * own + a) * height
            block = terms[first : first + height]
            ref[a] = block[:, :LANES].astype(ref.dtype)
            tail = jnp.where(tail_mask(a, height, rest), block[:, LANES:], tail)
        ref[own] = tail.astype(ref.dtype)


def line_forward(spec, line):
    half = 2 * LANES
    depth = line.shape[1] // 2
    return dot(line[:, :depth], spec[:, :half]) + dot(line[:, depth:], spec[:, half:])


def planes_of(mode_refs, inverse, weight_ref, stack_ref, planes_ref, own, rest):
    height = mode_refs[0].shape[1]
    half = 2 * LANES
    for k, ref in enumerate(mode_refs):
        tail = ref[own].astype(F32)
        for a in range(own):
            first = (k * own + a) * height
            stack_ref[first : first + height, :LANES] = ref[a]
            masked = jnp.where(tail_mask(a, height, rest), tail, 0.0)
            stack_ref[first : first + height, LANES:] = masked.astype(BF16)
    depth = inverse.shape[0] // 2
    for j in range(2):
        part = dot(inverse[j * depth : (j + 1) * depth, :], stack_ref[...])
        columns = slice(j * half, (j + 1) * half)
        planes_ref[:, columns] = (part * weight_ref[:, columns]).astype(BF16)


def gelu_slope(values):
    bell = jnp.exp(-0.5 * values * values) * (1.0 / math.sqrt(2.0 * math.pi))
    return 0.5 * (1.0 + lax.erf(values * (1.0 / math.sqrt(2.0)))) + values * bell


def iota(shape, axis):
    return lax.broadcasted_iota(jnp.int32, shape, axis)


def forward_kernel(own, rest, count, s_ref, fields_hbm, basis_hbm, line_hbm, flat_ref, *refs):
    outs, refs = refs[:count], refs[count:]
    fields_ref, basis_ref, line_ref, fields_sem, basis_sem, line_sem = refs
    rows, _, _ = fields_ref.shape
    parts = fields_sem.shape[0]
    part = rows // parts
    pieces = basis_sem.shape[0]
    piece = basis_ref.shape[0] // pieces
    fields = [
        pltpu.make_async_copy(
            fields_hbm.at[pl.ds(k * part, part)], fields_ref.at[pl.ds(k * part, part)], fields_sem.at[k]
        )
        for k in range(parts)
    ]
    basis = [
        pltpu.make_async_copy(
            basis_hbm.at[pl.ds(k * piece, piece)], basis_ref.at[pl.ds(k * piece, piece)], basis_sem.at[k]
        )
        for k in range(pieces)
    ]
    line = pltpu.make_async_copy(line_hbm.at[s_ref[0]], line_ref, line_sem)
    for copy in fields + basis + [line]:
        copy.start()
    for k, copy in enumerate(fields):
        copy.wait()
        spread_rows(fields_ref, flat_ref, k * part, part)
    total = None
    for k, copy in enumerate(basis):
        copy.wait()
        span = slice(k * piece, (k + 1) * piece)
        term = dot(flat_ref[:, span], basis_ref[span])
        total = term if total is None else total + term
    line.wait()
    emit_modes(line_forward(total.astype(BF16), line_ref[...]), outs, own, rest)


def prepare_kernel(planes, part, cot_hbm, weight_hbm, flat_ref, channel_ref, bias_ref, *refs):
    out_ref, local_ref, down_ref, weight_ref, cot_ref, sem = refs
    cot_copy = pltpu.make_async_copy(cot_hbm, cot_ref, sem.at[0])
    cot_copy.start()
    weight_copy = pltpu.make_async_copy(weight_hbm, weight_ref, sem.at[1])
    weight_copy.start()
    rows, columns = flat_ref.shape
    chans = rows // planes
    row = iota((rows, chans), 0)
    column = iota((rows, chans), 1)
    member = (row >= column * planes) & (row < (column + 1) * planes)
    spread = jnp.where(member, 1.0, 0.0).astype(BF16)
    same = lax.rem(iota((rows, rows), 0), planes) == lax.rem(iota((rows, rows), 1), planes)
    channel = channel_ref[...]
    up = dot_nt(dot(spread, channel).astype(BF16), spread)
    down = dot_nt(dot_nt(spread, channel).astype(BF16), spread)
    up = jnp.where(same, up, 0.0).astype(BF16)
    down_ref[...] = jnp.where(same, down, 0.0).astype(BF16)
    bias = jnp.sum(jnp.where(member, bias_ref[...], 0.0), axis=1, keepdims=True)
    step = 8 * LANES
    for k in range(columns // step):
        span = slice(k * step, (k + 1) * step)
        local_ref[:, span] = dot(up, flat_ref[:, span]) + bias
    cot_copy.wait()
    for k in range(rows // part):
        spread_rows(cot_ref, out_ref, k * part, part)
    weight_copy.wait()


def sum_modes(mode_refs, scale, total_ref, out_ref, own):
    for blk in range(own + 1):
        total = mode_refs[0][blk]
        for ref in mode_refs[1:]:
            total = total + ref[blk].astype(F32)
        total = total * scale
        total_ref[blk] = total
        out_ref[blk] = total.astype(BF16)


def load_wide(total_ref, wide_ref, a, own, rest):
    wide_ref[:, :LANES] = total_ref[a]
    wide_ref[:, LANES:] = pltpu.roll(total_ref[own], lax.rem(LANES - a * rest, LANES), 1)


def store_wide(wide_ref, tail_ref, out_ref, a, own, rest):
    out_ref[a] = wide_ref[:, :LANES].astype(BF16)
    moved = pltpu.roll(wide_ref[:, LANES:], a * rest, 1)
    height = moved.shape[0]
    tail_ref[...] = jnp.where(tail_mask(a, height, rest), moved, tail_ref[...])

    @pl.when(a == own - 1)
    def _():
        out_ref[own] = tail_ref[...].astype(BF16)


def mix_kernel(own, rest, count, scale, *refs):
    refs = refs[1:]
    modes, (weight_ref, out_ref, sum_ref) = refs[:count], refs[count : count + 3]
    total_ref, wide_ref, result_ref, tail_ref = refs[count + 3 :]
    chans = weight_ref.shape[2]
    pairs = weight_ref.shape[4]
    sum_modes(modes, scale, total_ref, sum_ref, own)
    result_ref[...] = jnp.zeros_like(result_ref)
    tail_ref[...] = jnp.zeros_like(tail_ref)

    @pl.loop(0, own)
    def _(a):
        load_wide(total_ref, wide_ref, a, own, rest)
        real = jnp.zeros((chans, pairs), F32)
        imag = jnp.zeros((chans, pairs), F32)
        for i in range(chans):
            w_real = weight_ref[a, 0, i].astype(F32)
            w_imag = weight_ref[a, 1, i].astype(F32)
            u_real = wide_ref[i : i + 1, :pairs]
            u_imag = wide_ref[chans + i : chans + i + 1, :pairs]
            real = real + (w_real * u_real - w_imag * u_imag)
            imag = imag + (w_real * u_imag + w_imag * u_real)
        result_ref[:chans, :pairs] = real
        result_ref[chans:, :pairs] = imag
        store_wide(result_ref, tail_ref, out_ref, a, own, rest)


def total_kernel(own, count, *refs):
    modes, (chan_ref, total_ref, sum_ref) = refs[:count], refs[count:]
    chans = chan_ref.shape[0]
    sum_modes(modes, 1.0, total_ref, sum_ref, own)
    chan = chan_ref[...]
    for ref in modes[1:]:
        chan = chan + (ref[own + 1, :chans].astype(F32) + ref[own + 1, chans:].astype(F32))
    upper = chan.astype(BF16)
    sum_ref[own + 1, :chans] = upper
    sum_ref[own + 1, chans:] = (chan - upper.astype(F32)).astype(BF16)


def mix_back_kernel(own, rest, ties, *refs):
    total_ref, weight_ref, out_ref, wide_ref, result_ref, tail_ref, part_ref = refs[ties:]
    chans = weight_ref.shape[2]
    pairs = weight_ref.shape[4]
    group = 8
    result_ref[...] = jnp.zeros_like(result_ref)
    tail_ref[...] = jnp.zeros_like(tail_ref)

    @pl.loop(0, own)
    def _(a):
        load_wide(total_ref, wide_ref, a, own, rest)
        g_real = wide_ref[:chans, :pairs]
        g_imag = wide_ref[chans:, :pairs]
        for i in range(chans):
            w_real = weight_ref[a, 0, i].astype(F32)
            w_imag = weight_ref[a, 1, i].astype(F32)
            real = w_real * g_real + w_imag * g_imag
            imag = w_real * g_imag - w_imag * g_real
            real = sum(real[k : k + group] for k in range(0, chans, group))
            imag = sum(imag[k : k + group] for k in range(0, chans, group))
            for r, value in enumerate((real, imag)):
                first = (r * chans + i) * group
                part_ref[0, first : first + group, :] = value[:, :LANES]
                part_ref[1, first : first + group, : pairs - LANES] = value[:, LANES:]
        for half in range(2):
            rows = [part_ref[half, pl.ds(k, 2 * chans, stride=group), :] for k in range(group)]
            result_ref[:, half * LANES : (half + 1) * LANES] = sum(rows[1:], rows[0])
        store_wide(result_ref, tail_ref, out_ref, a, own, rest)


def middle_kernel(own, rest, count, planes, ties, s_ref, *refs):
    refs = refs[ties:]
    modes, refs = refs[:count], refs[count:]
    inverse_ref, line_ref, weight_ref, flat_ref, cot_ref, local_ref, basis_ref = refs[:7]
    hidden_ref, chan_ref, refs = refs[7], refs[8], refs[9:]
    outs, (stack_ref, planes_ref) = refs[:count], refs[count:]
    planes_of(modes, inverse_ref[s_ref[0]], weight_ref, stack_ref, planes_ref, own, rest)
    rows, columns = flat_ref.shape
    step = 4 * LANES
    back = jnp.zeros((rows, weight_ref.shape[1]), F32)
    cross = jnp.zeros((rows, rows), F32)
    for k in range(columns // step):
        span = slice(k * step, (k + 1) * step)
        summed = dot_nt(planes_ref[...], basis_ref[span]) + local_ref[:, span]
        hidden = (cot_ref[:, span].astype(F32) * gelu_slope(summed)).astype(BF16)
        hidden_ref[:, span] = hidden
        back = back + dot(hidden, basis_ref[span])
        cross = cross + dot_nt(hidden, flat_ref[:, span])
    spec = (back * weight_ref[...]).astype(BF16)
    emit_modes(line_forward(spec, line_ref[s_ref[0]]), outs, own, rest)
    chans = rows // planes
    same = lax.rem(iota((rows, rows), 0), planes) == lax.rem(iota((rows, rows), 1), planes)
    cross = jnp.where(same, cross, 0.0)
    row, column = iota((chans, rows), 0), iota((chans, rows), 1)
    group = jnp.where((column >= row * planes) & (column < (row + 1) * planes), 1.0, 0.0)
    row, column = iota((rows, LANES), 0), iota((rows, LANES), 1)
    place = jnp.where((row >= column * planes) & (row < (column + 1) * planes), 1.0, 0.0)
    exact = functools.partial(jnp.dot, preferred_element_type=F32, precision=lax.Precision.HIGHEST)
    sums = jnp.where(column == chans, back[:, :1], 0.0)
    chan = exact(group, exact(cross, place) + sums)
    chan_ref[...] = chan
    upper = chan.astype(BF16)
    lower = (chan - upper.astype(F32)).astype(BF16)
    for ref in outs[1:]:
        ref[own + 1, :chans] = upper
        ref[own + 1, chans:] = lower


def last_kernel(own, rest, count, part, ties, s_ref, *refs):
    refs = refs[ties:]
    modes, refs = refs[:count], refs[count:]
    inverse_ref, weight_ref, mix_ref, hidden_ref, basis_ref, out_hbm = refs[:6]
    stack_ref, planes_ref, turned_ref, out_ref, sem = refs[6:]
    rows, ny_len, nz_len = out_ref.shape
    planes_of(modes, inverse_ref[s_ref[0]], weight_ref, stack_ref, planes_ref, own, rest)
    group = 4
    step = group * nz_len
    for k in range(ny_len // group):
        span = slice(k * step, (k + 1) * step)
        total = dot_nt(planes_ref[...], basis_ref[span]) + dot(mix_ref[...], hidden_ref[:, span])
        total = total.astype(BF16)
        for y in range(group):
            turned_ref[k * group + y] = total[:, y * nz_len : (y + 1) * nz_len]
    copies = []
    for k in range(rows // part):
        span = slice(k * part, (k + 1) * part)
        out_ref[span] = jnp.swapaxes(turned_ref[:, span], 0, 1)
        here = pl.ds(k * part, part)
        copies.append(pltpu.make_async_copy(out_ref.at[here], out_hbm.at[here], sem.at[k]))
        copies[-1].start()
    for copy in copies:
        copy.wait()


def load_cells(u_refs, g_refs, u_all, g_all, factor):
    chans = g_all.shape[2]
    for b, (u_ref, g_ref) in enumerate(zip(u_refs, g_refs, strict=True)):
        g_real = g_ref[0, :chans].astype(F32)
        g_imag = g_ref[0, chans:].astype(F32)
        u_real = u_ref[0, :chans].astype(F32) * factor
        u_imag = u_ref[0, chans:].astype(F32) * factor
        g_all[b, 0] = g_real + g_imag
        g_all[b, 1] = g_real
        g_all[b, 2] = g_imag
        u_all[b, 0] = u_real
        u_all[b, 1] = u_real + u_imag
        u_all[b, 2] = u_real - u_imag


TOGETHER = 4


def products(u_all, g_all, first):
    sums = [[None] * 3 for _ in range(TOGETHER)]
    for b in range(u_all.shape[0]):
        for t in range(3):
            grad = g_all[b, t]
            for k in range(TOGETHER):
                term = u_all[b, t, pl.ds(first + k, 1), :] * grad
                sums[k][t] = term if sums[k][t] is None else sums[k][t] + term
    return [(part[0] - part[2], part[0] - part[1]) for part in sums]


def tag_sum(refs, chans):
    total = jnp.zeros((chans, LANES), F32)
    for ref in refs:
        total = total + (ref[0, :chans].astype(F32) + ref[0, chans:].astype(F32))
    return total


def early_kernel(cells, ties, factor, *refs):
    refs = refs[ties:]
    u_refs, g_refs, c_refs = refs[:cells], refs[cells : 2 * cells], refs[2 * cells : 3 * cells]
    out_ref, chan_ref, u_all, g_all = refs[3 * cells :]
    chans = g_all.shape[2]
    load_cells(u_refs, g_refs, u_all, g_all, factor)

    @pl.when(pl.program_id(0) == 0)
    def _():
        chan_ref[...] = tag_sum(c_refs, chans)

    @pl.loop(0, chans, step=TOGETHER)
    def _(i):
        for k, parts in enumerate(products(u_all, g_all, i)):
            for r, part in enumerate(parts):
                out_ref[0, r, i + k] = part.astype(BF16)


def outer_kernel(rest, cells, sums, factor, norm, *refs):
    u_refs, g_refs, c_refs = refs[:cells], refs[cells : 2 * cells], refs[2 * cells : 3 * cells]
    refs = refs[3 * cells :]
    sum_refs, sum_chans, refs = refs[:sums], refs[sums : 2 * sums], refs[2 * sums :]
    out_ref, chan_ref, bias_ref, u_all, g_all, tail_ref = refs
    step = pl.program_id(0)
    chans = g_all.shape[2]
    load_cells(u_refs, g_refs, u_all, g_all, factor)

    def totals(i):
        for k, parts in enumerate(products(u_all, g_all, i)):
            for r, part in enumerate(parts):
                for ref in sum_refs:
                    part = part + ref[0, r, i + k].astype(F32)
                yield r, i + k, part

    @pl.when(step == 0)
    def _():
        chan = tag_sum(c_refs, chans)
        for ref in sum_chans:
            chan = chan + ref[...]
        chan = chan * norm
        chan_ref[...] = chan[:, :chans]
        same = iota((chans, LANES), 0) == iota((chans, LANES), 1)
        bias = jnp.sum(jnp.where(same, chan[:, chans : chans + 1], 0.0), axis=0, keepdims=True)
        bias_ref[...] = bias[:, :chans]

        @pl.loop(0, chans, step=TOGETHER)
        def _(i):
            for r, at, part in totals(i):
                tail_ref[r, at] = part

    @pl.when(step > 0)
    def _():
        shift = lax.rem(LANES - (step - 1) * rest, LANES)

        @pl.loop(0, chans, step=TOGETHER)
        def _(i):
            for r, at, part in totals(i):
                out_ref[0, r, at, :, :LANES] = part
                out_ref[0, r, at, :, LANES:] = pltpu.roll(tail_ref[r, at], shift, 1)[:, :rest]


def about(microseconds):
    return pl.CostEstimate(
        flops=int(microseconds * 1.15e9), bytes_accessed=int(microseconds * 3.6e6), transcendentals=0
    )


def call(kernel, name, time, ins, outs, scratch=(), limit=16):
    return pl.pallas_call(
        kernel,
        in_specs=ins,
        out_specs=[pl.BlockSpec(memory_space=out[2] if len(out) > 2 else pltpu.VMEM) for out in outs],
        out_shape=[jax.ShapeDtypeStruct(*out[:2]) for out in outs],
        scratch_shapes=list(scratch),
        compiler_params=pltpu.CompilerParams(vmem_limit_bytes=limit * 1024 * 1024),
        cost_estimate=about(time),
        name=name,
    )


def here(number):
    return [pl.BlockSpec(memory_space=pltpu.VMEM)] * number


def there(number):
    return [pl.BlockSpec(memory_space=pltpu.HBM)] * number


def send(array, axis, count, shift):
    return lax.ppermute(array, axis, [(i, (i + shift) % count) for i in range(count)])


def swap(array, bit, count):
    return lax.ppermute(array, "dp", [(i, i ^ bit) for i in range(count)])


def first_cells(array, count):
    if count & (count - 1) or count < 8:
        return []
    return [array, swap(array, 2, count)] + [swap(array, 4 * z, count) for z in range(1, count // 4)]


def order_cells(array, first, count):
    if not first:
        return [], list(lax.all_gather(array, "dp"))
    near = first[:2] + [piece for far in first[2:] for piece in (far, swap(far, 2, count))]
    return near[: len(near) // 2], near[len(near) // 2 :]


def scratch_cells(cells, chans):
    return [pltpu.VMEM((cells, 3, chans, LANES), F32)] * 2


def early_gradient(all_u, all_g, ties, own, cell_norm):
    cells = len(all_u)
    chans = all_u[0].shape[1] // 2
    block = (1,) + all_u[0].shape[1:]
    one = pl.BlockSpec(block, lambda i: (i, 0, 0))
    tag = pl.BlockSpec(block, lambda i: (own + 1, 0, 0))
    return pl.pallas_call(
        functools.partial(early_kernel, cells, len(ties), cell_norm),
        grid=(own + 1,),
        in_specs=there(len(ties)) + [one] * (2 * cells) + [tag] * cells,
        out_specs=[
            pl.BlockSpec((1, 2, chans, chans, LANES), lambda i: (i, 0, 0, 0, 0)),
            pl.BlockSpec((chans, LANES), lambda i: (0, 0)),
        ],
        out_shape=[
            jax.ShapeDtypeStruct((own + 1, 2, chans, chans, LANES), BF16),
            jax.ShapeDtypeStruct((chans, LANES), F32),
        ],
        scratch_shapes=scratch_cells(cells, chans),
        compiler_params=pltpu.CompilerParams(vmem_limit_bytes=16 * 1024 * 1024),
        cost_estimate=about(4.8),
        name="early",
    )(*ties, *all_u, *all_g, *all_g)


def weight_gradient(all_u, all_g, sums, weight_shape, norms):
    own, _, chans, _, pairs = weight_shape
    cell_norm, voxel_norm = norms
    block = (1,) + all_u[0].shape[1:]
    cells = len(all_u)
    at = lambda i: jnp.where(i == 0, own, i - 1)
    one = pl.BlockSpec(block, lambda i: (at(i), 0, 0))
    tag = pl.BlockSpec(block, lambda i: (own + 1, 0, 0))
    add = pl.BlockSpec((1, 2, chans, chans, LANES), lambda i: (at(i), 0, 0, 0, 0))
    add_chan = pl.BlockSpec((chans, LANES), lambda i: (0, 0))
    half = len(sums) // 2
    return pl.pallas_call(
        functools.partial(outer_kernel, pairs - LANES, cells, half, cell_norm, voxel_norm),
        grid=(own + 1,),
        in_specs=[one] * (2 * cells) + [tag] * cells + [add] * half + [add_chan] * half,
        out_specs=[
            pl.BlockSpec((1,) + weight_shape[1:], lambda i: (jnp.maximum(i - 1, 0), 0, 0, 0, 0)),
            pl.BlockSpec((chans, chans), lambda i: (0, 0)),
            pl.BlockSpec((1, chans), lambda i: (0, 0)),
        ],
        out_shape=[
            jax.ShapeDtypeStruct(weight_shape, F32),
            jax.ShapeDtypeStruct((chans, chans), F32),
            jax.ShapeDtypeStruct((1, chans), F32),
        ],
        scratch_shapes=scratch_cells(cells, chans) + [pltpu.VMEM((2, chans, chans, LANES), F32)],
        compiler_params=pltpu.CompilerParams(vmem_limit_bytes=20 * 1024 * 1024),
        cost_estimate=about(12.8),
        name="outer",
    )(*all_u, *all_g, *all_g, *sums)


def shards(count, cell_count, fields, cotangent, spectral_weight, channel_weight, channel_bias):
    _, chans, planes, ny_len, nz_len = fields.shape
    own, _, _, _, pairs = spectral_weight.shape
    rest = pairs - LANES
    rows = chans * planes
    columns = ny_len * nz_len
    block = min(rows, 64)
    scale = 1.0 / math.sqrt(planes * count * columns)
    cell_norm = 1.0 / math.sqrt(cell_count)
    voxel_norm = 1.0 / math.sqrt(cell_count * planes * count * columns)
    height = 2 * chans
    wide = 4 * LANES

    basis = jnp.asarray(plane_table(ny_len, nz_len, own))
    line_np = line_tables(chans, planes, count)
    line = jnp.asarray(line_np)
    inverse = jnp.asarray(np.ascontiguousarray(np.swapaxes(line_np, 1, 2)))
    up_weight = jnp.asarray(column_weight(own, scale))
    down_weight = jnp.asarray(np.full((1, wide), scale, np.float32))
    place = lax.axis_index("space").astype(jnp.int32).reshape(1)

    modes = ((own + 1, height, LANES), F32)
    sent = ((own + 1, height, LANES), BF16)
    tagged = ((own + 2, height, LANES), BF16)
    grid_like = (rows, ny_len, nz_len)

    flat, mine, *others = call(
        functools.partial(forward_kernel, own, rest, count),
        "forward",
        4.3,
        [pl.BlockSpec(memory_space=pltpu.SMEM)] + there(3),
        [((rows, columns), BF16), modes] + [sent] * (count - 1),
        [
            pltpu.VMEM(grid_like, BF16),
            pltpu.VMEM(basis.shape, BF16),
            pltpu.VMEM(line.shape[1:], BF16),
            pltpu.SemaphoreType.DMA((rows // block,)),
            pltpu.SemaphoreType.DMA((5,)),
            pltpu.SemaphoreType.DMA,
        ],
        52,
    )(place, fields.reshape(grid_like), basis, line)
    arrived = [send(array, "space", count, k + 1) for k, array in enumerate(others)]
    cot, local, mix_down, weights = call(
        functools.partial(prepare_kernel, planes, block),
        "prepare",
        2.5,
        there(2) + here(3),
        [((rows, columns), BF16), ((rows, columns), F32), ((rows, rows), BF16), (spectral_weight.shape, BF16)],
        [pltpu.VMEM(grid_like, BF16), pltpu.SemaphoreType.DMA((2,))],
        28,
    )(cotangent.reshape(grid_like), spectral_weight, flat, channel_weight, channel_bias.reshape(1, chans))

    mix_scratch = [
        pltpu.VMEM((height, 2 * LANES), F32),
        pltpu.VMEM((height, 2 * LANES), F32),
        pltpu.VMEM((height, LANES), F32),
    ]
    mixed, field_modes = call(
        functools.partial(mix_kernel, own, rest, count, scale),
        "mix",
        3.9,
        there(1) + here(count + 1),
        [sent, sent],
        [pltpu.VMEM(modes[0], F32)] + mix_scratch,
    )(cot, mine, *arrived, weights)

    u_first = first_cells(field_modes, cell_count)
    ties = u_first[1:3]
    all_mixed = [mixed] + [send(mixed, "space", count, -k) for k in range(1, count)]
    plane_scratch = [pltpu.VMEM((count * own * height, 2 * LANES), BF16), pltpu.VMEM((rows, wide), BF16)]
    hidden, chan, mine, *others = call(
        functools.partial(middle_kernel, own, rest, count, planes, len(ties)),
        "middle",
        6.3,
        [pl.BlockSpec(memory_space=pltpu.SMEM)] + there(len(ties)) + here(count + 7),
        [((rows, columns), BF16), ((chans, LANES), F32), modes] + [tagged] * (count - 1),
        plane_scratch,
    )(place, *ties, *all_mixed, inverse, line, up_weight, flat, cot, local, basis)
    arrived = [send(array, "space", count, k + 1) for k, array in enumerate(others)]

    total, grad_modes = call(
        functools.partial(total_kernel, own, count), "total", 1.0, here(count + 1), [modes, tagged]
    )(mine, *arrived, chan)
    ties = u_first[3:]
    (returned,) = call(
        functools.partial(mix_back_kernel, own, rest, len(ties)),
        "mix_back",
        4.1,
        there(len(ties)) + here(2),
        [sent],
        mix_scratch + [pltpu.VMEM((2, 2 * chans * 8, LANES), F32)],
    )(*ties, total, weights)

    g_first = first_cells(grad_modes, cell_count)
    all_returned = [returned] + [send(returned, "space", count, -k) for k in range(1, count)]
    early_u, late_u = order_cells(field_modes, u_first, cell_count)
    early_g, late_g = order_cells(grad_modes, g_first, cell_count)
    sums = []
    if early_u:
        late_u = late_u + [swap(piece, 1, cell_count) for piece in late_u]
        ties = all_returned + g_first[3:] + late_u
        part, part_chan = early_gradient(early_u, early_g, ties, own, cell_norm)
        sums = [part, swap(part, 1, cell_count), part_chan, swap(part_chan, 1, cell_count)]
        late_g = late_g + [swap(piece, 1, cell_count) for piece in late_g]
    ties = sums[:1]
    (grad_fields,) = call(
        functools.partial(last_kernel, own, rest, count, block, len(ties)),
        "last",
        4.4,
        [pl.BlockSpec(memory_space=pltpu.SMEM)] + there(len(ties)) + here(count + 5),
        [(grid_like, BF16, pltpu.HBM)],
        plane_scratch
        + [
            pltpu.VMEM((ny_len, rows, nz_len), BF16),
            pltpu.VMEM(grid_like, BF16),
            pltpu.SemaphoreType.DMA((rows // block,)),
        ],
    )(place, *ties, *all_returned, inverse, down_weight, mix_down, hidden, basis)

    grad_spectral, grad_channel, grad_bias = weight_gradient(
        late_u, late_g, sums, spectral_weight.shape, (cell_norm, voxel_norm)
    )
    return (grad_fields.reshape(fields.shape), grad_spectral, grad_channel, grad_bias.reshape(chans))


def solution(mesh):
    in_specs = (
        P("dp", None, "space", None, None),
        P("dp", None, "space", None, None),
        P("space", None, None, None, None),
        P(),
        P(),
    )
    out_specs = (P("dp", None, "space", None, None), P("space", None, None, None, None), P(), P())
    body = functools.partial(shards, mesh.shape["space"], mesh.shape["dp"])
    return jax.shard_map(body, mesh=mesh, in_specs=in_specs, out_specs=out_specs, check_vma=False)
```

time: 339 us -> 100 us (0.29); the launches traced: 333 us -> 99.8 us
  waiting for transfers between devices: 146 us -> 18.1 us
  blocking collectives: 57.2 us -> 0 us
  other arithmetic: 56 us -> 0.01 us
  Pallas kernels: 0 us -> 46.7 us
  starting transfers between devices: 0.29 us -> 32.3 us
  matrix products: 32 us -> 0 us
  local copies, waits for them, and re-layouts: 27.2 us -> 1.78 us
  between operations: 14.8 us -> 0.87 us
    psum x1 -> x0, waiting for transfers between devices: 146 us -> none  [shards(): lax.psum(weight_terms(field_modes, grad_modes_out).astype(jnp.bfloat16),...]
    pallas_call x0 -> x9, Pallas kernels: none -> 46.7 us  [the longest x1 12.8 us: weight_gradient(): pl.pallas_call(functools.partial(outer_kernel, pairs - LANES, cells, half...]
    psum x1 -> x0, blocking collectives: 41.1 us -> none  [shards(): lax.psum((local_channel, local_bias), ('dp', 'space'))]
    ppermute x0 -> x28, starting transfers between devices: none -> 32.3 us  [the longest x24 28.4 us: swap(): return lax.ppermute(array, 'dp', [(i, i ^ bit) for i in range(count)])]
    dot_general x11 -> x0, matrix products: 32 us -> none  [the longest x1 6.63 us: shards(): jnp.einsum('boxjp,qjp->boxq', mixed_planes, basis, preferred_element_type...]
    another operation x11 -> x0, other arithmetic: 24 us -> none
    ppermute x0 -> x28, waiting for transfers between devices: none -> 18.1 us  [the longest x24 13.7 us: swap(): return lax.ppermute(array, 'dp', [(i, i ^ bit) for i in range(count)])]
    all_gather x2 -> x0, blocking collectives: 16.1 us -> none  [spread_modes(): lax.all_gather(modes.astype(jnp.bfloat16), 'space', axis=2, tiled=True)]
  transfers between devices with their start and end apart: 3 -> 28, of which waited for: 1 -> 6; matrix products, arithmetic and copies ran while one was open for 11% -> 0% of each run, Pallas kernels for 0% -> 18%
where the time goes in v2:
time: 100 us; the launch traced here: 99.8 us
  Pallas kernels  46.7 us (47%)
  starting transfers between devices  32.3 us (32%)
  waiting for transfers between devices  18.1 us (18%)
  local copies, waits for them, and re-layouts  1.78 us (2%)
    ppermute x24, starting transfers between devices, swap(): return lax.ppermute(array, 'dp', [(i, i ^ bit) for i in range(count)])  28.4 us
    ppermute x24, waiting for transfers between devices, swap(): return lax.ppermute(array, 'dp', [(i, i ^ bit) for i in range(count)])  13.7 us
    pallas_call x1, Pallas kernels, weight_gradient(): pl.pallas_call(functools.partial(outer_kernel, pairs - LANES, cells, half...  12.8 us
    pallas_call x1, Pallas kernels, shards(): call(functools.partial(forward_kernel, own, rest, count), 'forward', 4.3,...  6.61 us
    pallas_call x1, Pallas kernels, shards(): call(functools.partial(middle_kernel, own, rest, count, planes, len(ties)...  6.2 us
    pallas_call x1, Pallas kernels, early_gradient(): pl.pallas_call(functools.partial(early_kernel, cells, len(ties), cell_nor...  5.05 us
    ppermute x4, waiting for transfers between devices, send(): lax.ppermute(array, axis, [(i, (i + shift) % count) for i in range(count)])  4.46 us
    pallas_call x1, Pallas kernels, shards(): call(functools.partial(last_kernel, own, rest, count, block, len(ties)),...  4.3 us
  transfers between devices with their start and end apart: 28, of which 6 were waited for; matrix products, arithmetic and copies ran while one was open for 0% of the time, Pallas kernels for 18%

profile of v2, /device:TPU:1, one launch (start us, length us, event | category | flops | bytes accessed | tf_op | source)
XLA Modules:
  0.0 99.8 jit_solution(17762239284380558362)
XLA Ops:
  0.7 6.6 %forward.1 = (bf16[256,5120]{1,0:T(8,128)(2,1)}, f32[9,64,128]{2,1,0:T(8,128)S(1)}, bf16[9,64,128]{2,1,0:T(8,128)(2,1)S(1)}) custom-call(s32[1]{0:T(128)} %bitcast.s_ref, bf16[256,40,128]{2,1,0:T(8,128)(2,1)} %bitcast.10, bf16[5120,512]{1,0:T(8,128)(2,1)} %constant.14.clone.basis_hbm.refs_10_.refs_7_, bf16[2,1024,512]{2,1,0:T(8,128)(2,1)} %constant.15.clone.line_hbm.refs_5_), custom_call_target="tpu_custom_call" | custom-call | flops 4944999936 | bytes 15480000 | tf_op jit(solution)/shard_map/forward/pallas_call | solution.py:593
  7.3 2.1 %collective-permute-start = (bf16[9,64,128]{2,1,0:T(8,128)(2,1)S(1)}, bf16[9,64,128]{2,1,0:T(8,128)(2,1)S(1)}, u32[]{:S(2)}, u32[]{:S(2)}) collective-permute-start(bf16[9,64,128]{2,1,0:T(8,128)(2,1)S(1)} %get-tuple-element.27), channel_id=1, source_target_pairs={{0,1},{1,0},{2,3},{3,2},{4,5},{5,4},{6,7},{7,6},{8,9},{9,8},{10,11... | collective-permute-start | bytes 442376 | tf_op jit(solution)/shard_map/ppermute | solution.py:486
  9.4 1.7 %copy-done.1 = bf16[256,5120]{1,0:T(8,128)(2,1)S(1)} copy-done((bf16[256,5120]{1,0:T(8,128)(2,1)S(1)}, bf16[256,5120]{1,0:T(8,128)(2,1)}, u32[]{:S(2)}) %copy-start.1) | copy-done | bytes 2621464
  11.1 3.7 %prepare.1 = (bf16[256,5120]{1,0:T(8,128)(2,1)S(1)}, f32[256,5120]{1,0:T(8,128)S(1)}, bf16[256,256]{1,0:T(8,128)(2,1)S(1)}, bf16[8,2,32,32,144]{4,3,2,1,0:T(8,128)(2,1)S(1)}) custom-call(bf16[256,40,128]{2,1,0:T(8,128)(2,1)S(1)} %bitcast.6, bf16[8,2,32,32,144]{4,3,2,1,0:T(8,128)(2,1)} %weight_hbm.1, bf16[256,5120]{1,0:T(8,128)(2,1)S(1)} %copy-done.1, ...), custom_call_target="tpu_custom_call" | custom-call | flops 2875000064 | bytes 9000000 | tf_op jit(solution)/shard_map/prepare/pallas_call | solution.py:610
  14.9 3.9 %mix.1 = (bf16[9,64,128]{2,1,0:T(8,128)(2,1)S(1)}, bf16[9,64,128]{2,1,0:T(8,128)(2,1)S(1)}) custom-call(bf16[256,5120]{1,0:T(8,128)(2,1)S(1)} %get-tuple-element.25.refs_0_.refs_8_, f32[9,64,128]{2,1,0:T(8,128)S(1)} %get-tuple-element.26.refs_1_, bf16[9,64,128]{2,1,0:T(8,128)(2,1)S(1)} %collective-permute-done.refs_2_, ...), custom_call_target="tpu_custom_call" | custom-call | flops 4485000192 | bytes 14040000 | tf_op jit(solution)/shard_map/mix/pallas_call | solution.py:625
  18.9 1.5 %collective-permute-start.4 = (bf16[9,64,128]{2,1,0:T(8,128)(2,1)S(1)}, bf16[9,64,128]{2,1,0:T(8,128)(2,1)S(1)}, u32[]{:S(2)}, u32[]{:S(2)}) collective-permute-start(bf16[9,64,128]{2,1,0:T(8,128)(2,1)S(1)} %get-tuple-element.29.refs_12_), channel_id=1, source_target_pairs={{0,8},{2,10},{4,12},{6,14},{8,0},{10,2},{12,4},{14,6},{16,24},{18,... | collective-permute-start | bytes 442376 | tf_op jit(solution)/shard_map/ppermute | solution.py:490
  20.5 1.2 %collective-permute-start.3 = (bf16[9,64,128]{2,1,0:T(8,128)(2,1)S(1)}, bf16[9,64,128]{2,1,0:T(8,128)(2,1)S(1)}, u32[]{:S(2)}, u32[]{:S(2)}) collective-permute-start(bf16[9,64,128]{2,1,0:T(8,128)(2,1)S(1)} %get-tuple-element.29.refs_12_), channel_id=1, source_target_pairs={{0,4},{2,6},{4,0},{6,2},{8,12},{10,14},{12,8},{14,10},{16,20},{18,... | collective-permute-start | bytes 442376 | tf_op jit(solution)/shard_map/ppermute | solution.py:490
  21.7 2.2 %collective-permute-start.2 = (bf16[9,64,128]{2,1,0:T(8,128)(2,1)S(1)}, bf16[9,64,128]{2,1,0:T(8,128)(2,1)S(1)}, u32[]{:S(2)}, u32[]{:S(2)}) collective-permute-start(bf16[9,64,128]{2,1,0:T(8,128)(2,1)S(1)} %get-tuple-element.29.refs_12_), channel_id=1, source_target_pairs={{0,24},{2,26},{4,28},{6,30},{8,16},{10,18},{12,20},{14,22},{16,8},... | collective-permute-start | bytes 442376 | tf_op jit(solution)/shard_map/ppermute | solution.py:490
  23.9 0.8 collective-permute-done.3.refs_0_.refs_13_
  24.8 6.2 %middle.1 = (bf16[256,5120]{1,0:T(8,128)(2,1)S(1)}, f32[32,128]{1,0:T(8,128)S(1)}, f32[9,64,128]{2,1,0:T(8,128)S(1)}, bf16[10,64,128]{2,1,0:T(8,128)(2,1)S(1)}) custom-call(s32[1]{0:T(128)} %bitcast.s_ref, bf16[9,64,128]{2,1,0:T(8,128)(2,1)S(1)} %collective-permute-done.3.refs_0_.refs_13_, bf16[9,64,128]{2,1,0:T(8,128)(2,1)S(1)} %collective-permute-done.4.refs_1_.refs_14_, ...), custom_call_target="tpu_custom_call" | custom-call | flops 7245000192 | bytes 22680000 | tf_op jit(solution)/shard_map/middle/pallas_call | solution.py:638
  31.0 1.3 %collective-permute-start.6 = (bf16[10,64,128]{2,1,0:T(8,128)(2,1)S(1)}, bf16[10,64,128]{2,1,0:T(8,128)(2,1)S(1)}, u32[]{:S(2)}, u32[]{:S(2)}) collective-permute-start(bf16[10,64,128]{2,1,0:T(8,128)(2,1)S(1)} %get-tuple-element.33), channel_id=1, source_target_pairs={{0,1},{1,0},{2,3},{3,2},{4,5},{5,4},{6,7},{7,6},{8,9},{9,8},{10,11... | collective-permute-start | bytes 491528 | tf_op jit(solution)/shard_map/ppermute | solution.py:486
  32.3 2.3 %collective-permute-start.1 = (bf16[9,64,128]{2,1,0:T(8,128)(2,1)S(1)}, bf16[9,64,128]{2,1,0:T(8,128)(2,1)S(1)}, u32[]{:S(2)}, u32[]{:S(2)}) collective-permute-start(bf16[9,64,128]{2,1,0:T(8,128)(2,1)S(1)} %get-tuple-element.29.refs_12_), channel_id=1, source_target_pairs={{0,16},{2,18},{4,20},{6,22},{8,24},{10,26},{12,28},{14,30},{16,0},... | collective-permute-start | bytes 442376 | tf_op jit(solution)/shard_map/ppermute | solution.py:490
  34.6 1.2 %collective-permute-start.16 = (bf16[9,64,128]{2,1,0:T(8,128)(2,1)S(1)}, bf16[9,64,128]{2,1,0:T(8,128)(2,1)S(1)}, u32[]{:S(2)}, u32[]{:S(2)}) collective-permute-start(bf16[9,64,128]{2,1,0:T(8,128)(2,1)S(1)} %collective-permute-done.4.refs_1_.refs_14_), channel_id=1, source_target_pairs={{0,4},{2,6},{4,0},{6,2},{8,12},{10,14},{12,8},{14,10},{16,20},{18,... | collective-permute-start | bytes 442376 | tf_op jit(solution)/shard_map/ppermute | solution.py:490
  36.3 2.4 %collective-permute-done.1.refs_0_.refs_4_ = bf16[9,64,128]{2,1,0:T(8,128)(2,1)S(1)} collective-permute-done((bf16[9,64,128]{2,1,0:T(8,128)(2,1)S(1)}, bf16[9,64,128]{2,1,0:T(8,128)(2,1)S(1)}, u32[]{:S(2)}, u32[]{:S(2)}) %collective-permute-start.1) | collective-permute-done | bytes 147488 | tf_op jit(solution)/shard_map/ppermute | solution.py:490
  38.7 1.1 %collective-permute-start.10 = (bf16[9,64,128]{2,1,0:T(8,128)(2,1)S(1)}, bf16[9,64,128]{2,1,0:T(8,128)(2,1)S(1)}, u32[]{:S(2)}, u32[]{:S(2)}) collective-permute-start(bf16[9,64,128]{2,1,0:T(8,128)(2,1)S(1)} %collective-permute-done.1.refs_0_.refs_4_), channel_id=1, source_target_pairs={{0,4},{2,6},{4,0},{6,2},{8,12},{10,14},{12,8},{14,10},{16,20},{18,... | collective-permute-start | bytes 442376 | tf_op jit(solution)/shard_map/ppermute | solution.py:490
  39.9 4.5 %collective-permute-start.14 = (bf16[9,64,128]{2,1,0:T(8,128)(2,1)S(1)}, bf16[9,64,128]{2,1,0:T(8,128)(2,1)S(1)}, u32[]{:S(2)}, u32[]{:S(2)}) collective-permute-start(bf16[9,64,128]{2,1,0:T(8,128)(2,1)S(1)} %collective-permute-done.2.refs_1_.refs_6_.refs_2_), channel_id=1, source_target_pairs={{0,2},{2,0},{4,6},{6,4},{8,10},{10,8},{12,14},{14,12},{16,18},{18,... | collective-permute-start | bytes 442376 | tf_op jit(solution)/shard_map/ppermute | solution.py:490
  44.4 1.4 %collective-permute-start.15 = (bf16[9,64,128]{2,1,0:T(8,128)(2,1)S(1)}, bf16[9,64,128]{2,1,0:T(8,128)(2,1)S(1)}, u32[]{:S(2)}, u32[]{:S(2)}) collective-permute-start(bf16[9,64,128]{2,1,0:T(8,128)(2,1)S(1)} %collective-permute-done.11.refs_7_.refs_3_), channel_id=1, source_target_pairs={{0,2},{2,0},{4,6},{6,4},{8,10},{10,8},{12,14},{14,12},{16,18},{18,... | collective-permute-start | bytes 442376 | tf_op jit(solution)/shard_map/ppermute | solution.py:490
  45.8 1.9 %collective-permute-start.13 = (bf16[9,64,128]{2,1,0:T(8,128)(2,1)S(1)}, bf16[9,64,128]{2,1,0:T(8,128)(2,1)S(1)}, u32[]{:S(2)}, u32[]{:S(2)}) collective-permute-start(bf16[9,64,128]{2,1,0:T(8,128)(2,1)S(1)} %collective-permute-done.10.refs_5_.refs_1_), channel_id=1, source_target_pairs={{0,2},{2,0},{4,6},{6,4},{8,10},{10,8},{12,14},{14,12},{16,18},{18,... | collective-permute-start | bytes 442376 | tf_op jit(solution)/shard_map/ppermute | solution.py:490
  47.7 1.5 %collective-permute-start.17 = (bf16[10,64,128]{2,1,0:T(8,128)(2,1)S(1)}, bf16[10,64,128]{2,1,0:T(8,128)(2,1)S(1)}, u32[]{:S(2)}, u32[]{:S(2)}) collective-permute-start(bf16[10,64,128]{2,1,0:T(8,128)(2,1)S(1)} %get-tuple-element.36.refs_16_.refs_20_), channel_id=1, source_target_pairs={{0,4},{2,6},{4,0},{6,2},{8,12},{10,14},{12,8},{14,10},{16,20},{18,... | collective-permute-start | bytes 491528 | tf_op jit(solution)/shard_map/ppermute | solution.py:490
  49.2 3.3 %collective-permute-start.9 = (bf16[10,64,128]{2,1,0:T(8,128)(2,1)S(1)}, bf16[10,64,128]{2,1,0:T(8,128)(2,1)S(1)}, u32[]{:S(2)}, u32[]{:S(2)}) collective-permute-start(bf16[10,64,128]{2,1,0:T(8,128)(2,1)S(1)} %get-tuple-element.36.refs_16_.refs_20_), channel_id=1, source_target_pairs={{0,24},{2,26},{4,28},{6,30},{8,16},{10,18},{12,20},{14,22},{16,8},... | collective-permute-start | bytes 491528 | tf_op jit(solution)/shard_map/ppermute | solution.py:490
  52.7 4.1 %mix_back.1.refs_0_.refs_1_ = bf16[9,64,128]{2,1,0:T(8,128)(2,1)S(1)} custom-call(bf16[9,64,128]{2,1,0:T(8,128)(2,1)S(1)} %collective-permute-done.1.refs_0_.refs_4_, bf16[9,64,128]{2,1,0:T(8,128)(2,1)S(1)} %collective-permute-done.2.refs_1_.refs_6_.refs_2_, f32[9,64,128]{2,1,0:T(8,128)S(1)} %get-tuple-element.35.refs_2_, ...), custom_call_target="tpu_custom_call" | custom-call | flops 4714999808 | bytes 14759999 | tf_op jit(solution)/shard_map/mix_back/pallas_call | solution.py:652
  57.3 4.4 %collective-permute-done.7.refs_1_.refs_2_ = bf16[9,64,128]{2,1,0:T(8,128)(2,1)S(1)} collective-permute-done((bf16[9,64,128]{2,1,0:T(8,128)(2,1)S(1)}, bf16[9,64,128]{2,1,0:T(8,128)(2,1)S(1)}, u32[]{:S(2)}, u32[]{:S(2)}) %collective-permute-start.7) | collective-permute-done | bytes 147488 | tf_op jit(solution)/shard_map/ppermute | solution.py:486
  61.8 4.5 %collective-permute-done.8.refs_2_.refs_8_.refs_16_ = bf16[10,64,128]{2,1,0:T(8,128)(2,1)S(1)} collective-permute-done((bf16[10,64,128]{2,1,0:T(8,128)(2,1)S(1)}, bf16[10,64,128]{2,1,0:T(8,128)(2,1)S(1)}, u32[]{:S(2)}, u32[]{:S(2)}) %collective-permute-start.8) | collective-permute-done | bytes 163872 | tf_op jit(solution)/shard_map/ppermute | solution.py:490
  66.3 5.0 %early.1 = (bf16[9,2,32,32,128]{4,3,2,1,0:T(8,128)(2,1)S(1)}, f32[32,128]{1,0:T(8,128)S(1)}) custom-call(bf16[9,64,128]{2,1,0:T(8,128)(2,1)S(1)} %mix_back.1.refs_0_.refs_1_, bf16[9,64,128]{2,1,0:T(8,128)(2,1)S(1)} %collective-permute-done.7.refs_1_.refs_2_, bf16[10,64,128]{2,1,0:T(8,128)(2,1)S(1)} %collective-permute-done.8.refs_2_.refs_8_.refs_16_, ...), custom_call_target="tpu_custom_call" | custom-call | flops 5520000000 | bytes 17280000 | tf_op jit(solution)/shard_map/early/pallas_call | solution.py:516
  71.3 1.2 %collective-permute-start.26 = (bf16[9,2,32,32,128]{4,3,2,1,0:T(8,128)(2,1)S(1)}, bf16[9,2,32,32,128]{4,3,2,1,0:T(8,128)(2,1)S(1)}, u32[]{:S(2)}, u32[]{:S(2)}) collective-permute-start(bf16[9,2,32,32,128]{4,3,2,1,0:T(8,128)(2,1)S(1)} %get-tuple-element.37.refs_0_.refs_24_), channel_id=1, source_target_pairs={{0,2},{2,0},{4,6},{6,4},{8,10},{10,8},{12,14},{14,12},{16,18},{18,... | collective-permute-start | bytes 14155784 | tf_op jit(solution)/shard_map/ppermute | solution.py:490
  72.6 1.4 %collective-permute-start.20 = (bf16[10,64,128]{2,1,0:T(8,128)(2,1)S(1)}, bf16[10,64,128]{2,1,0:T(8,128)(2,1)S(1)}, u32[]{:S(2)}, u32[]{:S(2)}) collective-permute-start(bf16[10,64,128]{2,1,0:T(8,128)(2,1)S(1)} %collective-permute-done.8.refs_2_.refs_8_.refs_16_), channel_id=1, source_target_pairs={{0,4},{2,6},{4,0},{6,2},{8,12},{10,14},{12,8},{14,10},{16,20},{18,... | collective-permute-start | bytes 491528 | tf_op jit(solution)/shard_map/ppermute | solution.py:490
  74.0 1.0 collective-permute-start.22
  75.0 5.2 %collective-permute-done.24.refs_14_.refs_22_ = bf16[10,64,128]{2,1,0:T(8,128)(2,1)S(1)} collective-permute-done((bf16[10,64,128]{2,1,0:T(8,128)(2,1)S(1)}, bf16[10,64,128]{2,1,0:T(8,128)(2,1)S(1)}, u32[]{:S(2)}, u32[]{:S(2)}) %collective-permute-start.24) | collective-permute-done | bytes 163872 | tf_op jit(solution)/shard_map/ppermute | solution.py:490
  80.8 0.6 collective-permute-done.20.refs_9_.refs_17_
  81.4 1.3 %collective-permute-start.23 = (bf16[10,64,128]{2,1,0:T(8,128)(2,1)S(1)}, bf16[10,64,128]{2,1,0:T(8,128)(2,1)S(1)}, u32[]{:S(2)}, u32[]{:S(2)}) collective-permute-start(bf16[10,64,128]{2,1,0:T(8,128)(2,1)S(1)} %collective-permute-done.20.refs_9_.refs_17_), channel_id=1, source_target_pairs={{0,2},{2,0},{4,6},{6,4},{8,10},{10,8},{12,14},{14,12},{16,18},{18,... | collective-permute-start | bytes 491528 | tf_op jit(solution)/shard_map/ppermute | solution.py:490
  82.7 4.3 %last.1 = bf16[256,40,128]{2,1,0:T(8,128)(2,1)} custom-call(s32[1]{0:T(128)} %bitcast.s_ref, bf16[9,2,32,32,128]{4,3,2,1,0:T(8,128)(2,1)S(1)} %get-tuple-element.37.refs_0_.refs_24_, bf16[9,64,128]{2,1,0:T(8,128)(2,1)S(1)} %mix_back.1.refs_0_.refs_1_, bf16[9,64,128]{2,1,0:T(8,128)(2,1)S(1)} %collective-permute-done.7.refs_1_.refs_2_, ...), custom_call_target="tpu_custom_call" | custom-call | flops 5059999744 | bytes 15840000 | tf_op jit(solution)/shard_map/last/pallas_call | solution.py:673
  87.0 12.8 %outer.1 = (f32[8,2,32,32,144]{4,3,2,1,0:T(8,128)}, f32[32,32]{1,0:T(8,128)}, f32[1,32]{1,0:T(1,128)}) custom-call(bf16[9,64,128]{2,1,0:T(8,128)(2,1)S(1)} %collective-permute-done.1.refs_0_.refs_4_, bf16[9,64,128]{2,1,0:T(8,128)(2,1)S(1)} %collective-permute-done.10.refs_5_.refs_1_, bf16[9,64,128]{2,1,0:T(8,128)(2,1)S(1)} %collective-permute-done.2.refs_1_.refs_6_.refs_2_, ...), custom_call_target="tpu_custom_call" | custom-call | flops 14720000000 | bytes 46080000 | tf_op jit(solution)/shard_map/outer/pallas_call | solution.py:546
  (53 shorter events, 2.0 us)
Async XLA Ops:
  7.3 7.6 %collective-permute-start = (bf16[9,64,128]{2,1,0:T(8,128)(2,1)S(1)}, bf16[9,64,128]{2,1,0:T(8,128)(2,1)S(1)}, u32[]{:S(2)}, u32[]{:S(2)}) collective-permute-start(bf16[9,64,128]{2,1,0:T(8,128)(2,1)S(1)} %get-tuple-element.27), channel_id=1, source_target_pairs={{0,1},{1,0},{2,3},{3,2},{4,5},{5,4},{6,7},{7,6},{8,9},{9,8},{10,11... | collective-permute-start | bytes 442376 | tf_op jit(solution)/shard_map/ppermute | solution.py:486
  11.1 13.6 %slice-start = ((s8[5242880]{0:T(1024)(128)(4,1)}), s8[4194304]{0:T(1024)(128)(4,1)S(1)}, s32[]{:S(2)}) async-start(s8[5242880]{0:T(1024)(128)(4,1)} %bitcast.8), calls=%async_computation | async-start | bytes 8388608
  14.9 9.9 %slice-start.1 = ((s8[5242880]{0:T(1024)(128)(4,1)}), s8[1048576]{0:T(1024)(128)(4,1)S(1)}, s32[]{:S(2)}) async-start(s8[5242880]{0:T(1024)(128)(4,1)} %bitcast.8), calls=%async_computation.1 | async-start | bytes 2097152
  14.9 9.9 %copy-start.4 = (bf16[2,512,1024]{2,1,0:T(8,128)(2,1)S(1)}, bf16[2,512,1024]{2,1,0:T(8,128)(2,1)}, u32[]{:S(2)}) copy-start(bf16[2,512,1024]{2,1,0:T(8,128)(2,1)} %constant.16.clone.refs_4_.refs_3_) | copy-start | bytes 6291460
  14.9 9.9 %copy-start.5 = (bf16[2,1024,512]{2,1,0:T(8,128)(2,1)S(1)}, bf16[2,1024,512]{2,1,0:T(8,128)(2,1)}, u32[]{:S(2)}) copy-start(bf16[2,1024,512]{2,1,0:T(8,128)(2,1)} %constant.15.clone.line_hbm.refs_5_) | copy-start | bytes 6291460
  18.8 5.1 %collective-permute-start.5 = (bf16[9,64,128]{2,1,0:T(8,128)(2,1)S(1)}, bf16[9,64,128]{2,1,0:T(8,128)(2,1)S(1)}, u32[]{:S(2)}, u32[]{:S(2)}) collective-permute-start(bf16[9,64,128]{2,1,0:T(8,128)(2,1)S(1)} %get-tuple-element.30.refs_2_), channel_id=1, source_target_pairs={{0,1},{1,0},{2,3},{3,2},{4,5},{5,4},{6,7},{7,6},{8,9},{9,8},{10,11... | collective-permute-start | bytes 442376 | tf_op jit(solution)/shard_map/ppermute | solution.py:486
  18.9 5.0 %collective-permute-start.4 = (bf16[9,64,128]{2,1,0:T(8,128)(2,1)S(1)}, bf16[9,64,128]{2,1,0:T(8,128)(2,1)S(1)}, u32[]{:S(2)}, u32[]{:S(2)}) collective-permute-start(bf16[9,64,128]{2,1,0:T(8,128)(2,1)S(1)} %get-tuple-element.29.refs_12_), channel_id=1, source_target_pairs={{0,8},{2,10},{4,12},{6,14},{8,0},{10,2},{12,4},{14,6},{16,24},{18,... | collective-permute-start | bytes 442376 | tf_op jit(solution)/shard_map/ppermute | solution.py:490
  20.5 4.3 %collective-permute-start.3 = (bf16[9,64,128]{2,1,0:T(8,128)(2,1)S(1)}, bf16[9,64,128]{2,1,0:T(8,128)(2,1)S(1)}, u32[]{:S(2)}, u32[]{:S(2)}) collective-permute-start(bf16[9,64,128]{2,1,0:T(8,128)(2,1)S(1)} %get-tuple-element.29.refs_12_), channel_id=1, source_target_pairs={{0,4},{2,6},{4,0},{6,2},{8,12},{10,14},{12,8},{14,10},{16,20},{18,... | collective-permute-start | bytes 442376 | tf_op jit(solution)/shard_map/ppermute | solution.py:490
  21.7 14.1 %collective-permute-start.2 = (bf16[9,64,128]{2,1,0:T(8,128)(2,1)S(1)}, bf16[9,64,128]{2,1,0:T(8,128)(2,1)S(1)}, u32[]{:S(2)}, u32[]{:S(2)}) collective-permute-start(bf16[9,64,128]{2,1,0:T(8,128)(2,1)S(1)} %get-tuple-element.29.refs_12_), channel_id=1, source_target_pairs={{0,24},{2,26},{4,28},{6,30},{8,16},{10,18},{12,20},{14,22},{16,8},... | collective-permute-start | bytes 442376 | tf_op jit(solution)/shard_map/ppermute | solution.py:490
  31.0 5.1 %collective-permute-start.6 = (bf16[10,64,128]{2,1,0:T(8,128)(2,1)S(1)}, bf16[10,64,128]{2,1,0:T(8,128)(2,1)S(1)}, u32[]{:S(2)}, u32[]{:S(2)}) collective-permute-start(bf16[10,64,128]{2,1,0:T(8,128)(2,1)S(1)} %get-tuple-element.33), channel_id=1, source_target_pairs={{0,1},{1,0},{2,3},{3,2},{4,5},{5,4},{6,7},{7,6},{8,9},{9,8},{10,11... | collective-permute-start | bytes 491528 | tf_op jit(solution)/shard_map/ppermute | solution.py:486
  32.3 6.5 %collective-permute-start.1 = (bf16[9,64,128]{2,1,0:T(8,128)(2,1)S(1)}, bf16[9,64,128]{2,1,0:T(8,128)(2,1)S(1)}, u32[]{:S(2)}, u32[]{:S(2)}) collective-permute-start(bf16[9,64,128]{2,1,0:T(8,128)(2,1)S(1)} %get-tuple-element.29.refs_12_), channel_id=1, source_target_pairs={{0,16},{2,18},{4,20},{6,22},{8,24},{10,26},{12,28},{14,30},{16,0},... | collective-permute-start | bytes 442376 | tf_op jit(solution)/shard_map/ppermute | solution.py:490
  34.6 9.8 %collective-permute-start.16 = (bf16[9,64,128]{2,1,0:T(8,128)(2,1)S(1)}, bf16[9,64,128]{2,1,0:T(8,128)(2,1)S(1)}, u32[]{:S(2)}, u32[]{:S(2)}) collective-permute-start(bf16[9,64,128]{2,1,0:T(8,128)(2,1)S(1)} %collective-permute-done.4.refs_1_.refs_14_), channel_id=1, source_target_pairs={{0,4},{2,6},{4,0},{6,2},{8,12},{10,14},{12,8},{14,10},{16,20},{18,... | collective-permute-start | bytes 442376 | tf_op jit(solution)/shard_map/ppermute | solution.py:490
  35.8 8.5 %collective-permute-start.11 = (bf16[9,64,128]{2,1,0:T(8,128)(2,1)S(1)}, bf16[9,64,128]{2,1,0:T(8,128)(2,1)S(1)}, u32[]{:S(2)}, u32[]{:S(2)}) collective-permute-start(bf16[9,64,128]{2,1,0:T(8,128)(2,1)S(1)} %collective-permute-done.2.refs_1_.refs_6_.refs_2_), channel_id=1, source_target_pairs={{0,4},{2,6},{4,0},{6,2},{8,12},{10,14},{12,8},{14,10},{16,20},{18,... | collective-permute-start | bytes 442376 | tf_op jit(solution)/shard_map/ppermute | solution.py:490
  36.1 16.4 %collective-permute-start.18 = (bf16[10,64,128]{2,1,0:T(8,128)(2,1)S(1)}, bf16[10,64,128]{2,1,0:T(8,128)(2,1)S(1)}, u32[]{:S(2)}, u32[]{:S(2)}) collective-permute-start(bf16[10,64,128]{2,1,0:T(8,128)(2,1)S(1)} %get-tuple-element.36.refs_16_.refs_20_), channel_id=1, source_target_pairs={{0,8},{2,10},{4,12},{6,14},{8,0},{10,2},{12,4},{14,6},{16,24},{18,... | collective-permute-start | bytes 491528 | tf_op jit(solution)/shard_map/ppermute | solution.py:490
  38.7 7.1 %collective-permute-start.10 = (bf16[9,64,128]{2,1,0:T(8,128)(2,1)S(1)}, bf16[9,64,128]{2,1,0:T(8,128)(2,1)S(1)}, u32[]{:S(2)}, u32[]{:S(2)}) collective-permute-start(bf16[9,64,128]{2,1,0:T(8,128)(2,1)S(1)} %collective-permute-done.1.refs_0_.refs_4_), channel_id=1, source_target_pairs={{0,4},{2,6},{4,0},{6,2},{8,12},{10,14},{12,8},{14,10},{16,20},{18,... | collective-permute-start | bytes 442376 | tf_op jit(solution)/shard_map/ppermute | solution.py:490
  39.9 7.9 %collective-permute-start.14 = (bf16[9,64,128]{2,1,0:T(8,128)(2,1)S(1)}, bf16[9,64,128]{2,1,0:T(8,128)(2,1)S(1)}, u32[]{:S(2)}, u32[]{:S(2)}) collective-permute-start(bf16[9,64,128]{2,1,0:T(8,128)(2,1)S(1)} %collective-permute-done.2.refs_1_.refs_6_.refs_2_), channel_id=1, source_target_pairs={{0,2},{2,0},{4,6},{6,4},{8,10},{10,8},{12,14},{14,12},{16,18},{18,... | collective-permute-start | bytes 442376 | tf_op jit(solution)/shard_map/ppermute | solution.py:490
  44.4 4.9 %collective-permute-start.12 = (bf16[9,64,128]{2,1,0:T(8,128)(2,1)S(1)}, bf16[9,64,128]{2,1,0:T(8,128)(2,1)S(1)}, u32[]{:S(2)}, u32[]{:S(2)}) collective-permute-start(bf16[9,64,128]{2,1,0:T(8,128)(2,1)S(1)} %collective-permute-done.1.refs_0_.refs_4_), channel_id=1, source_target_pairs={{0,2},{2,0},{4,6},{6,4},{8,10},{10,8},{12,14},{14,12},{16,18},{18,... | collective-permute-start | bytes 442376 | tf_op jit(solution)/shard_map/ppermute | solution.py:490
  44.4 8.2 %collective-permute-start.15 = (bf16[9,64,128]{2,1,0:T(8,128)(2,1)S(1)}, bf16[9,64,128]{2,1,0:T(8,128)(2,1)S(1)}, u32[]{:S(2)}, u32[]{:S(2)}) collective-permute-start(bf16[9,64,128]{2,1,0:T(8,128)(2,1)S(1)} %collective-permute-done.11.refs_7_.refs_3_), channel_id=1, source_target_pairs={{0,2},{2,0},{4,6},{6,4},{8,10},{10,8},{12,14},{14,12},{16,18},{18,... | collective-permute-start | bytes 442376 | tf_op jit(solution)/shard_map/ppermute | solution.py:490
  45.8 11.0 %collective-permute-start.13 = (bf16[9,64,128]{2,1,0:T(8,128)(2,1)S(1)}, bf16[9,64,128]{2,1,0:T(8,128)(2,1)S(1)}, u32[]{:S(2)}, u32[]{:S(2)}) collective-permute-start(bf16[9,64,128]{2,1,0:T(8,128)(2,1)S(1)} %collective-permute-done.10.refs_5_.refs_1_), channel_id=1, source_target_pairs={{0,2},{2,0},{4,6},{6,4},{8,10},{10,8},{12,14},{14,12},{16,18},{18,... | collective-permute-start | bytes 442376 | tf_op jit(solution)/shard_map/ppermute | solution.py:490
  47.7 14.0 %collective-permute-start.17 = (bf16[10,64,128]{2,1,0:T(8,128)(2,1)S(1)}, bf16[10,64,128]{2,1,0:T(8,128)(2,1)S(1)}, u32[]{:S(2)}, u32[]{:S(2)}) collective-permute-start(bf16[10,64,128]{2,1,0:T(8,128)(2,1)S(1)} %get-tuple-element.36.refs_16_.refs_20_), channel_id=1, source_target_pairs={{0,4},{2,6},{4,0},{6,2},{8,12},{10,14},{12,8},{14,10},{16,20},{18,... | collective-permute-start | bytes 491528 | tf_op jit(solution)/shard_map/ppermute | solution.py:490
  49.2 12.5 %collective-permute-start.9 = (bf16[10,64,128]{2,1,0:T(8,128)(2,1)S(1)}, bf16[10,64,128]{2,1,0:T(8,128)(2,1)S(1)}, u32[]{:S(2)}, u32[]{:S(2)}) collective-permute-start(bf16[10,64,128]{2,1,0:T(8,128)(2,1)S(1)} %get-tuple-element.36.refs_16_.refs_20_), channel_id=1, source_target_pairs={{0,24},{2,26},{4,28},{6,30},{8,16},{10,18},{12,20},{14,22},{16,8},... | collective-permute-start | bytes 491528 | tf_op jit(solution)/shard_map/ppermute | solution.py:490
  52.5 13.7 %collective-permute-start.8 = (bf16[10,64,128]{2,1,0:T(8,128)(2,1)S(1)}, bf16[10,64,128]{2,1,0:T(8,128)(2,1)S(1)}, u32[]{:S(2)}, u32[]{:S(2)}) collective-permute-start(bf16[10,64,128]{2,1,0:T(8,128)(2,1)S(1)} %get-tuple-element.36.refs_16_.refs_20_), channel_id=1, source_target_pairs={{0,16},{2,18},{4,20},{6,22},{8,24},{10,26},{12,28},{14,30},{16,0},... | collective-permute-start | bytes 491528 | tf_op jit(solution)/shard_map/ppermute | solution.py:490
  52.6 13.7 %collective-permute-start.19 = (bf16[10,64,128]{2,1,0:T(8,128)(2,1)S(1)}, bf16[10,64,128]{2,1,0:T(8,128)(2,1)S(1)}, u32[]{:S(2)}, u32[]{:S(2)}) collective-permute-start(bf16[10,64,128]{2,1,0:T(8,128)(2,1)S(1)} %collective-permute-done.18.refs_18_.refs_22_), channel_id=1, source_target_pairs={{0,4},{2,6},{4,0},{6,2},{8,12},{10,14},{12,8},{14,10},{16,20},{18,... | collective-permute-start | bytes 491528 | tf_op jit(solution)/shard_map/ppermute | solution.py:490
  56.8 4.9 %collective-permute-start.7 = (bf16[9,64,128]{2,1,0:T(8,128)(2,1)S(1)}, bf16[9,64,128]{2,1,0:T(8,128)(2,1)S(1)}, u32[]{:S(2)}, u32[]{:S(2)}) collective-permute-start(bf16[9,64,128]{2,1,0:T(8,128)(2,1)S(1)} %mix_back.1.refs_0_.refs_1_), channel_id=1, source_target_pairs={{0,1},{1,0},{2,3},{3,2},{4,5},{5,4},{6,7},{7,6},{8,9},{9,8},{10,11... | collective-permute-start | bytes 442376 | tf_op jit(solution)/shard_map/ppermute | solution.py:486
  71.3 15.7 %collective-permute-start.26 = (bf16[9,2,32,32,128]{4,3,2,1,0:T(8,128)(2,1)S(1)}, bf16[9,2,32,32,128]{4,3,2,1,0:T(8,128)(2,1)S(1)}, u32[]{:S(2)}, u32[]{:S(2)}) collective-permute-start(bf16[9,2,32,32,128]{4,3,2,1,0:T(8,128)(2,1)S(1)} %get-tuple-element.37.refs_0_.refs_24_), channel_id=1, source_target_pairs={{0,2},{2,0},{4,6},{6,4},{8,10},{10,8},{12,14},{14,12},{16,18},{18,... | collective-permute-start | bytes 14155784 | tf_op jit(solution)/shard_map/ppermute | solution.py:490
  72.5 7.8 %collective-permute-start.24 = (bf16[10,64,128]{2,1,0:T(8,128)(2,1)S(1)}, bf16[10,64,128]{2,1,0:T(8,128)(2,1)S(1)}, u32[]{:S(2)}, u32[]{:S(2)}) collective-permute-start(bf16[10,64,128]{2,1,0:T(8,128)(2,1)S(1)} %collective-permute-done.9.refs_3_.refs_10_.refs_18_), channel_id=1, source_target_pairs={{0,2},{2,0},{4,6},{6,4},{8,10},{10,8},{12,14},{14,12},{16,18},{18,... | collective-permute-start | bytes 491528 | tf_op jit(solution)/shard_map/ppermute | solution.py:490
  72.6 8.1 %collective-permute-start.21 = (bf16[10,64,128]{2,1,0:T(8,128)(2,1)S(1)}, bf16[10,64,128]{2,1,0:T(8,128)(2,1)S(1)}, u32[]{:S(2)}, u32[]{:S(2)}) collective-permute-start(bf16[10,64,128]{2,1,0:T(8,128)(2,1)S(1)} %collective-permute-done.9.refs_3_.refs_10_.refs_18_), channel_id=1, source_target_pairs={{0,4},{2,6},{4,0},{6,2},{8,12},{10,14},{12,8},{14,10},{16,20},{18,... | collective-permute-start | bytes 491528 | tf_op jit(solution)/shard_map/ppermute | solution.py:490
  72.6 8.8 %collective-permute-start.20 = (bf16[10,64,128]{2,1,0:T(8,128)(2,1)S(1)}, bf16[10,64,128]{2,1,0:T(8,128)(2,1)S(1)}, u32[]{:S(2)}, u32[]{:S(2)}) collective-permute-start(bf16[10,64,128]{2,1,0:T(8,128)(2,1)S(1)} %collective-permute-done.8.refs_2_.refs_8_.refs_16_), channel_id=1, source_target_pairs={{0,4},{2,6},{4,0},{6,2},{8,12},{10,14},{12,8},{14,10},{16,20},{18,... | collective-permute-start | bytes 491528 | tf_op jit(solution)/shard_map/ppermute | solution.py:490
  74.0 13.0 %collective-permute-start.22 = (bf16[10,64,128]{2,1,0:T(8,128)(2,1)S(1)}, bf16[10,64,128]{2,1,0:T(8,128)(2,1)S(1)}, u32[]{:S(2)}, u32[]{:S(2)}) collective-permute-start(bf16[10,64,128]{2,1,0:T(8,128)(2,1)S(1)} %collective-permute-done.8.refs_2_.refs_8_.refs_16_), channel_id=1, source_target_pairs={{0,2},{2,0},{4,6},{6,4},{8,10},{10,8},{12,14},{14,12},{16,18},{18,... | collective-permute-start | bytes 491528 | tf_op jit(solution)/shard_map/ppermute | solution.py:490
  80.2 6.8 %collective-permute-start.27 = (f32[32,128]{1,0:T(8,128)S(1)}, f32[32,128]{1,0:T(8,128)S(1)}, u32[]{:S(2)}, u32[]{:S(2)}) collective-permute-start(f32[32,128]{1,0:T(8,128)S(1)} %get-tuple-element.40.refs_26_), channel_id=1, source_target_pairs={{0,2},{2,0},{4,6},{6,4},{8,10},{10,8},{12,14},{14,12},{16,18},{18,... | collective-permute-start | bytes 49160 | tf_op jit(solution)/shard_map/ppermute | solution.py:490
  80.6 6.4 %collective-permute-start.25 = (bf16[10,64,128]{2,1,0:T(8,128)(2,1)S(1)}, bf16[10,64,128]{2,1,0:T(8,128)(2,1)S(1)}, u32[]{:S(2)}, u32[]{:S(2)}) collective-permute-start(bf16[10,64,128]{2,1,0:T(8,128)(2,1)S(1)} %collective-permute-done.21.refs_11_.refs_19_), channel_id=1, source_target_pairs={{0,2},{2,0},{4,6},{6,4},{8,10},{10,8},{12,14},{14,12},{16,18},{18,... | collective-permute-start | bytes 491528 | tf_op jit(solution)/shard_map/ppermute | solution.py:490
  81.4 5.6 %collective-permute-start.23 = (bf16[10,64,128]{2,1,0:T(8,128)(2,1)S(1)}, bf16[10,64,128]{2,1,0:T(8,128)(2,1)S(1)}, u32[]{:S(2)}, u32[]{:S(2)}) collective-permute-start(bf16[10,64,128]{2,1,0:T(8,128)(2,1)S(1)} %collective-permute-done.20.refs_9_.refs_17_), channel_id=1, source_target_pairs={{0,2},{2,0},{4,6},{6,4},{8,10},{10,8},{12,14},{14,12},{16,18},{18,... | collective-permute-start | bytes 491528 | tf_op jit(solution)/shard_map/ppermute | solution.py:490
  (5 other events, 37.8 us)

commit v3 on v2

--- a/solution.py
+++ b/solution.py
@@ -358,13 +358,13 @@
         copy.wait()
 
 
-def load_cells(u_refs, g_refs, u_all, g_all, factor):
+def load_cells(u_refs, g_refs, blk, u_all, g_all, factor):
     chans = g_all.shape[2]
     for b, (u_ref, g_ref) in enumerate(zip(u_refs, g_refs, strict=True)):
-        g_real = g_ref[0, :chans].astype(F32)
-        g_imag = g_ref[0, chans:].astype(F32)
-        u_real = u_ref[0, :chans].astype(F32) * factor
-        u_imag = u_ref[0, chans:].astype(F32) * factor
+        g_real = g_ref[blk, :chans].astype(F32)
+        g_imag = g_ref[blk, chans:].astype(F32)
+        u_real = u_ref[blk, :chans].astype(F32) * factor
+        u_imag = u_ref[blk, chans:].astype(F32) * factor
         g_all[b, 0] = g_real + g_imag
         g_all[b, 1] = g_real
         g_all[b, 2] = g_imag
@@ -387,50 +387,51 @@
     return [(part[0] - part[2], part[0] - part[1]) for part in sums]
 
 
-def tag_sum(refs, chans):
+def tag_sum(refs, at, chans):
     total = jnp.zeros((chans, LANES), F32)
     for ref in refs:
-        total = total + (ref[0, :chans].astype(F32) + ref[0, chans:].astype(F32))
+        total = total + (ref[at, :chans].astype(F32) + ref[at, chans:].astype(F32))
     return total
 
 
 def early_kernel(cells, ties, factor, *refs):
     refs = refs[ties:]
-    u_refs, g_refs, c_refs = refs[:cells], refs[cells : 2 * cells], refs[2 * cells : 3 * cells]
-    out_ref, chan_ref, u_all, g_all = refs[3 * cells :]
+    u_refs, g_refs = refs[:cells], refs[cells : 2 * cells]
+    out_ref, chan_ref, u_all, g_all = refs[2 * cells :]
     chans = g_all.shape[2]
-    load_cells(u_refs, g_refs, u_all, g_all, factor)
-
-    @pl.when(pl.program_id(0) == 0)
-    def _():
-        chan_ref[...] = tag_sum(c_refs, chans)
-
-    @pl.loop(0, chans, step=TOGETHER)
-    def _(i):
-        for k, parts in enumerate(products(u_all, g_all, i)):
-            for r, part in enumerate(parts):
-                out_ref[0, r, i + k] = part.astype(BF16)
+    chan_ref[...] = tag_sum(g_refs, out_ref.shape[0], chans)
+
+    @pl.loop(0, out_ref.shape[0])
+    def _(blk):
+        load_cells(u_refs, g_refs, blk, u_all, g_all, factor)
+
+        @pl.loop(0, chans, step=TOGETHER)
+        def _(i):
+            for k, parts in enumerate(products(u_all, g_all, i)):
+                for r, part in enumerate(parts):
+                    out_ref[blk, r, i + k] = part.astype(BF16)
 
 
 def outer_kernel(rest, cells, sums, factor, norm, *refs):
-    u_refs, g_refs, c_refs = refs[:cells], refs[cells : 2 * cells], refs[2 * cells : 3 * cells]
-    refs = refs[3 * cells :]
+    u_refs, g_refs, refs = refs[:cells], refs[cells : 2 * cells], refs[2 * cells :]
     sum_refs, sum_chans, refs = refs[:sums], refs[sums : 2 * sums], refs[2 * sums :]
     out_ref, chan_ref, bias_ref, u_all, g_all, tail_ref = refs
     step = pl.program_id(0)
+    own = pl.num_programs(0) - 1
+    blk = jnp.where(step == 0, own, step - 1)
     chans = g_all.shape[2]
-    load_cells(u_refs, g_refs, u_all, g_all, factor)
+    load_cells(u_refs, g_refs, blk, u_all, g_all, factor)
 
     def totals(i):
         for k, parts in enumerate(products(u_all, g_all, i)):
             for r, part in enumerate(parts):
                 for ref in sum_refs:
-                    part = part + ref[0, r, i + k].astype(F32)
+                    part = part + ref[blk, r, i + k].astype(F32)
                 yield r, i + k, part
 
     @pl.when(step == 0)
     def _():
-        chan = tag_sum(c_refs, chans)
+        chan = tag_sum(g_refs, own + 1, chans)
         for ref in sum_chans:
             chan = chan + ref[...]
         chan = chan * norm
@@ -439,7 +440,7 @@
         bias = jnp.sum(jnp.where(same, chan[:, chans : chans + 1], 0.0), axis=0, keepdims=True)
         bias_ref[...] = bias[:, :chans]
 
-        @pl.loop(0, chans, step=TOGETHER)
+        @pl.loop(0, chans, step=TOGETHER, unroll=2)
         def _(i):
             for r, at, part in totals(i):
                 tail_ref[r, at] = part
@@ -448,7 +449,7 @@
     def _():
         shift = lax.rem(LANES - (step - 1) * rest, LANES)
 
-        @pl.loop(0, chans, step=TOGETHER)
+        @pl.loop(0, chans, step=TOGETHER, unroll=2)
         def _(i):
             for r, at, part in totals(i):
                 out_ref[0, r, at, :, :LANES] = part
@@ -510,43 +511,25 @@
 def early_gradient(all_u, all_g, ties, own, cell_norm):
     cells = len(all_u)
     chans = all_u[0].shape[1] // 2
-    block = (1,) + all_u[0].shape[1:]
-    one = pl.BlockSpec(block, lambda i: (i, 0, 0))
-    tag = pl.BlockSpec(block, lambda i: (own + 1, 0, 0))
-    return pl.pallas_call(
+    return call(
         functools.partial(early_kernel, cells, len(ties), cell_norm),
-        grid=(own + 1,),
-        in_specs=there(len(ties)) + [one] * (2 * cells) + [tag] * cells,
-        out_specs=[
-            pl.BlockSpec((1, 2, chans, chans, LANES), lambda i: (i, 0, 0, 0, 0)),
-            pl.BlockSpec((chans, LANES), lambda i: (0, 0)),
-        ],
-        out_shape=[
-            jax.ShapeDtypeStruct((own + 1, 2, chans, chans, LANES), BF16),
-            jax.ShapeDtypeStruct((chans, LANES), F32),
-        ],
-        scratch_shapes=scratch_cells(cells, chans),
-        compiler_params=pltpu.CompilerParams(vmem_limit_bytes=16 * 1024 * 1024),
-        cost_estimate=about(4.8),
-        name="early",
-    )(*ties, *all_u, *all_g, *all_g)
+        "early",
+        4.8,
+        there(len(ties)) + here(2 * cells),
+        [((own + 1, 2, chans, chans, LANES), BF16), ((chans, LANES), F32)],
+        scratch_cells(cells, chans),
+    )(*ties, *all_u, *all_g)
 
 
 def weight_gradient(all_u, all_g, sums, weight_shape, norms):
     own, _, chans, _, pairs = weight_shape
     cell_norm, voxel_norm = norms
-    block = (1,) + all_u[0].shape[1:]
     cells = len(all_u)
-    at = lambda i: jnp.where(i == 0, own, i - 1)
-    one = pl.BlockSpec(block, lambda i: (at(i), 0, 0))
-    tag = pl.BlockSpec(block, lambda i: (own + 1, 0, 0))
-    add = pl.BlockSpec((1, 2, chans, chans, LANES), lambda i: (at(i), 0, 0, 0, 0))
-    add_chan = pl.BlockSpec((chans, LANES), lambda i: (0, 0))
     half = len(sums) // 2
     return pl.pallas_call(
         functools.partial(outer_kernel, pairs - LANES, cells, half, cell_norm, voxel_norm),
         grid=(own + 1,),
-        in_specs=[one] * (2 * cells) + [tag] * cells + [add] * half + [add_chan] * half,
+        in_specs=here(2 * cells + 2 * half),
         out_specs=[
             pl.BlockSpec((1,) + weight_shape[1:], lambda i: (jnp.maximum(i - 1, 0), 0, 0, 0, 0)),
             pl.BlockSpec((chans, chans), lambda i: (0, 0)),
@@ -561,7 +544,7 @@
         compiler_params=pltpu.CompilerParams(vmem_limit_bytes=20 * 1024 * 1024),
         cost_estimate=about(12.8),
         name="outer",
-    )(*all_u, *all_g, *all_g, *sums)
+    )(*all_u, *all_g, *sums)
 
 
 def shards(count, cell_count, fields, cotangent, spectral_weight, channel_weight, channel_bias):

time: 100 us -> 99.4 us (level)
  transfers between devices with their start and end apart: 28 -> 28, of which waited for: 6 -> 6; matrix products, arithmetic and copies ran while one was open for 0% -> 0% of each run, Pallas kernels for 18% -> 19%
where the time goes in v3:
time: 99.4 us; the launch traced here: 99.3 us
  Pallas kernels  46.2 us (46%)
  starting transfers between devices  32.3 us (32%)
  waiting for transfers between devices  18.1 us (18%)
  local copies, waits for them, and re-layouts  1.78 us (2%)
    ppermute x24, starting transfers between devices, swap(): return lax.ppermute(array, 'dp', [(i, i ^ bit) for i in range(count)])  28.4 us
    ppermute x24, waiting for transfers between devices, swap(): return lax.ppermute(array, 'dp', [(i, i ^ bit) for i in range(count)])  13.7 us
    pallas_call x1, Pallas kernels, weight_gradient(): pl.pallas_call(functools.partial(outer_kernel, pairs - LANES, cells, half...  12.3 us
    pallas_call x1, Pallas kernels, shards(): call(functools.partial(forward_kernel, own, rest, count), 'forward', 4.3,...  6.61 us
    pallas_call x1, Pallas kernels, shards(): call(functools.partial(middle_kernel, own, rest, count, planes, len(ties)...  6.2 us
    pallas_call x1, Pallas kernels, early_gradient(): call(functools.partial(early_kernel, cells, len(ties), cell_norm), 'early...  4.99 us
    ppermute x4, waiting for transfers between devices, send(): lax.ppermute(array, axis, [(i, (i + shift) % count) for i in range(count)])  4.46 us
    pallas_call x1, Pallas kernels, shards(): call(functools.partial(last_kernel, own, rest, count, block, len(ties)),...  4.29 us
  transfers between devices with their start and end apart: 28, of which 6 were waited for; matrix products, arithmetic and copies ran while one was open for 0% of the time, Pallas kernels for 19%

profile of v3, /device:TPU:1, one launch (start us, length us, event | category | flops | bytes accessed | tf_op | source)
XLA Modules:
  0.0 99.3 jit_solution(14671090133451378288)
XLA Ops:
  0.7 6.6 %forward.1 = (bf16[256,5120]{1,0:T(8,128)(2,1)}, f32[9,64,128]{2,1,0:T(8,128)S(1)}, bf16[9,64,128]{2,1,0:T(8,128)(2,1)S(1)}) custom-call(s32[1]{0:T(128)} %bitcast.s_ref, bf16[256,40,128]{2,1,0:T(8,128)(2,1)} %bitcast.10, bf16[5120,512]{1,0:T(8,128)(2,1)} %constant.14.clone.basis_hbm.refs_10_.refs_7_, bf16[2,1024,512]{2,1,0:T(8,128)(2,1)} %constant.15.clone.line_hbm.refs_5_), custom_call_target="tpu_custom_call" | custom-call | flops 4944999936 | bytes 15480000 | tf_op jit(solution)/shard_map/forward/pallas_call | solution.py:576
  7.3 2.1 %collective-permute-start = (bf16[9,64,128]{2,1,0:T(8,128)(2,1)S(1)}, bf16[9,64,128]{2,1,0:T(8,128)(2,1)S(1)}, u32[]{:S(2)}, u32[]{:S(2)}) collective-permute-start(bf16[9,64,128]{2,1,0:T(8,128)(2,1)S(1)} %get-tuple-element.27), channel_id=1, source_target_pairs={{0,1},{1,0},{2,3},{3,2},{4,5},{5,4},{6,7},{7,6},{8,9},{9,8},{10,11... | collective-permute-start | bytes 442376 | tf_op jit(solution)/shard_map/ppermute | solution.py:487
  9.4 1.7 %copy-done.1 = bf16[256,5120]{1,0:T(8,128)(2,1)S(1)} copy-done((bf16[256,5120]{1,0:T(8,128)(2,1)S(1)}, bf16[256,5120]{1,0:T(8,128)(2,1)}, u32[]{:S(2)}) %copy-start.1) | copy-done | bytes 2621464
  11.1 3.7 %prepare.1 = (bf16[256,5120]{1,0:T(8,128)(2,1)S(1)}, f32[256,5120]{1,0:T(8,128)S(1)}, bf16[256,256]{1,0:T(8,128)(2,1)S(1)}, bf16[8,2,32,32,144]{4,3,2,1,0:T(8,128)(2,1)S(1)}) custom-call(bf16[256,40,128]{2,1,0:T(8,128)(2,1)S(1)} %bitcast.6, bf16[8,2,32,32,144]{4,3,2,1,0:T(8,128)(2,1)} %weight_hbm.1, bf16[256,5120]{1,0:T(8,128)(2,1)S(1)} %copy-done.1, ...), custom_call_target="tpu_custom_call" | custom-call | flops 2875000064 | bytes 9000000 | tf_op jit(solution)/shard_map/prepare/pallas_call | solution.py:593
  14.9 3.9 %mix.1 = (bf16[9,64,128]{2,1,0:T(8,128)(2,1)S(1)}, bf16[9,64,128]{2,1,0:T(8,128)(2,1)S(1)}) custom-call(bf16[256,5120]{1,0:T(8,128)(2,1)S(1)} %get-tuple-element.25.refs_0_.refs_8_, f32[9,64,128]{2,1,0:T(8,128)S(1)} %get-tuple-element.26.refs_1_, bf16[9,64,128]{2,1,0:T(8,128)(2,1)S(1)} %collective-permute-done.refs_2_, ...), custom_call_target="tpu_custom_call" | custom-call | flops 4485000192 | bytes 14040000 | tf_op jit(solution)/shard_map/mix/pallas_call | solution.py:608
  18.9 1.5 %collective-permute-start.4 = (bf16[9,64,128]{2,1,0:T(8,128)(2,1)S(1)}, bf16[9,64,128]{2,1,0:T(8,128)(2,1)S(1)}, u32[]{:S(2)}, u32[]{:S(2)}) collective-permute-start(bf16[9,64,128]{2,1,0:T(8,128)(2,1)S(1)} %get-tuple-element.29.refs_12_), channel_id=1, source_target_pairs={{0,8},{2,10},{4,12},{6,14},{8,0},{10,2},{12,4},{14,6},{16,24},{18,... | collective-permute-start | bytes 442376 | tf_op jit(solution)/shard_map/ppermute | solution.py:491
  20.5 1.2 %collective-permute-start.3 = (bf16[9,64,128]{2,1,0:T(8,128)(2,1)S(1)}, bf16[9,64,128]{2,1,0:T(8,128)(2,1)S(1)}, u32[]{:S(2)}, u32[]{:S(2)}) collective-permute-start(bf16[9,64,128]{2,1,0:T(8,128)(2,1)S(1)} %get-tuple-element.29.refs_12_), channel_id=1, source_target_pairs={{0,4},{2,6},{4,0},{6,2},{8,12},{10,14},{12,8},{14,10},{16,20},{18,... | collective-permute-start | bytes 442376 | tf_op jit(solution)/shard_map/ppermute | solution.py:491
  21.7 2.2 %collective-permute-start.2 = (bf16[9,64,128]{2,1,0:T(8,128)(2,1)S(1)}, bf16[9,64,128]{2,1,0:T(8,128)(2,1)S(1)}, u32[]{:S(2)}, u32[]{:S(2)}) collective-permute-start(bf16[9,64,128]{2,1,0:T(8,128)(2,1)S(1)} %get-tuple-element.29.refs_12_), channel_id=1, source_target_pairs={{0,24},{2,26},{4,28},{6,30},{8,16},{10,18},{12,20},{14,22},{16,8},... | collective-permute-start | bytes 442376 | tf_op jit(solution)/shard_map/ppermute | solution.py:491
  23.9 0.8 collective-permute-done.3.refs_0_.refs_13_
  24.8 6.2 %middle.1 = (bf16[256,5120]{1,0:T(8,128)(2,1)S(1)}, f32[32,128]{1,0:T(8,128)S(1)}, f32[9,64,128]{2,1,0:T(8,128)S(1)}, bf16[10,64,128]{2,1,0:T(8,128)(2,1)S(1)}) custom-call(s32[1]{0:T(128)} %bitcast.s_ref, bf16[9,64,128]{2,1,0:T(8,128)(2,1)S(1)} %collective-permute-done.3.refs_0_.refs_13_, bf16[9,64,128]{2,1,0:T(8,128)(2,1)S(1)} %collective-permute-done.4.refs_1_.refs_14_, ...), custom_call_target="tpu_custom_call" | custom-call | flops 7245000192 | bytes 22680000 | tf_op jit(solution)/shard_map/middle/pallas_call | solution.py:621
  31.0 1.3 %collective-permute-start.6 = (bf16[10,64,128]{2,1,0:T(8,128)(2,1)S(1)}, bf16[10,64,128]{2,1,0:T(8,128)(2,1)S(1)}, u32[]{:S(2)}, u32[]{:S(2)}) collective-permute-start(bf16[10,64,128]{2,1,0:T(8,128)(2,1)S(1)} %get-tuple-element.33), channel_id=1, source_target_pairs={{0,1},{1,0},{2,3},{3,2},{4,5},{5,4},{6,7},{7,6},{8,9},{9,8},{10,11... | collective-permute-start | bytes 491528 | tf_op jit(solution)/shard_map/ppermute | solution.py:487
  32.3 2.3 %collective-permute-start.1 = (bf16[9,64,128]{2,1,0:T(8,128)(2,1)S(1)}, bf16[9,64,128]{2,1,0:T(8,128)(2,1)S(1)}, u32[]{:S(2)}, u32[]{:S(2)}) collective-permute-start(bf16[9,64,128]{2,1,0:T(8,128)(2,1)S(1)} %get-tuple-element.29.refs_12_), channel_id=1, source_target_pairs={{0,16},{2,18},{4,20},{6,22},{8,24},{10,26},{12,28},{14,30},{16,0},... | collective-permute-start | bytes 442376 | tf_op jit(solution)/shard_map/ppermute | solution.py:491
  34.6 1.2 %collective-permute-start.16 = (bf16[9,64,128]{2,1,0:T(8,128)(2,1)S(1)}, bf16[9,64,128]{2,1,0:T(8,128)(2,1)S(1)}, u32[]{:S(2)}, u32[]{:S(2)}) collective-permute-start(bf16[9,64,128]{2,1,0:T(8,128)(2,1)S(1)} %collective-permute-done.4.refs_1_.refs_14_), channel_id=1, source_target_pairs={{0,4},{2,6},{4,0},{6,2},{8,12},{10,14},{12,8},{14,10},{16,20},{18,... | collective-permute-start | bytes 442376 | tf_op jit(solution)/shard_map/ppermute | solution.py:491
  36.3 2.4 %collective-permute-done.1.refs_0_.refs_4_ = bf16[9,64,128]{2,1,0:T(8,128)(2,1)S(1)} collective-permute-done((bf16[9,64,128]{2,1,0:T(8,128)(2,1)S(1)}, bf16[9,64,128]{2,1,0:T(8,128)(2,1)S(1)}, u32[]{:S(2)}, u32[]{:S(2)}) %collective-permute-start.1) | collective-permute-done | bytes 147488 | tf_op jit(solution)/shard_map/ppermute | solution.py:491
  38.7 1.1 %collective-permute-start.10 = (bf16[9,64,128]{2,1,0:T(8,128)(2,1)S(1)}, bf16[9,64,128]{2,1,0:T(8,128)(2,1)S(1)}, u32[]{:S(2)}, u32[]{:S(2)}) collective-permute-start(bf16[9,64,128]{2,1,0:T(8,128)(2,1)S(1)} %collective-permute-done.1.refs_0_.refs_4_), channel_id=1, source_target_pairs={{0,4},{2,6},{4,0},{6,2},{8,12},{10,14},{12,8},{14,10},{16,20},{18,... | collective-permute-start | bytes 442376 | tf_op jit(solution)/shard_map/ppermute | solution.py:491
  39.9 4.5 %collective-permute-start.14 = (bf16[9,64,128]{2,1,0:T(8,128)(2,1)S(1)}, bf16[9,64,128]{2,1,0:T(8,128)(2,1)S(1)}, u32[]{:S(2)}, u32[]{:S(2)}) collective-permute-start(bf16[9,64,128]{2,1,0:T(8,128)(2,1)S(1)} %collective-permute-done.2.refs_1_.refs_6_.refs_2_), channel_id=1, source_target_pairs={{0,2},{2,0},{4,6},{6,4},{8,10},{10,8},{12,14},{14,12},{16,18},{18,... | collective-permute-start | bytes 442376 | tf_op jit(solution)/shard_map/ppermute | solution.py:491
  44.4 1.4 %collective-permute-start.15 = (bf16[9,64,128]{2,1,0:T(8,128)(2,1)S(1)}, bf16[9,64,128]{2,1,0:T(8,128)(2,1)S(1)}, u32[]{:S(2)}, u32[]{:S(2)}) collective-permute-start(bf16[9,64,128]{2,1,0:T(8,128)(2,1)S(1)} %collective-permute-done.11.refs_7_.refs_3_), channel_id=1, source_target_pairs={{0,2},{2,0},{4,6},{6,4},{8,10},{10,8},{12,14},{14,12},{16,18},{18,... | collective-permute-start | bytes 442376 | tf_op jit(solution)/shard_map/ppermute | solution.py:491
  45.8 1.9 %collective-permute-start.13 = (bf16[9,64,128]{2,1,0:T(8,128)(2,1)S(1)}, bf16[9,64,128]{2,1,0:T(8,128)(2,1)S(1)}, u32[]{:S(2)}, u32[]{:S(2)}) collective-permute-start(bf16[9,64,128]{2,1,0:T(8,128)(2,1)S(1)} %collective-permute-done.10.refs_5_.refs_1_), channel_id=1, source_target_pairs={{0,2},{2,0},{4,6},{6,4},{8,10},{10,8},{12,14},{14,12},{16,18},{18,... | collective-permute-start | bytes 442376 | tf_op jit(solution)/shard_map/ppermute | solution.py:491
  47.7 1.5 %collective-permute-start.17 = (bf16[10,64,128]{2,1,0:T(8,128)(2,1)S(1)}, bf16[10,64,128]{2,1,0:T(8,128)(2,1)S(1)}, u32[]{:S(2)}, u32[]{:S(2)}) collective-permute-start(bf16[10,64,128]{2,1,0:T(8,128)(2,1)S(1)} %get-tuple-element.36.refs_16_), channel_id=1, source_target_pairs={{0,4},{2,6},{4,0},{6,2},{8,12},{10,14},{12,8},{14,10},{16,20},{18,... | collective-permute-start | bytes 491528 | tf_op jit(solution)/shard_map/ppermute | solution.py:491
  49.2 3.3 %collective-permute-start.9 = (bf16[10,64,128]{2,1,0:T(8,128)(2,1)S(1)}, bf16[10,64,128]{2,1,0:T(8,128)(2,1)S(1)}, u32[]{:S(2)}, u32[]{:S(2)}) collective-permute-start(bf16[10,64,128]{2,1,0:T(8,128)(2,1)S(1)} %get-tuple-element.36.refs_16_), channel_id=1, source_target_pairs={{0,24},{2,26},{4,28},{6,30},{8,16},{10,18},{12,20},{14,22},{16,8},... | collective-permute-start | bytes 491528 | tf_op jit(solution)/shard_map/ppermute | solution.py:491
  52.7 4.1 %mix_back.1.refs_0_.refs_1_ = bf16[9,64,128]{2,1,0:T(8,128)(2,1)S(1)} custom-call(bf16[9,64,128]{2,1,0:T(8,128)(2,1)S(1)} %collective-permute-done.1.refs_0_.refs_4_, bf16[9,64,128]{2,1,0:T(8,128)(2,1)S(1)} %collective-permute-done.2.refs_1_.refs_6_.refs_2_, f32[9,64,128]{2,1,0:T(8,128)S(1)} %get-tuple-element.35.refs_2_, ...), custom_call_target="tpu_custom_call" | custom-call | flops 4714999808 | bytes 14759999 | tf_op jit(solution)/shard_map/mix_back/pallas_call | solution.py:635
  57.3 4.4 %collective-permute-done.7.refs_1_.refs_2_ = bf16[9,64,128]{2,1,0:T(8,128)(2,1)S(1)} collective-permute-done((bf16[9,64,128]{2,1,0:T(8,128)(2,1)S(1)}, bf16[9,64,128]{2,1,0:T(8,128)(2,1)S(1)}, u32[]{:S(2)}, u32[]{:S(2)}) %collective-permute-start.7) | collective-permute-done | bytes 147488 | tf_op jit(solution)/shard_map/ppermute | solution.py:487
  61.8 4.5 %collective-permute-done.8.refs_2_.refs_8_ = bf16[10,64,128]{2,1,0:T(8,128)(2,1)S(1)} collective-permute-done((bf16[10,64,128]{2,1,0:T(8,128)(2,1)S(1)}, bf16[10,64,128]{2,1,0:T(8,128)(2,1)S(1)}, u32[]{:S(2)}, u32[]{:S(2)}) %collective-permute-start.8) | collective-permute-done | bytes 163872 | tf_op jit(solution)/shard_map/ppermute | solution.py:491
  66.3 5.0 %early.1 = (bf16[9,2,32,32,128]{4,3,2,1,0:T(8,128)(2,1)S(1)}, f32[32,128]{1,0:T(8,128)S(1)}) custom-call(bf16[9,64,128]{2,1,0:T(8,128)(2,1)S(1)} %mix_back.1.refs_0_.refs_1_, bf16[9,64,128]{2,1,0:T(8,128)(2,1)S(1)} %collective-permute-done.7.refs_1_.refs_2_, bf16[10,64,128]{2,1,0:T(8,128)(2,1)S(1)} %collective-permute-done.8.refs_2_.refs_8_, ...), custom_call_target="tpu_custom_call" | custom-call | flops 5520000000 | bytes 17280000 | tf_op jit(solution)/shard_map/early/pallas_call | solution.py:514
  71.3 1.2 %collective-permute-start.26 = (bf16[9,2,32,32,128]{4,3,2,1,0:T(8,128)(2,1)S(1)}, bf16[9,2,32,32,128]{4,3,2,1,0:T(8,128)(2,1)S(1)}, u32[]{:S(2)}, u32[]{:S(2)}) collective-permute-start(bf16[9,2,32,32,128]{4,3,2,1,0:T(8,128)(2,1)S(1)} %get-tuple-element.37.refs_0_.refs_16_), channel_id=1, source_target_pairs={{0,2},{2,0},{4,6},{6,4},{8,10},{10,8},{12,14},{14,12},{16,18},{18,... | collective-permute-start | bytes 14155784 | tf_op jit(solution)/shard_map/ppermute | solution.py:491
  72.6 1.4 %collective-permute-start.20 = (bf16[10,64,128]{2,1,0:T(8,128)(2,1)S(1)}, bf16[10,64,128]{2,1,0:T(8,128)(2,1)S(1)}, u32[]{:S(2)}, u32[]{:S(2)}) collective-permute-start(bf16[10,64,128]{2,1,0:T(8,128)(2,1)S(1)} %collective-permute-done.8.refs_2_.refs_8_), channel_id=1, source_target_pairs={{0,4},{2,6},{4,0},{6,2},{8,12},{10,14},{12,8},{14,10},{16,20},{18,... | collective-permute-start | bytes 491528 | tf_op jit(solution)/shard_map/ppermute | solution.py:491
  74.0 1.0 collective-permute-start.22
  75.0 5.2 %collective-permute-done.24.refs_14_ = bf16[10,64,128]{2,1,0:T(8,128)(2,1)S(1)} collective-permute-done((bf16[10,64,128]{2,1,0:T(8,128)(2,1)S(1)}, bf16[10,64,128]{2,1,0:T(8,128)(2,1)S(1)}, u32[]{:S(2)}, u32[]{:S(2)}) %collective-permute-start.24) | collective-permute-done | bytes 163872 | tf_op jit(solution)/shard_map/ppermute | solution.py:491
  80.7 0.6 collective-permute-done.20.refs_9_
  81.4 1.3 %collective-permute-start.23 = (bf16[10,64,128]{2,1,0:T(8,128)(2,1)S(1)}, bf16[10,64,128]{2,1,0:T(8,128)(2,1)S(1)}, u32[]{:S(2)}, u32[]{:S(2)}) collective-permute-start(bf16[10,64,128]{2,1,0:T(8,128)(2,1)S(1)} %collective-permute-done.20.refs_9_), channel_id=1, source_target_pairs={{0,2},{2,0},{4,6},{6,4},{8,10},{10,8},{12,14},{14,12},{16,18},{18,... | collective-permute-start | bytes 491528 | tf_op jit(solution)/shard_map/ppermute | solution.py:491
  82.6 4.3 %last.1 = bf16[256,40,128]{2,1,0:T(8,128)(2,1)} custom-call(s32[1]{0:T(128)} %bitcast.s_ref, bf16[9,2,32,32,128]{4,3,2,1,0:T(8,128)(2,1)S(1)} %get-tuple-element.37.refs_0_.refs_16_, bf16[9,64,128]{2,1,0:T(8,128)(2,1)S(1)} %mix_back.1.refs_0_.refs_1_, bf16[9,64,128]{2,1,0:T(8,128)(2,1)S(1)} %collective-permute-done.7.refs_1_.refs_2_, ...), custom_call_target="tpu_custom_call" | custom-call | flops 5059999744 | bytes 15840000 | tf_op jit(solution)/shard_map/last/pallas_call | solution.py:656
  87.0 12.3 %outer.1 = (f32[8,2,32,32,144]{4,3,2,1,0:T(8,128)}, f32[32,32]{1,0:T(8,128)}, f32[1,32]{1,0:T(1,128)}) custom-call(bf16[9,64,128]{2,1,0:T(8,128)(2,1)S(1)} %collective-permute-done.1.refs_0_.refs_4_, bf16[9,64,128]{2,1,0:T(8,128)(2,1)S(1)} %collective-permute-done.10.refs_5_.refs_1_, bf16[9,64,128]{2,1,0:T(8,128)(2,1)S(1)} %collective-permute-done.2.refs_1_.refs_6_.refs_2_, ...), custom_call_target="tpu_custom_call" | custom-call | flops 14720000000 | bytes 46080000 | tf_op jit(solution)/shard_map/outer/pallas_call | solution.py:529
  (53 shorter events, 2.0 us)
Async XLA Ops:
  7.3 7.6 %collective-permute-start = (bf16[9,64,128]{2,1,0:T(8,128)(2,1)S(1)}, bf16[9,64,128]{2,1,0:T(8,128)(2,1)S(1)}, u32[]{:S(2)}, u32[]{:S(2)}) collective-permute-start(bf16[9,64,128]{2,1,0:T(8,128)(2,1)S(1)} %get-tuple-element.27), channel_id=1, source_target_pairs={{0,1},{1,0},{2,3},{3,2},{4,5},{5,4},{6,7},{7,6},{8,9},{9,8},{10,11... | collective-permute-start | bytes 442376 | tf_op jit(solution)/shard_map/ppermute | solution.py:487
  11.1 13.6 %slice-start = ((s8[5242880]{0:T(1024)(128)(4,1)}), s8[4194304]{0:T(1024)(128)(4,1)S(1)}, s32[]{:S(2)}) async-start(s8[5242880]{0:T(1024)(128)(4,1)} %bitcast.8), calls=%async_computation | async-start | bytes 8388608
  14.9 9.9 %slice-start.1 = ((s8[5242880]{0:T(1024)(128)(4,1)}), s8[1048576]{0:T(1024)(128)(4,1)S(1)}, s32[]{:S(2)}) async-start(s8[5242880]{0:T(1024)(128)(4,1)} %bitcast.8), calls=%async_computation.1 | async-start | bytes 2097152
  14.9 9.9 %copy-start.4 = (bf16[2,512,1024]{2,1,0:T(8,128)(2,1)S(1)}, bf16[2,512,1024]{2,1,0:T(8,128)(2,1)}, u32[]{:S(2)}) copy-start(bf16[2,512,1024]{2,1,0:T(8,128)(2,1)} %constant.16.clone.refs_4_.refs_3_) | copy-start | bytes 6291460
  14.9 9.9 %copy-start.5 = (bf16[2,1024,512]{2,1,0:T(8,128)(2,1)S(1)}, bf16[2,1024,512]{2,1,0:T(8,128)(2,1)}, u32[]{:S(2)}) copy-start(bf16[2,1024,512]{2,1,0:T(8,128)(2,1)} %constant.15.clone.line_hbm.refs_5_) | copy-start | bytes 6291460
  18.8 5.1 %collective-permute-start.5 = (bf16[9,64,128]{2,1,0:T(8,128)(2,1)S(1)}, bf16[9,64,128]{2,1,0:T(8,128)(2,1)S(1)}, u32[]{:S(2)}, u32[]{:S(2)}) collective-permute-start(bf16[9,64,128]{2,1,0:T(8,128)(2,1)S(1)} %get-tuple-element.30.refs_2_), channel_id=1, source_target_pairs={{0,1},{1,0},{2,3},{3,2},{4,5},{5,4},{6,7},{7,6},{8,9},{9,8},{10,11... | collective-permute-start | bytes 442376 | tf_op jit(solution)/shard_map/ppermute | solution.py:487
  18.9 5.0 %collective-permute-start.4 = (bf16[9,64,128]{2,1,0:T(8,128)(2,1)S(1)}, bf16[9,64,128]{2,1,0:T(8,128)(2,1)S(1)}, u32[]{:S(2)}, u32[]{:S(2)}) collective-permute-start(bf16[9,64,128]{2,1,0:T(8,128)(2,1)S(1)} %get-tuple-element.29.refs_12_), channel_id=1, source_target_pairs={{0,8},{2,10},{4,12},{6,14},{8,0},{10,2},{12,4},{14,6},{16,24},{18,... | collective-permute-start | bytes 442376 | tf_op jit(solution)/shard_map/ppermute | solution.py:491
  20.5 4.3 %collective-permute-start.3 = (bf16[9,64,128]{2,1,0:T(8,128)(2,1)S(1)}, bf16[9,64,128]{2,1,0:T(8,128)(2,1)S(1)}, u32[]{:S(2)}, u32[]{:S(2)}) collective-permute-start(bf16[9,64,128]{2,1,0:T(8,128)(2,1)S(1)} %get-tuple-element.29.refs_12_), channel_id=1, source_target_pairs={{0,4},{2,6},{4,0},{6,2},{8,12},{10,14},{12,8},{14,10},{16,20},{18,... | collective-permute-start | bytes 442376 | tf_op jit(solution)/shard_map/ppermute | solution.py:491
  21.7 14.1 %collective-permute-start.2 = (bf16[9,64,128]{2,1,0:T(8,128)(2,1)S(1)}, bf16[9,64,128]{2,1,0:T(8,128)(2,1)S(1)}, u32[]{:S(2)}, u32[]{:S(2)}) collective-permute-start(bf16[9,64,128]{2,1,0:T(8,128)(2,1)S(1)} %get-tuple-element.29.refs_12_), channel_id=1, source_target_pairs={{0,24},{2,26},{4,28},{6,30},{8,16},{10,18},{12,20},{14,22},{16,8},... | collective-permute-start | bytes 442376 | tf_op jit(solution)/shard_map/ppermute | solution.py:491
  31.0 5.1 %collective-permute-start.6 = (bf16[10,64,128]{2,1,0:T(8,128)(2,1)S(1)}, bf16[10,64,128]{2,1,0:T(8,128)(2,1)S(1)}, u32[]{:S(2)}, u32[]{:S(2)}) collective-permute-start(bf16[10,64,128]{2,1,0:T(8,128)(2,1)S(1)} %get-tuple-element.33), channel_id=1, source_target_pairs={{0,1},{1,0},{2,3},{3,2},{4,5},{5,4},{6,7},{7,6},{8,9},{9,8},{10,11... | collective-permute-start | bytes 491528 | tf_op jit(solution)/shard_map/ppermute | solution.py:487
  32.3 6.5 %collective-permute-start.1 = (bf16[9,64,128]{2,1,0:T(8,128)(2,1)S(1)}, bf16[9,64,128]{2,1,0:T(8,128)(2,1)S(1)}, u32[]{:S(2)}, u32[]{:S(2)}) collective-permute-start(bf16[9,64,128]{2,1,0:T(8,128)(2,1)S(1)} %get-tuple-element.29.refs_12_), channel_id=1, source_target_pairs={{0,16},{2,18},{4,20},{6,22},{8,24},{10,26},{12,28},{14,30},{16,0},... | collective-permute-start | bytes 442376 | tf_op jit(solution)/shard_map/ppermute | solution.py:491
  34.6 9.8 %collective-permute-start.16 = (bf16[9,64,128]{2,1,0:T(8,128)(2,1)S(1)}, bf16[9,64,128]{2,1,0:T(8,128)(2,1)S(1)}, u32[]{:S(2)}, u32[]{:S(2)}) collective-permute-start(bf16[9,64,128]{2,1,0:T(8,128)(2,1)S(1)} %collective-permute-done.4.refs_1_.refs_14_), channel_id=1, source_target_pairs={{0,4},{2,6},{4,0},{6,2},{8,12},{10,14},{12,8},{14,10},{16,20},{18,... | collective-permute-start | bytes 442376 | tf_op jit(solution)/shard_map/ppermute | solution.py:491
  35.8 8.5 %collective-permute-start.11 = (bf16[9,64,128]{2,1,0:T(8,128)(2,1)S(1)}, bf16[9,64,128]{2,1,0:T(8,128)(2,1)S(1)}, u32[]{:S(2)}, u32[]{:S(2)}) collective-permute-start(bf16[9,64,128]{2,1,0:T(8,128)(2,1)S(1)} %collective-permute-done.2.refs_1_.refs_6_.refs_2_), channel_id=1, source_target_pairs={{0,4},{2,6},{4,0},{6,2},{8,12},{10,14},{12,8},{14,10},{16,20},{18,... | collective-permute-start | bytes 442376 | tf_op jit(solution)/shard_map/ppermute | solution.py:491
  36.1 16.4 %collective-permute-start.18 = (bf16[10,64,128]{2,1,0:T(8,128)(2,1)S(1)}, bf16[10,64,128]{2,1,0:T(8,128)(2,1)S(1)}, u32[]{:S(2)}, u32[]{:S(2)}) collective-permute-start(bf16[10,64,128]{2,1,0:T(8,128)(2,1)S(1)} %get-tuple-element.36.refs_16_), channel_id=1, source_target_pairs={{0,8},{2,10},{4,12},{6,14},{8,0},{10,2},{12,4},{14,6},{16,24},{18,... | collective-permute-start | bytes 491528 | tf_op jit(solution)/shard_map/ppermute | solution.py:491
  38.7 7.1 %collective-permute-start.10 = (bf16[9,64,128]{2,1,0:T(8,128)(2,1)S(1)}, bf16[9,64,128]{2,1,0:T(8,128)(2,1)S(1)}, u32[]{:S(2)}, u32[]{:S(2)}) collective-permute-start(bf16[9,64,128]{2,1,0:T(8,128)(2,1)S(1)} %collective-permute-done.1.refs_0_.refs_4_), channel_id=1, source_target_pairs={{0,4},{2,6},{4,0},{6,2},{8,12},{10,14},{12,8},{14,10},{16,20},{18,... | collective-permute-start | bytes 442376 | tf_op jit(solution)/shard_map/ppermute | solution.py:491
  39.9 7.9 %collective-permute-start.14 = (bf16[9,64,128]{2,1,0:T(8,128)(2,1)S(1)}, bf16[9,64,128]{2,1,0:T(8,128)(2,1)S(1)}, u32[]{:S(2)}, u32[]{:S(2)}) collective-permute-start(bf16[9,64,128]{2,1,0:T(8,128)(2,1)S(1)} %collective-permute-done.2.refs_1_.refs_6_.refs_2_), channel_id=1, source_target_pairs={{0,2},{2,0},{4,6},{6,4},{8,10},{10,8},{12,14},{14,12},{16,18},{18,... | collective-permute-start | bytes 442376 | tf_op jit(solution)/shard_map/ppermute | solution.py:491
  44.4 4.9 %collective-permute-start.12 = (bf16[9,64,128]{2,1,0:T(8,128)(2,1)S(1)}, bf16[9,64,128]{2,1,0:T(8,128)(2,1)S(1)}, u32[]{:S(2)}, u32[]{:S(2)}) collective-permute-start(bf16[9,64,128]{2,1,0:T(8,128)(2,1)S(1)} %collective-permute-done.1.refs_0_.refs_4_), channel_id=1, source_target_pairs={{0,2},{2,0},{4,6},{6,4},{8,10},{10,8},{12,14},{14,12},{16,18},{18,... | collective-permute-start | bytes 442376 | tf_op jit(solution)/shard_map/ppermute | solution.py:491
  44.4 8.2 %collective-permute-start.15 = (bf16[9,64,128]{2,1,0:T(8,128)(2,1)S(1)}, bf16[9,64,128]{2,1,0:T(8,128)(2,1)S(1)}, u32[]{:S(2)}, u32[]{:S(2)}) collective-permute-start(bf16[9,64,128]{2,1,0:T(8,128)(2,1)S(1)} %collective-permute-done.11.refs_7_.refs_3_), channel_id=1, source_target_pairs={{0,2},{2,0},{4,6},{6,4},{8,10},{10,8},{12,14},{14,12},{16,18},{18,... | collective-permute-start | bytes 442376 | tf_op jit(solution)/shard_map/ppermute | solution.py:491
  45.8 11.0 %collective-permute-start.13 = (bf16[9,64,128]{2,1,0:T(8,128)(2,1)S(1)}, bf16[9,64,128]{2,1,0:T(8,128)(2,1)S(1)}, u32[]{:S(2)}, u32[]{:S(2)}) collective-permute-start(bf16[9,64,128]{2,1,0:T(8,128)(2,1)S(1)} %collective-permute-done.10.refs_5_.refs_1_), channel_id=1, source_target_pairs={{0,2},{2,0},{4,6},{6,4},{8,10},{10,8},{12,14},{14,12},{16,18},{18,... | collective-permute-start | bytes 442376 | tf_op jit(solution)/shard_map/ppermute | solution.py:491
  47.7 14.0 %collective-permute-start.17 = (bf16[10,64,128]{2,1,0:T(8,128)(2,1)S(1)}, bf16[10,64,128]{2,1,0:T(8,128)(2,1)S(1)}, u32[]{:S(2)}, u32[]{:S(2)}) collective-permute-start(bf16[10,64,128]{2,1,0:T(8,128)(2,1)S(1)} %get-tuple-element.36.refs_16_), channel_id=1, source_target_pairs={{0,4},{2,6},{4,0},{6,2},{8,12},{10,14},{12,8},{14,10},{16,20},{18,... | collective-permute-start | bytes 491528 | tf_op jit(solution)/shard_map/ppermute | solution.py:491
  49.2 12.5 %collective-permute-start.9 = (bf16[10,64,128]{2,1,0:T(8,128)(2,1)S(1)}, bf16[10,64,128]{2,1,0:T(8,128)(2,1)S(1)}, u32[]{:S(2)}, u32[]{:S(2)}) collective-permute-start(bf16[10,64,128]{2,1,0:T(8,128)(2,1)S(1)} %get-tuple-element.36.refs_16_), channel_id=1, source_target_pairs={{0,24},{2,26},{4,28},{6,30},{8,16},{10,18},{12,20},{14,22},{16,8},... | collective-permute-start | bytes 491528 | tf_op jit(solution)/shard_map/ppermute | solution.py:491
  52.5 13.7 %collective-permute-start.8 = (bf16[10,64,128]{2,1,0:T(8,128)(2,1)S(1)}, bf16[10,64,128]{2,1,0:T(8,128)(2,1)S(1)}, u32[]{:S(2)}, u32[]{:S(2)}) collective-permute-start(bf16[10,64,128]{2,1,0:T(8,128)(2,1)S(1)} %get-tuple-element.36.refs_16_), channel_id=1, source_target_pairs={{0,16},{2,18},{4,20},{6,22},{8,24},{10,26},{12,28},{14,30},{16,0},... | collective-permute-start | bytes 491528 | tf_op jit(solution)/shard_map/ppermute | solution.py:491
  52.6 13.7 %collective-permute-start.19 = (bf16[10,64,128]{2,1,0:T(8,128)(2,1)S(1)}, bf16[10,64,128]{2,1,0:T(8,128)(2,1)S(1)}, u32[]{:S(2)}, u32[]{:S(2)}) collective-permute-start(bf16[10,64,128]{2,1,0:T(8,128)(2,1)S(1)} %collective-permute-done.18.refs_18_), channel_id=1, source_target_pairs={{0,4},{2,6},{4,0},{6,2},{8,12},{10,14},{12,8},{14,10},{16,20},{18,... | collective-permute-start | bytes 491528 | tf_op jit(solution)/shard_map/ppermute | solution.py:491
  56.8 4.9 %collective-permute-start.7 = (bf16[9,64,128]{2,1,0:T(8,128)(2,1)S(1)}, bf16[9,64,128]{2,1,0:T(8,128)(2,1)S(1)}, u32[]{:S(2)}, u32[]{:S(2)}) collective-permute-start(bf16[9,64,128]{2,1,0:T(8,128)(2,1)S(1)} %mix_back.1.refs_0_.refs_1_), channel_id=1, source_target_pairs={{0,1},{1,0},{2,3},{3,2},{4,5},{5,4},{6,7},{7,6},{8,9},{9,8},{10,11... | collective-permute-start | bytes 442376 | tf_op jit(solution)/shard_map/ppermute | solution.py:487
  71.3 15.7 %collective-permute-start.26 = (bf16[9,2,32,32,128]{4,3,2,1,0:T(8,128)(2,1)S(1)}, bf16[9,2,32,32,128]{4,3,2,1,0:T(8,128)(2,1)S(1)}, u32[]{:S(2)}, u32[]{:S(2)}) collective-permute-start(bf16[9,2,32,32,128]{4,3,2,1,0:T(8,128)(2,1)S(1)} %get-tuple-element.37.refs_0_.refs_16_), channel_id=1, source_target_pairs={{0,2},{2,0},{4,6},{6,4},{8,10},{10,8},{12,14},{14,12},{16,18},{18,... | collective-permute-start | bytes 14155784 | tf_op jit(solution)/shard_map/ppermute | solution.py:491
  72.4 7.8 %collective-permute-start.24 = (bf16[10,64,128]{2,1,0:T(8,128)(2,1)S(1)}, bf16[10,64,128]{2,1,0:T(8,128)(2,1)S(1)}, u32[]{:S(2)}, u32[]{:S(2)}) collective-permute-start(bf16[10,64,128]{2,1,0:T(8,128)(2,1)S(1)} %collective-permute-done.9.refs_3_.refs_10_), channel_id=1, source_target_pairs={{0,2},{2,0},{4,6},{6,4},{8,10},{10,8},{12,14},{14,12},{16,18},{18,... | collective-permute-start | bytes 491528 | tf_op jit(solution)/shard_map/ppermute | solution.py:491
  72.5 8.1 %collective-permute-start.21 = (bf16[10,64,128]{2,1,0:T(8,128)(2,1)S(1)}, bf16[10,64,128]{2,1,0:T(8,128)(2,1)S(1)}, u32[]{:S(2)}, u32[]{:S(2)}) collective-permute-start(bf16[10,64,128]{2,1,0:T(8,128)(2,1)S(1)} %collective-permute-done.9.refs_3_.refs_10_), channel_id=1, source_target_pairs={{0,4},{2,6},{4,0},{6,2},{8,12},{10,14},{12,8},{14,10},{16,20},{18,... | collective-permute-start | bytes 491528 | tf_op jit(solution)/shard_map/ppermute | solution.py:491
  72.6 8.8 %collective-permute-start.20 = (bf16[10,64,128]{2,1,0:T(8,128)(2,1)S(1)}, bf16[10,64,128]{2,1,0:T(8,128)(2,1)S(1)}, u32[]{:S(2)}, u32[]{:S(2)}) collective-permute-start(bf16[10,64,128]{2,1,0:T(8,128)(2,1)S(1)} %collective-permute-done.8.refs_2_.refs_8_), channel_id=1, source_target_pairs={{0,4},{2,6},{4,0},{6,2},{8,12},{10,14},{12,8},{14,10},{16,20},{18,... | collective-permute-start | bytes 491528 | tf_op jit(solution)/shard_map/ppermute | solution.py:491
  74.0 13.0 %collective-permute-start.22 = (bf16[10,64,128]{2,1,0:T(8,128)(2,1)S(1)}, bf16[10,64,128]{2,1,0:T(8,128)(2,1)S(1)}, u32[]{:S(2)}, u32[]{:S(2)}) collective-permute-start(bf16[10,64,128]{2,1,0:T(8,128)(2,1)S(1)} %collective-permute-done.8.refs_2_.refs_8_), channel_id=1, source_target_pairs={{0,2},{2,0},{4,6},{6,4},{8,10},{10,8},{12,14},{14,12},{16,18},{18,... | collective-permute-start | bytes 491528 | tf_op jit(solution)/shard_map/ppermute | solution.py:491
  80.2 6.7 %collective-permute-start.27 = (f32[32,128]{1,0:T(8,128)S(1)}, f32[32,128]{1,0:T(8,128)S(1)}, u32[]{:S(2)}, u32[]{:S(2)}) collective-permute-start(f32[32,128]{1,0:T(8,128)S(1)} %get-tuple-element.40.refs_18_), channel_id=1, source_target_pairs={{0,2},{2,0},{4,6},{6,4},{8,10},{10,8},{12,14},{14,12},{16,18},{18,... | collective-permute-start | bytes 49160 | tf_op jit(solution)/shard_map/ppermute | solution.py:491
  80.6 6.4 %collective-permute-start.25 = (bf16[10,64,128]{2,1,0:T(8,128)(2,1)S(1)}, bf16[10,64,128]{2,1,0:T(8,128)(2,1)S(1)}, u32[]{:S(2)}, u32[]{:S(2)}) collective-permute-start(bf16[10,64,128]{2,1,0:T(8,128)(2,1)S(1)} %collective-permute-done.21.refs_11_), channel_id=1, source_target_pairs={{0,2},{2,0},{4,6},{6,4},{8,10},{10,8},{12,14},{14,12},{16,18},{18,... | collective-permute-start | bytes 491528 | tf_op jit(solution)/shard_map/ppermute | solution.py:491
  81.4 5.6 %collective-permute-start.23 = (bf16[10,64,128]{2,1,0:T(8,128)(2,1)S(1)}, bf16[10,64,128]{2,1,0:T(8,128)(2,1)S(1)}, u32[]{:S(2)}, u32[]{:S(2)}) collective-permute-start(bf16[10,64,128]{2,1,0:T(8,128)(2,1)S(1)} %collective-permute-done.20.refs_9_), channel_id=1, source_target_pairs={{0,2},{2,0},{4,6},{6,4},{8,10},{10,8},{12,14},{14,12},{16,18},{18,... | collective-permute-start | bytes 491528 | tf_op jit(solution)/shard_map/ppermute | solution.py:491
  (5 other events, 37.8 us)

commit v4 on v3

--- a/solution.py
+++ b/solution.py
@@ -405,7 +405,7 @@
     def _(blk):
         load_cells(u_refs, g_refs, blk, u_all, g_all, factor)
 
-        @pl.loop(0, chans, step=TOGETHER)
+        @pl.loop(0, chans, step=TOGETHER, unroll=2)
         def _(i):
             for k, parts in enumerate(products(u_all, g_all, i)):
                 for r, part in enumerate(parts):

time: 99.4 us -> 99.1 us (level)
  no operation moved by 1% of the time
where the time goes in v4:
time: 99.1 us; the launch traced here: 99 us
  Pallas kernels  45.9 us (46%)
  starting transfers between devices  32.3 us (33%)
  waiting for transfers between devices  18.1 us (18%)
  local copies, waits for them, and re-layouts  1.78 us (2%)
    ppermute x24, starting transfers between devices, swap(): return lax.ppermute(array, 'dp', [(i, i ^ bit) for i in range(count)])  28.4 us
    ppermute x24, waiting for transfers between devices, swap(): return lax.ppermute(array, 'dp', [(i, i ^ bit) for i in range(count)])  13.7 us
    pallas_call x1, Pallas kernels, weight_gradient(): pl.pallas_call(functools.partial(outer_kernel, pairs - LANES, cells, half...  12.3 us
    pallas_call x1, Pallas kernels, shards(): call(functools.partial(forward_kernel, own, rest, count), 'forward', 4.3,...  6.61 us
    pallas_call x1, Pallas kernels, shards(): call(functools.partial(middle_kernel, own, rest, count, planes, len(ties)...  6.2 us
    pallas_call x1, Pallas kernels, early_gradient(): call(functools.partial(early_kernel, cells, len(ties), cell_norm), 'early...  4.66 us
    ppermute x4, waiting for transfers between devices, send(): lax.ppermute(array, axis, [(i, (i + shift) % count) for i in range(count)])  4.46 us
    pallas_call x1, Pallas kernels, shards(): call(functools.partial(last_kernel, own, rest, count, block, len(ties)),...  4.3 us
  transfers between devices with their start and end apart: 28, of which 6 were waited for; matrix products, arithmetic and copies ran while one was open for 0% of the time, Pallas kernels for 19%

profile of v4, /device:TPU:1, one launch (start us, length us, event | category | flops | bytes accessed | tf_op | source)
XLA Modules:
  0.0 99.0 jit_solution(5202953355645279995)
XLA Ops:
  0.7 6.6 %forward.1 = (bf16[256,5120]{1,0:T(8,128)(2,1)}, f32[9,64,128]{2,1,0:T(8,128)S(1)}, bf16[9,64,128]{2,1,0:T(8,128)(2,1)S(1)}) custom-call(s32[1]{0:T(128)} %bitcast.s_ref, bf16[256,40,128]{2,1,0:T(8,128)(2,1)} %bitcast.10, bf16[5120,512]{1,0:T(8,128)(2,1)} %constant.14.clone.basis_hbm.refs_10_.refs_7_, bf16[2,1024,512]{2,1,0:T(8,128)(2,1)} %constant.15.clone.line_hbm.refs_5_), custom_call_target="tpu_custom_call" | custom-call | flops 4944999936 | bytes 15480000 | tf_op jit(solution)/shard_map/forward/pallas_call | solution.py:576
  7.3 2.1 %collective-permute-start = (bf16[9,64,128]{2,1,0:T(8,128)(2,1)S(1)}, bf16[9,64,128]{2,1,0:T(8,128)(2,1)S(1)}, u32[]{:S(2)}, u32[]{:S(2)}) collective-permute-start(bf16[9,64,128]{2,1,0:T(8,128)(2,1)S(1)} %get-tuple-element.27), channel_id=1, source_target_pairs={{0,1},{1,0},{2,3},{3,2},{4,5},{5,4},{6,7},{7,6},{8,9},{9,8},{10,11... | collective-permute-start | bytes 442376 | tf_op jit(solution)/shard_map/ppermute | solution.py:487
  9.4 1.7 %copy-done.1 = bf16[256,5120]{1,0:T(8,128)(2,1)S(1)} copy-done((bf16[256,5120]{1,0:T(8,128)(2,1)S(1)}, bf16[256,5120]{1,0:T(8,128)(2,1)}, u32[]{:S(2)}) %copy-start.1) | copy-done | bytes 2621464
  11.1 3.7 %prepare.1 = (bf16[256,5120]{1,0:T(8,128)(2,1)S(1)}, f32[256,5120]{1,0:T(8,128)S(1)}, bf16[256,256]{1,0:T(8,128)(2,1)S(1)}, bf16[8,2,32,32,144]{4,3,2,1,0:T(8,128)(2,1)S(1)}) custom-call(bf16[256,40,128]{2,1,0:T(8,128)(2,1)S(1)} %bitcast.6, bf16[8,2,32,32,144]{4,3,2,1,0:T(8,128)(2,1)} %weight_hbm.1, bf16[256,5120]{1,0:T(8,128)(2,1)S(1)} %copy-done.1, ...), custom_call_target="tpu_custom_call" | custom-call | flops 2875000064 | bytes 9000000 | tf_op jit(solution)/shard_map/prepare/pallas_call | solution.py:593
  14.9 3.9 %mix.1 = (bf16[9,64,128]{2,1,0:T(8,128)(2,1)S(1)}, bf16[9,64,128]{2,1,0:T(8,128)(2,1)S(1)}) custom-call(bf16[256,5120]{1,0:T(8,128)(2,1)S(1)} %get-tuple-element.25.refs_0_.refs_8_, f32[9,64,128]{2,1,0:T(8,128)S(1)} %get-tuple-element.26.refs_1_, bf16[9,64,128]{2,1,0:T(8,128)(2,1)S(1)} %collective-permute-done.refs_2_, ...), custom_call_target="tpu_custom_call" | custom-call | flops 4485000192 | bytes 14040000 | tf_op jit(solution)/shard_map/mix/pallas_call | solution.py:608
  18.9 1.5 %collective-permute-start.4 = (bf16[9,64,128]{2,1,0:T(8,128)(2,1)S(1)}, bf16[9,64,128]{2,1,0:T(8,128)(2,1)S(1)}, u32[]{:S(2)}, u32[]{:S(2)}) collective-permute-start(bf16[9,64,128]{2,1,0:T(8,128)(2,1)S(1)} %get-tuple-element.29.refs_12_), channel_id=1, source_target_pairs={{0,8},{2,10},{4,12},{6,14},{8,0},{10,2},{12,4},{14,6},{16,24},{18,... | collective-permute-start | bytes 442376 | tf_op jit(solution)/shard_map/ppermute | solution.py:491
  20.5 1.2 %collective-permute-start.3 = (bf16[9,64,128]{2,1,0:T(8,128)(2,1)S(1)}, bf16[9,64,128]{2,1,0:T(8,128)(2,1)S(1)}, u32[]{:S(2)}, u32[]{:S(2)}) collective-permute-start(bf16[9,64,128]{2,1,0:T(8,128)(2,1)S(1)} %get-tuple-element.29.refs_12_), channel_id=1, source_target_pairs={{0,4},{2,6},{4,0},{6,2},{8,12},{10,14},{12,8},{14,10},{16,20},{18,... | collective-permute-start | bytes 442376 | tf_op jit(solution)/shard_map/ppermute | solution.py:491
  21.7 2.2 %collective-permute-start.2 = (bf16[9,64,128]{2,1,0:T(8,128)(2,1)S(1)}, bf16[9,64,128]{2,1,0:T(8,128)(2,1)S(1)}, u32[]{:S(2)}, u32[]{:S(2)}) collective-permute-start(bf16[9,64,128]{2,1,0:T(8,128)(2,1)S(1)} %get-tuple-element.29.refs_12_), channel_id=1, source_target_pairs={{0,24},{2,26},{4,28},{6,30},{8,16},{10,18},{12,20},{14,22},{16,8},... | collective-permute-start | bytes 442376 | tf_op jit(solution)/shard_map/ppermute | solution.py:491
  23.9 0.8 collective-permute-done.3.refs_0_.refs_13_
  24.8 6.2 %middle.1 = (bf16[256,5120]{1,0:T(8,128)(2,1)S(1)}, f32[32,128]{1,0:T(8,128)S(1)}, f32[9,64,128]{2,1,0:T(8,128)S(1)}, bf16[10,64,128]{2,1,0:T(8,128)(2,1)S(1)}) custom-call(s32[1]{0:T(128)} %bitcast.s_ref, bf16[9,64,128]{2,1,0:T(8,128)(2,1)S(1)} %collective-permute-done.3.refs_0_.refs_13_, bf16[9,64,128]{2,1,0:T(8,128)(2,1)S(1)} %collective-permute-done.4.refs_1_.refs_14_, ...), custom_call_target="tpu_custom_call" | custom-call | flops 7245000192 | bytes 22680000 | tf_op jit(solution)/shard_map/middle/pallas_call | solution.py:621
  31.0 1.3 %collective-permute-start.6 = (bf16[10,64,128]{2,1,0:T(8,128)(2,1)S(1)}, bf16[10,64,128]{2,1,0:T(8,128)(2,1)S(1)}, u32[]{:S(2)}, u32[]{:S(2)}) collective-permute-start(bf16[10,64,128]{2,1,0:T(8,128)(2,1)S(1)} %get-tuple-element.33), channel_id=1, source_target_pairs={{0,1},{1,0},{2,3},{3,2},{4,5},{5,4},{6,7},{7,6},{8,9},{9,8},{10,11... | collective-permute-start | bytes 491528 | tf_op jit(solution)/shard_map/ppermute | solution.py:487
  32.3 2.3 %collective-permute-start.1 = (bf16[9,64,128]{2,1,0:T(8,128)(2,1)S(1)}, bf16[9,64,128]{2,1,0:T(8,128)(2,1)S(1)}, u32[]{:S(2)}, u32[]{:S(2)}) collective-permute-start(bf16[9,64,128]{2,1,0:T(8,128)(2,1)S(1)} %get-tuple-element.29.refs_12_), channel_id=1, source_target_pairs={{0,16},{2,18},{4,20},{6,22},{8,24},{10,26},{12,28},{14,30},{16,0},... | collective-permute-start | bytes 442376 | tf_op jit(solution)/shard_map/ppermute | solution.py:491
  34.6 1.2 %collective-permute-start.16 = (bf16[9,64,128]{2,1,0:T(8,128)(2,1)S(1)}, bf16[9,64,128]{2,1,0:T(8,128)(2,1)S(1)}, u32[]{:S(2)}, u32[]{:S(2)}) collective-permute-start(bf16[9,64,128]{2,1,0:T(8,128)(2,1)S(1)} %collective-permute-done.4.refs_1_.refs_14_), channel_id=1, source_target_pairs={{0,4},{2,6},{4,0},{6,2},{8,12},{10,14},{12,8},{14,10},{16,20},{18,... | collective-permute-start | bytes 442376 | tf_op jit(solution)/shard_map/ppermute | solution.py:491
  36.3 2.4 %collective-permute-done.1.refs_0_.refs_4_ = bf16[9,64,128]{2,1,0:T(8,128)(2,1)S(1)} collective-permute-done((bf16[9,64,128]{2,1,0:T(8,128)(2,1)S(1)}, bf16[9,64,128]{2,1,0:T(8,128)(2,1)S(1)}, u32[]{:S(2)}, u32[]{:S(2)}) %collective-permute-start.1) | collective-permute-done | bytes 147488 | tf_op jit(solution)/shard_map/ppermute | solution.py:491
  38.7 1.1 %collective-permute-start.10 = (bf16[9,64,128]{2,1,0:T(8,128)(2,1)S(1)}, bf16[9,64,128]{2,1,0:T(8,128)(2,1)S(1)}, u32[]{:S(2)}, u32[]{:S(2)}) collective-permute-start(bf16[9,64,128]{2,1,0:T(8,128)(2,1)S(1)} %collective-permute-done.1.refs_0_.refs_4_), channel_id=1, source_target_pairs={{0,4},{2,6},{4,0},{6,2},{8,12},{10,14},{12,8},{14,10},{16,20},{18,... | collective-permute-start | bytes 442376 | tf_op jit(solution)/shard_map/ppermute | solution.py:491
  39.9 4.5 %collective-permute-start.14 = (bf16[9,64,128]{2,1,0:T(8,128)(2,1)S(1)}, bf16[9,64,128]{2,1,0:T(8,128)(2,1)S(1)}, u32[]{:S(2)}, u32[]{:S(2)}) collective-permute-start(bf16[9,64,128]{2,1,0:T(8,128)(2,1)S(1)} %collective-permute-done.2.refs_1_.refs_6_.refs_2_), channel_id=1, source_target_pairs={{0,2},{2,0},{4,6},{6,4},{8,10},{10,8},{12,14},{14,12},{16,18},{18,... | collective-permute-start | bytes 442376 | tf_op jit(solution)/shard_map/ppermute | solution.py:491
  44.4 1.4 %collective-permute-start.15 = (bf16[9,64,128]{2,1,0:T(8,128)(2,1)S(1)}, bf16[9,64,128]{2,1,0:T(8,128)(2,1)S(1)}, u32[]{:S(2)}, u32[]{:S(2)}) collective-permute-start(bf16[9,64,128]{2,1,0:T(8,128)(2,1)S(1)} %collective-permute-done.11.refs_7_.refs_3_), channel_id=1, source_target_pairs={{0,2},{2,0},{4,6},{6,4},{8,10},{10,8},{12,14},{14,12},{16,18},{18,... | collective-permute-start | bytes 442376 | tf_op jit(solution)/shard_map/ppermute | solution.py:491
  45.8 1.9 %collective-permute-start.13 = (bf16[9,64,128]{2,1,0:T(8,128)(2,1)S(1)}, bf16[9,64,128]{2,1,0:T(8,128)(2,1)S(1)}, u32[]{:S(2)}, u32[]{:S(2)}) collective-permute-start(bf16[9,64,128]{2,1,0:T(8,128)(2,1)S(1)} %collective-permute-done.10.refs_5_.refs_1_), channel_id=1, source_target_pairs={{0,2},{2,0},{4,6},{6,4},{8,10},{10,8},{12,14},{14,12},{16,18},{18,... | collective-permute-start | bytes 442376 | tf_op jit(solution)/shard_map/ppermute | solution.py:491
  47.7 1.5 %collective-permute-start.17 = (bf16[10,64,128]{2,1,0:T(8,128)(2,1)S(1)}, bf16[10,64,128]{2,1,0:T(8,128)(2,1)S(1)}, u32[]{:S(2)}, u32[]{:S(2)}) collective-permute-start(bf16[10,64,128]{2,1,0:T(8,128)(2,1)S(1)} %get-tuple-element.36.refs_16_), channel_id=1, source_target_pairs={{0,4},{2,6},{4,0},{6,2},{8,12},{10,14},{12,8},{14,10},{16,20},{18,... | collective-permute-start | bytes 491528 | tf_op jit(solution)/shard_map/ppermute | solution.py:491
  49.2 3.3 %collective-permute-start.9 = (bf16[10,64,128]{2,1,0:T(8,128)(2,1)S(1)}, bf16[10,64,128]{2,1,0:T(8,128)(2,1)S(1)}, u32[]{:S(2)}, u32[]{:S(2)}) collective-permute-start(bf16[10,64,128]{2,1,0:T(8,128)(2,1)S(1)} %get-tuple-element.36.refs_16_), channel_id=1, source_target_pairs={{0,24},{2,26},{4,28},{6,30},{8,16},{10,18},{12,20},{14,22},{16,8},... | collective-permute-start | bytes 491528 | tf_op jit(solution)/shard_map/ppermute | solution.py:491
  52.7 4.1 %mix_back.1.refs_0_.refs_1_ = bf16[9,64,128]{2,1,0:T(8,128)(2,1)S(1)} custom-call(bf16[9,64,128]{2,1,0:T(8,128)(2,1)S(1)} %collective-permute-done.1.refs_0_.refs_4_, bf16[9,64,128]{2,1,0:T(8,128)(2,1)S(1)} %collective-permute-done.2.refs_1_.refs_6_.refs_2_, f32[9,64,128]{2,1,0:T(8,128)S(1)} %get-tuple-element.35.refs_2_, ...), custom_call_target="tpu_custom_call" | custom-call | flops 4714999808 | bytes 14759999 | tf_op jit(solution)/shard_map/mix_back/pallas_call | solution.py:635
  57.3 4.4 %collective-permute-done.7.refs_1_.refs_2_ = bf16[9,64,128]{2,1,0:T(8,128)(2,1)S(1)} collective-permute-done((bf16[9,64,128]{2,1,0:T(8,128)(2,1)S(1)}, bf16[9,64,128]{2,1,0:T(8,128)(2,1)S(1)}, u32[]{:S(2)}, u32[]{:S(2)}) %collective-permute-start.7) | collective-permute-done | bytes 147488 | tf_op jit(solution)/shard_map/ppermute | solution.py:487
  61.8 4.5 %collective-permute-done.8.refs_2_.refs_8_ = bf16[10,64,128]{2,1,0:T(8,128)(2,1)S(1)} collective-permute-done((bf16[10,64,128]{2,1,0:T(8,128)(2,1)S(1)}, bf16[10,64,128]{2,1,0:T(8,128)(2,1)S(1)}, u32[]{:S(2)}, u32[]{:S(2)}) %collective-permute-start.8) | collective-permute-done | bytes 163872 | tf_op jit(solution)/shard_map/ppermute | solution.py:491
  66.3 4.7 %early.1 = (bf16[9,2,32,32,128]{4,3,2,1,0:T(8,128)(2,1)S(1)}, f32[32,128]{1,0:T(8,128)S(1)}) custom-call(bf16[9,64,128]{2,1,0:T(8,128)(2,1)S(1)} %mix_back.1.refs_0_.refs_1_, bf16[9,64,128]{2,1,0:T(8,128)(2,1)S(1)} %collective-permute-done.7.refs_1_.refs_2_, bf16[10,64,128]{2,1,0:T(8,128)(2,1)S(1)} %collective-permute-done.8.refs_2_.refs_8_, ...), custom_call_target="tpu_custom_call" | custom-call | flops 5520000000 | bytes 17280000 | tf_op jit(solution)/shard_map/early/pallas_call | solution.py:514
  70.9 1.2 %collective-permute-start.26 = (bf16[9,2,32,32,128]{4,3,2,1,0:T(8,128)(2,1)S(1)}, bf16[9,2,32,32,128]{4,3,2,1,0:T(8,128)(2,1)S(1)}, u32[]{:S(2)}, u32[]{:S(2)}) collective-permute-start(bf16[9,2,32,32,128]{4,3,2,1,0:T(8,128)(2,1)S(1)} %get-tuple-element.37.refs_0_.refs_16_), channel_id=1, source_target_pairs={{0,2},{2,0},{4,6},{6,4},{8,10},{10,8},{12,14},{14,12},{16,18},{18,... | collective-permute-start | bytes 14155784 | tf_op jit(solution)/shard_map/ppermute | solution.py:491
  72.2 1.4 %collective-permute-start.20 = (bf16[10,64,128]{2,1,0:T(8,128)(2,1)S(1)}, bf16[10,64,128]{2,1,0:T(8,128)(2,1)S(1)}, u32[]{:S(2)}, u32[]{:S(2)}) collective-permute-start(bf16[10,64,128]{2,1,0:T(8,128)(2,1)S(1)} %collective-permute-done.8.refs_2_.refs_8_), channel_id=1, source_target_pairs={{0,4},{2,6},{4,0},{6,2},{8,12},{10,14},{12,8},{14,10},{16,20},{18,... | collective-permute-start | bytes 491528 | tf_op jit(solution)/shard_map/ppermute | solution.py:491
  73.6 1.0 %collective-permute-start.22 = (bf16[10,64,128]{2,1,0:T(8,128)(2,1)S(1)}, bf16[10,64,128]{2,1,0:T(8,128)(2,1)S(1)}, u32[]{:S(2)}, u32[]{:S(2)}) collective-permute-start(bf16[10,64,128]{2,1,0:T(8,128)(2,1)S(1)} %collective-permute-done.8.refs_2_.refs_8_), channel_id=1, source_target_pairs={{0,2},{2,0},{4,6},{6,4},{8,10},{10,8},{12,14},{14,12},{16,18},{18,... | collective-permute-start | bytes 491528 | tf_op jit(solution)/shard_map/ppermute | solution.py:491
  74.6 5.2 %collective-permute-done.24.refs_14_ = bf16[10,64,128]{2,1,0:T(8,128)(2,1)S(1)} collective-permute-done((bf16[10,64,128]{2,1,0:T(8,128)(2,1)S(1)}, bf16[10,64,128]{2,1,0:T(8,128)(2,1)S(1)}, u32[]{:S(2)}, u32[]{:S(2)}) %collective-permute-start.24) | collective-permute-done | bytes 163872 | tf_op jit(solution)/shard_map/ppermute | solution.py:491
  80.4 0.6 collective-permute-done.20.refs_9_
  81.0 1.3 %collective-permute-start.23 = (bf16[10,64,128]{2,1,0:T(8,128)(2,1)S(1)}, bf16[10,64,128]{2,1,0:T(8,128)(2,1)S(1)}, u32[]{:S(2)}, u32[]{:S(2)}) collective-permute-start(bf16[10,64,128]{2,1,0:T(8,128)(2,1)S(1)} %collective-permute-done.20.refs_9_), channel_id=1, source_target_pairs={{0,2},{2,0},{4,6},{6,4},{8,10},{10,8},{12,14},{14,12},{16,18},{18,... | collective-permute-start | bytes 491528 | tf_op jit(solution)/shard_map/ppermute | solution.py:491
  82.3 4.3 %last.1 = bf16[256,40,128]{2,1,0:T(8,128)(2,1)} custom-call(s32[1]{0:T(128)} %bitcast.s_ref, bf16[9,2,32,32,128]{4,3,2,1,0:T(8,128)(2,1)S(1)} %get-tuple-element.37.refs_0_.refs_16_, bf16[9,64,128]{2,1,0:T(8,128)(2,1)S(1)} %mix_back.1.refs_0_.refs_1_, bf16[9,64,128]{2,1,0:T(8,128)(2,1)S(1)} %collective-permute-done.7.refs_1_.refs_2_, ...), custom_call_target="tpu_custom_call" | custom-call | flops 5059999744 | bytes 15840000 | tf_op jit(solution)/shard_map/last/pallas_call | solution.py:656
  86.7 12.3 %outer.1 = (f32[8,2,32,32,144]{4,3,2,1,0:T(8,128)}, f32[32,32]{1,0:T(8,128)}, f32[1,32]{1,0:T(1,128)}) custom-call(bf16[9,64,128]{2,1,0:T(8,128)(2,1)S(1)} %collective-permute-done.1.refs_0_.refs_4_, bf16[9,64,128]{2,1,0:T(8,128)(2,1)S(1)} %collective-permute-done.10.refs_5_.refs_1_, bf16[9,64,128]{2,1,0:T(8,128)(2,1)S(1)} %collective-permute-done.2.refs_1_.refs_6_.refs_2_, ...), custom_call_target="tpu_custom_call" | custom-call | flops 14720000000 | bytes 46080000 | tf_op jit(solution)/shard_map/outer/pallas_call | solution.py:529
  (53 shorter events, 2.0 us)
Async XLA Ops:
  7.3 7.6 %collective-permute-start = (bf16[9,64,128]{2,1,0:T(8,128)(2,1)S(1)}, bf16[9,64,128]{2,1,0:T(8,128)(2,1)S(1)}, u32[]{:S(2)}, u32[]{:S(2)}) collective-permute-start(bf16[9,64,128]{2,1,0:T(8,128)(2,1)S(1)} %get-tuple-element.27), channel_id=1, source_target_pairs={{0,1},{1,0},{2,3},{3,2},{4,5},{5,4},{6,7},{7,6},{8,9},{9,8},{10,11... | collective-permute-start | bytes 442376 | tf_op jit(solution)/shard_map/ppermute | solution.py:487
  11.1 13.6 %slice-start = ((s8[5242880]{0:T(1024)(128)(4,1)}), s8[4194304]{0:T(1024)(128)(4,1)S(1)}, s32[]{:S(2)}) async-start(s8[5242880]{0:T(1024)(128)(4,1)} %bitcast.8), calls=%async_computation | async-start | bytes 8388608
  14.9 9.9 %slice-start.1 = ((s8[5242880]{0:T(1024)(128)(4,1)}), s8[1048576]{0:T(1024)(128)(4,1)S(1)}, s32[]{:S(2)}) async-start(s8[5242880]{0:T(1024)(128)(4,1)} %bitcast.8), calls=%async_computation.1 | async-start | bytes 2097152
  14.9 9.9 %copy-start.4 = (bf16[2,512,1024]{2,1,0:T(8,128)(2,1)S(1)}, bf16[2,512,1024]{2,1,0:T(8,128)(2,1)}, u32[]{:S(2)}) copy-start(bf16[2,512,1024]{2,1,0:T(8,128)(2,1)} %constant.16.clone.refs_4_.refs_3_) | copy-start | bytes 6291460
  14.9 9.9 %copy-start.5 = (bf16[2,1024,512]{2,1,0:T(8,128)(2,1)S(1)}, bf16[2,1024,512]{2,1,0:T(8,128)(2,1)}, u32[]{:S(2)}) copy-start(bf16[2,1024,512]{2,1,0:T(8,128)(2,1)} %constant.15.clone.line_hbm.refs_5_) | copy-start | bytes 6291460
  18.8 5.1 %collective-permute-start.5 = (bf16[9,64,128]{2,1,0:T(8,128)(2,1)S(1)}, bf16[9,64,128]{2,1,0:T(8,128)(2,1)S(1)}, u32[]{:S(2)}, u32[]{:S(2)}) collective-permute-start(bf16[9,64,128]{2,1,0:T(8,128)(2,1)S(1)} %get-tuple-element.30.refs_2_), channel_id=1, source_target_pairs={{0,1},{1,0},{2,3},{3,2},{4,5},{5,4},{6,7},{7,6},{8,9},{9,8},{10,11... | collective-permute-start | bytes 442376 | tf_op jit(solution)/shard_map/ppermute | solution.py:487
  18.9 5.0 %collective-permute-start.4 = (bf16[9,64,128]{2,1,0:T(8,128)(2,1)S(1)}, bf16[9,64,128]{2,1,0:T(8,128)(2,1)S(1)}, u32[]{:S(2)}, u32[]{:S(2)}) collective-permute-start(bf16[9,64,128]{2,1,0:T(8,128)(2,1)S(1)} %get-tuple-element.29.refs_12_), channel_id=1, source_target_pairs={{0,8},{2,10},{4,12},{6,14},{8,0},{10,2},{12,4},{14,6},{16,24},{18,... | collective-permute-start | bytes 442376 | tf_op jit(solution)/shard_map/ppermute | solution.py:491
  20.5 4.3 %collective-permute-start.3 = (bf16[9,64,128]{2,1,0:T(8,128)(2,1)S(1)}, bf16[9,64,128]{2,1,0:T(8,128)(2,1)S(1)}, u32[]{:S(2)}, u32[]{:S(2)}) collective-permute-start(bf16[9,64,128]{2,1,0:T(8,128)(2,1)S(1)} %get-tuple-element.29.refs_12_), channel_id=1, source_target_pairs={{0,4},{2,6},{4,0},{6,2},{8,12},{10,14},{12,8},{14,10},{16,20},{18,... | collective-permute-start | bytes 442376 | tf_op jit(solution)/shard_map/ppermute | solution.py:491
  21.7 14.1 %collective-permute-start.2 = (bf16[9,64,128]{2,1,0:T(8,128)(2,1)S(1)}, bf16[9,64,128]{2,1,0:T(8,128)(2,1)S(1)}, u32[]{:S(2)}, u32[]{:S(2)}) collective-permute-start(bf16[9,64,128]{2,1,0:T(8,128)(2,1)S(1)} %get-tuple-element.29.refs_12_), channel_id=1, source_target_pairs={{0,24},{2,26},{4,28},{6,30},{8,16},{10,18},{12,20},{14,22},{16,8},... | collective-permute-start | bytes 442376 | tf_op jit(solution)/shard_map/ppermute | solution.py:491
  31.0 5.1 %collective-permute-start.6 = (bf16[10,64,128]{2,1,0:T(8,128)(2,1)S(1)}, bf16[10,64,128]{2,1,0:T(8,128)(2,1)S(1)}, u32[]{:S(2)}, u32[]{:S(2)}) collective-permute-start(bf16[10,64,128]{2,1,0:T(8,128)(2,1)S(1)} %get-tuple-element.33), channel_id=1, source_target_pairs={{0,1},{1,0},{2,3},{3,2},{4,5},{5,4},{6,7},{7,6},{8,9},{9,8},{10,11... | collective-permute-start | bytes 491528 | tf_op jit(solution)/shard_map/ppermute | solution.py:487
  32.3 6.5 %collective-permute-start.1 = (bf16[9,64,128]{2,1,0:T(8,128)(2,1)S(1)}, bf16[9,64,128]{2,1,0:T(8,128)(2,1)S(1)}, u32[]{:S(2)}, u32[]{:S(2)}) collective-permute-start(bf16[9,64,128]{2,1,0:T(8,128)(2,1)S(1)} %get-tuple-element.29.refs_12_), channel_id=1, source_target_pairs={{0,16},{2,18},{4,20},{6,22},{8,24},{10,26},{12,28},{14,30},{16,0},... | collective-permute-start | bytes 442376 | tf_op jit(solution)/shard_map/ppermute | solution.py:491
  34.6 9.8 %collective-permute-start.16 = (bf16[9,64,128]{2,1,0:T(8,128)(2,1)S(1)}, bf16[9,64,128]{2,1,0:T(8,128)(2,1)S(1)}, u32[]{:S(2)}, u32[]{:S(2)}) collective-permute-start(bf16[9,64,128]{2,1,0:T(8,128)(2,1)S(1)} %collective-permute-done.4.refs_1_.refs_14_), channel_id=1, source_target_pairs={{0,4},{2,6},{4,0},{6,2},{8,12},{10,14},{12,8},{14,10},{16,20},{18,... | collective-permute-start | bytes 442376 | tf_op jit(solution)/shard_map/ppermute | solution.py:491
  35.8 8.5 %collective-permute-start.11 = (bf16[9,64,128]{2,1,0:T(8,128)(2,1)S(1)}, bf16[9,64,128]{2,1,0:T(8,128)(2,1)S(1)}, u32[]{:S(2)}, u32[]{:S(2)}) collective-permute-start(bf16[9,64,128]{2,1,0:T(8,128)(2,1)S(1)} %collective-permute-done.2.refs_1_.refs_6_.refs_2_), channel_id=1, source_target_pairs={{0,4},{2,6},{4,0},{6,2},{8,12},{10,14},{12,8},{14,10},{16,20},{18,... | collective-permute-start | bytes 442376 | tf_op jit(solution)/shard_map/ppermute | solution.py:491
  36.1 16.4 %collective-permute-start.18 = (bf16[10,64,128]{2,1,0:T(8,128)(2,1)S(1)}, bf16[10,64,128]{2,1,0:T(8,128)(2,1)S(1)}, u32[]{:S(2)}, u32[]{:S(2)}) collective-permute-start(bf16[10,64,128]{2,1,0:T(8,128)(2,1)S(1)} %get-tuple-element.36.refs_16_), channel_id=1, source_target_pairs={{0,8},{2,10},{4,12},{6,14},{8,0},{10,2},{12,4},{14,6},{16,24},{18,... | collective-permute-start | bytes 491528 | tf_op jit(solution)/shard_map/ppermute | solution.py:491
  38.7 7.1 %collective-permute-start.10 = (bf16[9,64,128]{2,1,0:T(8,128)(2,1)S(1)}, bf16[9,64,128]{2,1,0:T(8,128)(2,1)S(1)}, u32[]{:S(2)}, u32[]{:S(2)}) collective-permute-start(bf16[9,64,128]{2,1,0:T(8,128)(2,1)S(1)} %collective-permute-done.1.refs_0_.refs_4_), channel_id=1, source_target_pairs={{0,4},{2,6},{4,0},{6,2},{8,12},{10,14},{12,8},{14,10},{16,20},{18,... | collective-permute-start | bytes 442376 | tf_op jit(solution)/shard_map/ppermute | solution.py:491
  39.9 7.9 %collective-permute-start.14 = (bf16[9,64,128]{2,1,0:T(8,128)(2,1)S(1)}, bf16[9,64,128]{2,1,0:T(8,128)(2,1)S(1)}, u32[]{:S(2)}, u32[]{:S(2)}) collective-permute-start(bf16[9,64,128]{2,1,0:T(8,128)(2,1)S(1)} %collective-permute-done.2.refs_1_.refs_6_.refs_2_), channel_id=1, source_target_pairs={{0,2},{2,0},{4,6},{6,4},{8,10},{10,8},{12,14},{14,12},{16,18},{18,... | collective-permute-start | bytes 442376 | tf_op jit(solution)/shard_map/ppermute | solution.py:491
  44.4 4.9 %collective-permute-start.12 = (bf16[9,64,128]{2,1,0:T(8,128)(2,1)S(1)}, bf16[9,64,128]{2,1,0:T(8,128)(2,1)S(1)}, u32[]{:S(2)}, u32[]{:S(2)}) collective-permute-start(bf16[9,64,128]{2,1,0:T(8,128)(2,1)S(1)} %collective-permute-done.1.refs_0_.refs_4_), channel_id=1, source_target_pairs={{0,2},{2,0},{4,6},{6,4},{8,10},{10,8},{12,14},{14,12},{16,18},{18,... | collective-permute-start | bytes 442376 | tf_op jit(solution)/shard_map/ppermute | solution.py:491
  44.4 8.2 %collective-permute-start.15 = (bf16[9,64,128]{2,1,0:T(8,128)(2,1)S(1)}, bf16[9,64,128]{2,1,0:T(8,128)(2,1)S(1)}, u32[]{:S(2)}, u32[]{:S(2)}) collective-permute-start(bf16[9,64,128]{2,1,0:T(8,128)(2,1)S(1)} %collective-permute-done.11.refs_7_.refs_3_), channel_id=1, source_target_pairs={{0,2},{2,0},{4,6},{6,4},{8,10},{10,8},{12,14},{14,12},{16,18},{18,... | collective-permute-start | bytes 442376 | tf_op jit(solution)/shard_map/ppermute | solution.py:491
  45.8 11.0 %collective-permute-start.13 = (bf16[9,64,128]{2,1,0:T(8,128)(2,1)S(1)}, bf16[9,64,128]{2,1,0:T(8,128)(2,1)S(1)}, u32[]{:S(2)}, u32[]{:S(2)}) collective-permute-start(bf16[9,64,128]{2,1,0:T(8,128)(2,1)S(1)} %collective-permute-done.10.refs_5_.refs_1_), channel_id=1, source_target_pairs={{0,2},{2,0},{4,6},{6,4},{8,10},{10,8},{12,14},{14,12},{16,18},{18,... | collective-permute-start | bytes 442376 | tf_op jit(solution)/shard_map/ppermute | solution.py:491
  47.7 14.0 %collective-permute-start.17 = (bf16[10,64,128]{2,1,0:T(8,128)(2,1)S(1)}, bf16[10,64,128]{2,1,0:T(8,128)(2,1)S(1)}, u32[]{:S(2)}, u32[]{:S(2)}) collective-permute-start(bf16[10,64,128]{2,1,0:T(8,128)(2,1)S(1)} %get-tuple-element.36.refs_16_), channel_id=1, source_target_pairs={{0,4},{2,6},{4,0},{6,2},{8,12},{10,14},{12,8},{14,10},{16,20},{18,... | collective-permute-start | bytes 491528 | tf_op jit(solution)/shard_map/ppermute | solution.py:491
  49.2 12.5 %collective-permute-start.9 = (bf16[10,64,128]{2,1,0:T(8,128)(2,1)S(1)}, bf16[10,64,128]{2,1,0:T(8,128)(2,1)S(1)}, u32[]{:S(2)}, u32[]{:S(2)}) collective-permute-start(bf16[10,64,128]{2,1,0:T(8,128)(2,1)S(1)} %get-tuple-element.36.refs_16_), channel_id=1, source_target_pairs={{0,24},{2,26},{4,28},{6,30},{8,16},{10,18},{12,20},{14,22},{16,8},... | collective-permute-start | bytes 491528 | tf_op jit(solution)/shard_map/ppermute | solution.py:491
  52.5 13.7 %collective-permute-start.8 = (bf16[10,64,128]{2,1,0:T(8,128)(2,1)S(1)}, bf16[10,64,128]{2,1,0:T(8,128)(2,1)S(1)}, u32[]{:S(2)}, u32[]{:S(2)}) collective-permute-start(bf16[10,64,128]{2,1,0:T(8,128)(2,1)S(1)} %get-tuple-element.36.refs_16_), channel_id=1, source_target_pairs={{0,16},{2,18},{4,20},{6,22},{8,24},{10,26},{12,28},{14,30},{16,0},... | collective-permute-start | bytes 491528 | tf_op jit(solution)/shard_map/ppermute | solution.py:491
  52.6 13.7 %collective-permute-start.19 = (bf16[10,64,128]{2,1,0:T(8,128)(2,1)S(1)}, bf16[10,64,128]{2,1,0:T(8,128)(2,1)S(1)}, u32[]{:S(2)}, u32[]{:S(2)}) collective-permute-start(bf16[10,64,128]{2,1,0:T(8,128)(2,1)S(1)} %collective-permute-done.18.refs_18_), channel_id=1, source_target_pairs={{0,4},{2,6},{4,0},{6,2},{8,12},{10,14},{12,8},{14,10},{16,20},{18,... | collective-permute-start | bytes 491528 | tf_op jit(solution)/shard_map/ppermute | solution.py:491
  56.8 4.9 %collective-permute-start.7 = (bf16[9,64,128]{2,1,0:T(8,128)(2,1)S(1)}, bf16[9,64,128]{2,1,0:T(8,128)(2,1)S(1)}, u32[]{:S(2)}, u32[]{:S(2)}) collective-permute-start(bf16[9,64,128]{2,1,0:T(8,128)(2,1)S(1)} %mix_back.1.refs_0_.refs_1_), channel_id=1, source_target_pairs={{0,1},{1,0},{2,3},{3,2},{4,5},{5,4},{6,7},{7,6},{8,9},{9,8},{10,11... | collective-permute-start | bytes 442376 | tf_op jit(solution)/shard_map/ppermute | solution.py:487
  70.9 15.7 %collective-permute-start.26 = (bf16[9,2,32,32,128]{4,3,2,1,0:T(8,128)(2,1)S(1)}, bf16[9,2,32,32,128]{4,3,2,1,0:T(8,128)(2,1)S(1)}, u32[]{:S(2)}, u32[]{:S(2)}) collective-permute-start(bf16[9,2,32,32,128]{4,3,2,1,0:T(8,128)(2,1)S(1)} %get-tuple-element.37.refs_0_.refs_16_), channel_id=1, source_target_pairs={{0,2},{2,0},{4,6},{6,4},{8,10},{10,8},{12,14},{14,12},{16,18},{18,... | collective-permute-start | bytes 14155784 | tf_op jit(solution)/shard_map/ppermute | solution.py:491
  72.1 7.8 %collective-permute-start.24 = (bf16[10,64,128]{2,1,0:T(8,128)(2,1)S(1)}, bf16[10,64,128]{2,1,0:T(8,128)(2,1)S(1)}, u32[]{:S(2)}, u32[]{:S(2)}) collective-permute-start(bf16[10,64,128]{2,1,0:T(8,128)(2,1)S(1)} %collective-permute-done.9.refs_3_.refs_10_), channel_id=1, source_target_pairs={{0,2},{2,0},{4,6},{6,4},{8,10},{10,8},{12,14},{14,12},{16,18},{18,... | collective-permute-start | bytes 491528 | tf_op jit(solution)/shard_map/ppermute | solution.py:491
  72.2 8.1 %collective-permute-start.21 = (bf16[10,64,128]{2,1,0:T(8,128)(2,1)S(1)}, bf16[10,64,128]{2,1,0:T(8,128)(2,1)S(1)}, u32[]{:S(2)}, u32[]{:S(2)}) collective-permute-start(bf16[10,64,128]{2,1,0:T(8,128)(2,1)S(1)} %collective-permute-done.9.refs_3_.refs_10_), channel_id=1, source_target_pairs={{0,4},{2,6},{4,0},{6,2},{8,12},{10,14},{12,8},{14,10},{16,20},{18,... | collective-permute-start | bytes 491528 | tf_op jit(solution)/shard_map/ppermute | solution.py:491
  72.2 8.8 %collective-permute-start.20 = (bf16[10,64,128]{2,1,0:T(8,128)(2,1)S(1)}, bf16[10,64,128]{2,1,0:T(8,128)(2,1)S(1)}, u32[]{:S(2)}, u32[]{:S(2)}) collective-permute-start(bf16[10,64,128]{2,1,0:T(8,128)(2,1)S(1)} %collective-permute-done.8.refs_2_.refs_8_), channel_id=1, source_target_pairs={{0,4},{2,6},{4,0},{6,2},{8,12},{10,14},{12,8},{14,10},{16,20},{18,... | collective-permute-start | bytes 491528 | tf_op jit(solution)/shard_map/ppermute | solution.py:491
  73.6 13.0 %collective-permute-start.22 = (bf16[10,64,128]{2,1,0:T(8,128)(2,1)S(1)}, bf16[10,64,128]{2,1,0:T(8,128)(2,1)S(1)}, u32[]{:S(2)}, u32[]{:S(2)}) collective-permute-start(bf16[10,64,128]{2,1,0:T(8,128)(2,1)S(1)} %collective-permute-done.8.refs_2_.refs_8_), channel_id=1, source_target_pairs={{0,2},{2,0},{4,6},{6,4},{8,10},{10,8},{12,14},{14,12},{16,18},{18,... | collective-permute-start | bytes 491528 | tf_op jit(solution)/shard_map/ppermute | solution.py:491
  79.9 6.8 %collective-permute-start.27 = (f32[32,128]{1,0:T(8,128)S(1)}, f32[32,128]{1,0:T(8,128)S(1)}, u32[]{:S(2)}, u32[]{:S(2)}) collective-permute-start(f32[32,128]{1,0:T(8,128)S(1)} %get-tuple-element.40.refs_18_), channel_id=1, source_target_pairs={{0,2},{2,0},{4,6},{6,4},{8,10},{10,8},{12,14},{14,12},{16,18},{18,... | collective-permute-start | bytes 49160 | tf_op jit(solution)/shard_map/ppermute | solution.py:491
  80.2 6.4 %collective-permute-start.25 = (bf16[10,64,128]{2,1,0:T(8,128)(2,1)S(1)}, bf16[10,64,128]{2,1,0:T(8,128)(2,1)S(1)}, u32[]{:S(2)}, u32[]{:S(2)}) collective-permute-start(bf16[10,64,128]{2,1,0:T(8,128)(2,1)S(1)} %collective-permute-done.21.refs_11_), channel_id=1, source_target_pairs={{0,2},{2,0},{4,6},{6,4},{8,10},{10,8},{12,14},{14,12},{16,18},{18,... | collective-permute-start | bytes 491528 | tf_op jit(solution)/shard_map/ppermute | solution.py:491
  81.0 5.6 %collective-permute-start.23 = (bf16[10,64,128]{2,1,0:T(8,128)(2,1)S(1)}, bf16[10,64,128]{2,1,0:T(8,128)(2,1)S(1)}, u32[]{:S(2)}, u32[]{:S(2)}) collective-permute-start(bf16[10,64,128]{2,1,0:T(8,128)(2,1)S(1)} %collective-permute-done.20.refs_9_), channel_id=1, source_target_pairs={{0,2},{2,0},{4,6},{6,4},{8,10},{10,8},{12,14},{14,12},{16,18},{18,... | collective-permute-start | bytes 491528 | tf_op jit(solution)/shard_map/ppermute | solution.py:491
  (5 other events, 37.8 us)
